TPU v7x, 32 devices: a whole 2x2x4 slice. The times are simulated.
32 devices in a mesh: chan: 8 (over z, x), rep: 4 (over y, core).
Axes of the slice: x: 2, y: 2, z: 4, core: 2. Of those that a mesh axis runs over, the one named last changes fastest.
Arguments:
- strain: bfloat16 [128, 131072], P('chan', 'rep'), may hold values from -60 to 60
- fir_taps: float32 [60], replicated, may hold values from -0.75 to 0.75
- spatial: float32 [9], replicated, may hold values from -2 to 2
Outputs:
- cross_tiles: float32 [128, 5, 32, 32], P('chan', None, 'rep')
All inputs are finite; a program needn't handle non-finite values.
Results may differ from a plain program's by a relative error of at most 0.0023.
Values may be sent and summed in bfloat16 or wider, within the bound.
No kernel may reach another device: no remote copies, remote signals or barrier semaphores. Data moves between devices by JAX's collectives and lax.ppermute only.
A program may use at most 64 MiB of HBM per device.

v0:
```python
import math

import jax
import jax.numpy as jnp
from jax import lax
from jax.sharding import PartitionSpec as P

NFFT = 1024
BINS = 32
FIRST_BIN = 16
STEPS = 4


epsilon = 1e-05


def passed_along(shard, axis, by):
    count = lax.axis_size(axis)
    pairs = [(i, i + by) for i in range(count) if 0 <= i + by < count]
    return lax.ppermute(shard, axis, pairs)


def padded_2(cells, sides, width):
    for axis, dim in sides:
        count = lax.axis_size(axis)
        ends = count - 1
        head = lax.slice_in_dim(cells, 0, width, axis=dim)
        tail = lax.slice_in_dim(cells, cells.shape[dim] - width, cells.shape[dim], axis=dim)
        cells = jnp.concatenate(
            [
                lax.ppermute(tail, axis, [(i, (i + 1) % count) for i in range(ends)]),
                cells,
                lax.ppermute(head, axis, [((i + 1) % count, i) for i in range(ends)]),
            ],
            axis=dim,
        )
    return cells


def from_behind(block, axis, distance):
    devices = range(lax.axis_size(axis))
    route = [((i - distance) % len(devices), i) for i in devices]
    return lax.ppermute(block, axis, route)


def toeplitz_pair(fir_taps):
    source_pos = jnp.arange(128, dtype=jnp.int32)[:, None]
    target_pos = jnp.arange(128, dtype=jnp.int32)[None, :]
    tap_slots = jnp.arange(fir_taps.shape[0], dtype=jnp.int32)
    lag_now = (target_pos - source_pos)[:, :, None]
    lag_before = (target_pos + 128 - source_pos)[:, :, None]
    zero_value = jnp.zeros((), fir_taps.dtype)
    taps_now = jnp.sum(jnp.where(lag_now == tap_slots, fir_taps, zero_value), axis=2)
    taps_before = jnp.sum(jnp.where(lag_before == tap_slots, fir_taps, zero_value), axis=2)
    return (taps_now, taps_before)


def dft_table(bin_count, first_bin, dft_length, float_type):
    sample_pos = jnp.arange(dft_length, dtype=jnp.int32)[:, None]
    freq_bins = (first_bin + jnp.arange(bin_count, dtype=jnp.int32))[None, :]
    phase_index = sample_pos * freq_bins % dft_length
    phase_angle = phase_index.astype(float_type) * (2.0 * math.pi / dft_length)
    inverse_root = 1.0 / math.sqrt(dft_length)
    return jnp.concatenate([jnp.cos(phase_angle), -jnp.sin(phase_angle)], axis=1) * inverse_root


def window_spectra(channel_rows, spatial, taps_now, taps_before, dft_matrix):
    filter_span = spatial.shape[0]
    row_count = channel_rows.shape[0] - filter_span + 1
    mixed_rows = spatial[0] * channel_rows[0:row_count]
    for offset in range(1, filter_span):
        mixed_rows = mixed_rows + spatial[offset] * channel_rows[offset : offset + row_count]
    time_blocks = mixed_rows.reshape(row_count, -1, 128)
    band_pass = jnp.einsum(
        "cbj,ji->cbi", time_blocks[:, 1:], taps_now, precision=lax.Precision.HIGHEST
    )
    band_pass = band_pass + jnp.einsum(
        "cbj,ji->cbi", time_blocks[:, :-1], taps_before, precision=lax.Precision.HIGHEST
    )
    window_data = band_pass.reshape(row_count, -1, dft_matrix.shape[0])
    window_power = jnp.mean(window_data * window_data, axis=2, keepdims=True)
    normalized = window_data / jnp.sqrt(window_power + epsilon)
    spectra = jnp.einsum("cwn,nm->cwm", normalized, dft_matrix, precision=lax.Precision.HIGHEST)
    return spectra.reshape(row_count, spectra.shape[1], 2, -1).astype(jnp.bfloat16)


def cross_tile(own_spec, other_spec):
    own_real, own_imag = (own_spec[:, :, 0], own_spec[:, :, 1])
    other_real, other_imag = (other_spec[:, :, 0], other_spec[:, :, 1])
    cross_real = jnp.einsum(
        "cwf,kwf->cfk", own_real, other_real, preferred_element_type=jnp.float32
    )
    cross_real = cross_real + jnp.einsum(
        "cwf,kwf->cfk", own_imag, other_imag, preferred_element_type=jnp.float32
    )
    cross_imag = jnp.einsum(
        "cwf,kwf->cfk", own_imag, other_real, preferred_element_type=jnp.float32
    )
    cross_imag = cross_imag - jnp.einsum(
        "cwf,kwf->cfk", own_real, other_imag, preferred_element_type=jnp.float32
    )
    return jnp.concatenate([cross_real, cross_imag], axis=2)


def per_device(strain, fir_taps, spatial):
    taps_now, taps_before = toeplitz_pair(fir_taps)
    dft_matrix = dft_table(BINS, FIRST_BIN, NFFT, fir_taps.dtype)
    rim_width = spatial.shape[0] // 2
    history = strain[:, strain.shape[1] - 128 :]
    earlier = passed_along(history, "rep", 1)
    extended = jnp.concatenate([earlier, strain], axis=1)
    padded = padded_2(extended, (("chan", 0),), rim_width)
    spectra = window_spectra(padded.astype(jnp.float32), spatial, taps_now, taps_before, dft_matrix)
    inverse = 1.0 / (spectra.shape[1] * lax.axis_size("rep"))
    spectra = lax.all_to_all(spectra, "rep", split_axis=3, concat_axis=1, tiled=True)
    tile_list = [cross_tile(spectra, spectra)]
    partner = spectra
    for offset in range(STEPS):
        partner = from_behind(partner, "chan", -1)
        tile_list.append(cross_tile(spectra, partner))
    partial_tiles = jnp.stack(tile_list, axis=1) * inverse
    return partial_tiles


def solution(mesh):
    in_specs = (P("chan", "rep"), P(), P())
    out_specs = P("chan", None, "rep", None)
    return jax.shard_map(
        per_device, mesh=mesh, in_specs=in_specs, out_specs=out_specs, check_vma=False
    )
```

profile of v0, /device:TPU:0, one launch (start us, length us, event | category | flops | bytes accessed | tf_op | source)
XLA Modules:
  0.0 84.5 jit_solution(7840038666615068160)
XLA Ops:
  0.7 2.3 %collective-permute-start = (bf16[16,128]{1,0:T(8,128)(2,1)S(1)}, bf16[16,128]{1,0:T(8,128)(2,1)S(1)}, u32[]{:S(2)}, u32[]{:S(2)}) collective-permute-start(bf16[16,128]{1,0:T(8,128)(2,1)S(1)} %slice.110), channel_id=1, source_target_pairs={{0,1},{1,2},{2,3},{4,5},{5,6},{6,7},{8,9},{9,10},{10,11},{12,13},{... | collective-permute-start | bytes 12296 | tf_op jit(solution)/shard_map/ppermute | solution.py:20
  3.7 1.7 %fusion.55 = (f32[1]{0:T(128)}, f32[1]{0:T(128)}, f32[1]{0:T(128)}, f32[1]{0:T(128)}, f32[1]{0:T(128)}, /*index=5*/f32[1]{0:T(128)}, f32[1]{0:T(128)}, f32[1]{0:T(128)}, f32[1]{0:T(128)}) fusion(f32[9]{0:T(128)} %param.5), kind=kLoop, calls=%fused_computation.108 | loop fusion | bytes 72 | tf_op jit(solution)/shard_map/slice | solution.py:70
  5.4 1.3 %constant_dynamic-update-slice_fusion = bf16[16,32896]{1,0:T(8,128)(2,1)S(1)} fusion(bf16[16,32896]{1,0:T(8,128)(2,1)S(1)} %constant_dynamic-update-slice_fusion.1, bf16[16,32768]{1,0:T(8,128)(2,1)} %param.3), kind=kLoop, calls=%fused_computation.100 | loop fusion | bytes 2097152 | tf_op jit(solution)/shard_map/concatenate | solution.py:111
  6.9 4.2 %collective-permute-start.1 = (bf16[4,32896]{1,0:T(4,128)(2,1)S(1)}, bf16[4,32896]{1,0:T(4,128)(2,1)S(1)}, u32[]{:S(2)}, u32[]{:S(2)}) collective-permute-start(bf16[4,32896]{1,0:T(4,128)(2,1)S(1)} %get-tuple-element.7), channel_id=1, source_target_pairs={{0,4},{4,8},{8,12},{12,16},{16,20},{20,24},{24,28},{1,5},{5,9},{9,... | collective-permute-start | bytes 789512 | tf_op jit(solution)/shard_map/ppermute | solution.py:31
  11.2 1.3 %collective-permute-start.2 = (bf16[4,32896]{1,0:T(4,128)(2,1)S(1)}, bf16[4,32896]{1,0:T(4,128)(2,1)S(1)}, u32[]{:S(2)}, u32[]{:S(2)}) collective-permute-start(bf16[4,32896]{1,0:T(4,128)(2,1)S(1)} %get-tuple-element.8), channel_id=1, source_target_pairs={{4,0},{8,4},{12,8},{16,12},{20,16},{24,20},{28,24},{5,1},{9,5},{13... | collective-permute-start | bytes 789512 | tf_op jit(solution)/shard_map/ppermute | solution.py:33
  12.5 0.8 select_reduce_fusion.1
  13.3 9.2 %collective-permute-done.1 = bf16[4,32896]{1,0:T(4,128)(2,1)S(1)} collective-permute-done((bf16[4,32896]{1,0:T(4,128)(2,1)S(1)}, bf16[4,32896]{1,0:T(4,128)(2,1)S(1)}, u32[]{:S(2)}, u32[]{:S(2)}) %collective-permute-start.1) | collective-permute-done | bytes 263200 | tf_op jit(solution)/shard_map/ppermute | solution.py:31
  23.1 8.8 %fusion = f32[16,32896]{1,0:T(8,128)} fusion(f32[24,32896]{1,0:T(8,128)S(1)} %maximum_convert_fusion, f32[]{:T(128)} %bitcast.8, f32[]{:T(128)} %bitcast.7, f32[]{:T(128)} %bitcast.6, f32[]{:T(128)} %bitcast.5, f32[]{:T(128)} %bitcast.4, f32[]{:T(128)} %bitcast.3, f32[]{:T(128)} %bitcast.2, f32[]{:T(128)} %bitcast.1, f32[]{:T(128)} %bitcast), kind=kLoop, calls=%fused_computation.5 | loop fusion | flops 8947712 | bytes 21053476 | tf_op jit(solution)/shard_map/add | solution.py:72
  32.0 1.7 %reshape.57 = f32[16,257,128]{2,1,0:T(8,128)S(1)} reshape(f32[16,32896]{1,0:T(8,128)} %fusion) | data formatting | bytes 4210688 | tf_op jit(solution)/shard_map/reshape | solution.py:73
  33.7 2.0 %fusion.8 = f32[16,256,128]{1,2,0:T(8,128)S(1)} fusion(f32[16,257,128]{2,1,0:T(8,128)S(1)} %reshape.57, f32[128,128]{1,0:T(8,128)S(1)} %get-tuple-element.6), kind=kOutput, calls=%fused_computation.21 | convolution fusion | flops 805306368 | bytes 4259840 | tf_op jit(solution)/shard_map/cbj,ji->cbi/dot_general | solution.py:77
  35.7 3.7 %multiply_reduce_fusion = (f32[16,256]{1,0:T(8,128)S(1)}, f32[16,256,128]{1,2,0:T(8,128)}) fusion(f32[16,256,128]{1,2,0:T(8,128)S(1)} %fusion.8, f32[128,128]{1,0:T(8,128)S(1)} %get-tuple-element.5, f32[16,257,128]{2,1,0:T(8,128)S(1)} %reshape.57), kind=kOutput, calls=%fused_computation.27 | convolution fusion | flops 806875136 | bytes 6373376 | tf_op jit(solution)/shard_map/cbj,ji->cbi/dot_general | solution.py:74
  39.7 1.9 %broadcast_divide_fusion = f32[16,256,128]{1,2,0:T(8,128)S(1)} fusion(f32[16,256,128]{1,2,0:T(8,128)} %get-tuple-element.21, f32[16,256]{1,0:T(8,128)S(1)} %copy.21), kind=kLoop, calls=%fused_computation.51 | loop fusion | flops 524288 | bytes 4210688 | tf_op jit(solution)/shard_map/div | solution.py:82
  41.5 1.9 %copy.22 = f32[16,256,128]{2,1,0:T(8,128)} copy(f32[16,256,128]{1,2,0:T(8,128)S(1)} %broadcast_divide_fusion) | data formatting | bytes 4194304 | tf_op jit(solution)/shard_map/div | solution.py:82
  43.4 1.7 %reshape.60 = f32[16,32,1024,1]{2,1,0,3:T(8,128)S(1)} reshape(f32[16,256,128]{2,1,0:T(8,128)} %copy.22) | data formatting | bytes 4194304 | tf_op jit(solution)/shard_map/div | solution.py:82
  45.1 1.8 %fusion.17 = bf16[16,32,2,32]{3,1,2,0:T(8,128)(2,1)S(1)} fusion(f32[2,32,1024,1]{2,1,0,3:T(8,128)S(1)} %bitcast.139, f32[16,32,1024,1]{2,1,0,3:T(8,128)S(1)} %reshape.60), kind=kOutput, calls=%fused_computation.30 | convolution fusion | flops 402685952 | bytes 2424832 | tf_op jit(solution)/shard_map/cwn,nm->cwm/dot_general | solution.py:83
  47.6 6.5 %all_to_all.18 = bf16[4,2,4096]{2,1,0:T(2,128)(2,1)S(1)} all-to-all(bf16[4,2,4096]{2,1,0:T(2,128)(2,1)S(1)} %reshape.63), channel_id=1, replica_groups=mesh['chan'=8,'rep'=4] {'rep'}, dimensions={0} | all-to-all | bytes 131072 | tf_op jit(solution)/shard_map/all_to_all | solution.py:115
  54.7 5.4 %collective-permute-start.3 = (bf16[16,128,2,8]{1,0,3,2:T(8,128)(2,1)S(1)}, bf16[16,128,2,8]{1,0,3,2:T(8,128)(2,1)S(1)}, u32[]{:S(2)}, u32[]{:S(2)}) collective-permute-start(bf16[16,128,2,8]{1,0,3,2:T(8,128)(2,1)S(1)} %all_to_all.16), channel_id=1, source_target_pairs={{4,0},{8,4},{12,8},{16,12},{20,16},{24,20},{28,24},{0,28},{5,1},{9... | collective-permute-start | bytes 196616 | tf_op jit(solution)/shard_map/ppermute | solution.py:43
  60.8 1.2 %collective-permute-done.3 = bf16[16,128,2,8]{1,0,3,2:T(8,128)(2,1)S(1)} collective-permute-done((bf16[16,128,2,8]{1,0,3,2:T(8,128)(2,1)S(1)}, bf16[16,128,2,8]{1,0,3,2:T(8,128)(2,1)S(1)}, u32[]{:S(2)}, u32[]{:S(2)}) %collective-permute-start.3) | collective-permute-done | bytes 65568 | tf_op jit(solution)/shard_map/ppermute | solution.py:43
  62.1 5.1 %collective-permute-start.4 = (bf16[16,128,2,8]{1,0,3,2:T(8,128)(2,1)S(1)}, bf16[16,128,2,8]{1,0,3,2:T(8,128)(2,1)S(1)}, u32[]{:S(2)}, u32[]{:S(2)}) collective-permute-start(bf16[16,128,2,8]{1,0,3,2:T(8,128)(2,1)S(1)} %collective-permute-done.3), channel_id=1, source_target_pairs={{4,0},{8,4},{12,8},{16,12},{20,16},{24,20},{28,24},{0,28},{5,1},{9... | collective-permute-start | bytes 196616 | tf_op jit(solution)/shard_map/ppermute | solution.py:43
  67.8 1.2 %collective-permute-done.4 = bf16[16,128,2,8]{1,0,3,2:T(8,128)(2,1)S(1)} collective-permute-done((bf16[16,128,2,8]{1,0,3,2:T(8,128)(2,1)S(1)}, bf16[16,128,2,8]{1,0,3,2:T(8,128)(2,1)S(1)}, u32[]{:S(2)}, u32[]{:S(2)}) %collective-permute-start.4) | collective-permute-done | bytes 65568 | tf_op jit(solution)/shard_map/ppermute | solution.py:43
  69.0 5.1 %collective-permute-start.5 = (bf16[16,128,2,8]{1,0,3,2:T(8,128)(2,1)S(1)}, bf16[16,128,2,8]{1,0,3,2:T(8,128)(2,1)S(1)}, u32[]{:S(2)}, u32[]{:S(2)}) collective-permute-start(bf16[16,128,2,8]{1,0,3,2:T(8,128)(2,1)S(1)} %collective-permute-done.4), channel_id=1, source_target_pairs={{4,0},{8,4},{12,8},{16,12},{20,16},{24,20},{28,24},{0,28},{5,1},{9... | collective-permute-start | bytes 196616 | tf_op jit(solution)/shard_map/ppermute | solution.py:43
  74.7 1.2 %collective-permute-done.5 = bf16[16,128,2,8]{1,0,3,2:T(8,128)(2,1)S(1)} collective-permute-done((bf16[16,128,2,8]{1,0,3,2:T(8,128)(2,1)S(1)}, bf16[16,128,2,8]{1,0,3,2:T(8,128)(2,1)S(1)}, u32[]{:S(2)}, u32[]{:S(2)}) %collective-permute-start.5) | collective-permute-done | bytes 65568 | tf_op jit(solution)/shard_map/ppermute | solution.py:43
  76.0 5.1 %collective-permute-start.6 = (bf16[16,128,2,8]{1,0,3,2:T(8,128)(2,1)S(1)}, bf16[16,128,2,8]{1,0,3,2:T(8,128)(2,1)S(1)}, u32[]{:S(2)}, u32[]{:S(2)}) collective-permute-start(bf16[16,128,2,8]{1,0,3,2:T(8,128)(2,1)S(1)} %collective-permute-done.5), channel_id=1, source_target_pairs={{4,0},{8,4},{12,8},{16,12},{20,16},{24,20},{28,24},{0,28},{5,1},{9... | collective-permute-start | bytes 196616 | tf_op jit(solution)/shard_map/ppermute | solution.py:43
  81.7 1.2 %collective-permute-done.6 = bf16[16,128,2,8]{1,0,3,2:T(8,128)(2,1)S(1)} collective-permute-done((bf16[16,128,2,8]{1,0,3,2:T(8,128)(2,1)S(1)}, bf16[16,128,2,8]{1,0,3,2:T(8,128)(2,1)S(1)}, u32[]{:S(2)}, u32[]{:S(2)}) %collective-permute-start.6) | collective-permute-done | bytes 65568 | tf_op jit(solution)/shard_map/ppermute | solution.py:43
  (51 shorter events, 7.7 us)
Async XLA Ops:
  0.0 12.5 %copy-start = (f32[60]{0:T(128)S(1)}, f32[60]{0:T(128)}, u32[]{:S(2)}) copy-start(f32[60]{0:T(128)} %param.4) | copy-start | bytes 724
  0.7 4.7 %collective-permute-start = (bf16[16,128]{1,0:T(8,128)(2,1)S(1)}, bf16[16,128]{1,0:T(8,128)(2,1)S(1)}, u32[]{:S(2)}, u32[]{:S(2)}) collective-permute-start(bf16[16,128]{1,0:T(8,128)(2,1)S(1)} %slice.110), channel_id=1, source_target_pairs={{0,1},{1,2},{2,3},{4,5},{5,6},{6,7},{8,9},{9,10},{10,11},{12,13},{... | collective-permute-start | bytes 12296 | tf_op jit(solution)/shard_map/ppermute | solution.py:20
  6.9 15.6 %collective-permute-start.1 = (bf16[4,32896]{1,0:T(4,128)(2,1)S(1)}, bf16[4,32896]{1,0:T(4,128)(2,1)S(1)}, u32[]{:S(2)}, u32[]{:S(2)}) collective-permute-start(bf16[4,32896]{1,0:T(4,128)(2,1)S(1)} %get-tuple-element.7), channel_id=1, source_target_pairs={{0,4},{4,8},{8,12},{12,16},{16,20},{20,24},{24,28},{1,5},{5,9},{9,... | collective-permute-start | bytes 789512 | tf_op jit(solution)/shard_map/ppermute | solution.py:31
  11.2 11.4 %collective-permute-start.2 = (bf16[4,32896]{1,0:T(4,128)(2,1)S(1)}, bf16[4,32896]{1,0:T(4,128)(2,1)S(1)}, u32[]{:S(2)}, u32[]{:S(2)}) collective-permute-start(bf16[4,32896]{1,0:T(4,128)(2,1)S(1)} %get-tuple-element.8), channel_id=1, source_target_pairs={{4,0},{8,4},{12,8},{16,12},{20,16},{24,20},{28,24},{5,1},{9,5},{13... | collective-permute-start | bytes 789512 | tf_op jit(solution)/shard_map/ppermute | solution.py:33
  54.7 7.3 %collective-permute-start.3 = (bf16[16,128,2,8]{1,0,3,2:T(8,128)(2,1)S(1)}, bf16[16,128,2,8]{1,0,3,2:T(8,128)(2,1)S(1)}, u32[]{:S(2)}, u32[]{:S(2)}) collective-permute-start(bf16[16,128,2,8]{1,0,3,2:T(8,128)(2,1)S(1)} %all_to_all.16), channel_id=1, source_target_pairs={{4,0},{8,4},{12,8},{16,12},{20,16},{24,20},{28,24},{0,28},{5,1},{9... | collective-permute-start | bytes 196616 | tf_op jit(solution)/shard_map/ppermute | solution.py:43
  62.1 7.0 %collective-permute-start.4 = (bf16[16,128,2,8]{1,0,3,2:T(8,128)(2,1)S(1)}, bf16[16,128,2,8]{1,0,3,2:T(8,128)(2,1)S(1)}, u32[]{:S(2)}, u32[]{:S(2)}) collective-permute-start(bf16[16,128,2,8]{1,0,3,2:T(8,128)(2,1)S(1)} %collective-permute-done.3), channel_id=1, source_target_pairs={{4,0},{8,4},{12,8},{16,12},{20,16},{24,20},{28,24},{0,28},{5,1},{9... | collective-permute-start | bytes 196616 | tf_op jit(solution)/shard_map/ppermute | solution.py:43
  69.0 7.0 %collective-permute-start.5 = (bf16[16,128,2,8]{1,0,3,2:T(8,128)(2,1)S(1)}, bf16[16,128,2,8]{1,0,3,2:T(8,128)(2,1)S(1)}, u32[]{:S(2)}, u32[]{:S(2)}) collective-permute-start(bf16[16,128,2,8]{1,0,3,2:T(8,128)(2,1)S(1)} %collective-permute-done.4), channel_id=1, source_target_pairs={{4,0},{8,4},{12,8},{16,12},{20,16},{24,20},{28,24},{0,28},{5,1},{9... | collective-permute-start | bytes 196616 | tf_op jit(solution)/shard_map/ppermute | solution.py:43
  76.0 7.0 %collective-permute-start.6 = (bf16[16,128,2,8]{1,0,3,2:T(8,128)(2,1)S(1)}, bf16[16,128,2,8]{1,0,3,2:T(8,128)(2,1)S(1)}, u32[]{:S(2)}, u32[]{:S(2)}) collective-permute-start(bf16[16,128,2,8]{1,0,3,2:T(8,128)(2,1)S(1)} %collective-permute-done.5), channel_id=1, source_target_pairs={{4,0},{8,4},{12,8},{16,12},{20,16},{24,20},{28,24},{0,28},{5,1},{9... | collective-permute-start | bytes 196616 | tf_op jit(solution)/shard_map/ppermute | solution.py:43
where the time goes:
time: 84.9 us; the launch traced here: 84.5 us
  starting transfers between devices  28.5 us (34%)
  waiting for transfers between devices  14.2 us (17%)
  other arithmetic  13.3 us (16%)
  local copies, waits for them, and re-layouts  11.4 us (13%)
  matrix products  10.3 us (12%)
  blocking collectives  6.49 us (8%)
    ppermute x4, starting transfers between devices, from_behind(): return lax.ppermute(block, axis, route)  20.6 us
    ppermute x1, waiting for transfers between devices, padded_2(): lax.ppermute(tail, axis, [(i, (i + 1) % count) for i in range(ends)])  9.22 us
    add x1, other arithmetic, window_spectra(): mixed_rows + spatial[offset] * channel_rows[offset:offset + row_count]  8.84 us
    all_to_all x1, blocking collectives, per_device(): lax.all_to_all(spectra, 'rep', split_axis=3, concat_axis=1, tiled=True)  6.49 us
    ppermute x4, waiting for transfers between devices, from_behind(): return lax.ppermute(block, axis, route)  4.94 us
    ppermute x1, starting transfers between devices, padded_2(): lax.ppermute(tail, axis, [(i, (i + 1) % count) for i in range(ends)])  4.24 us
    dot_general x1, matrix products, window_spectra(): jnp.einsum('cbj,ji->cbi', time_blocks[:, 1:], taps_now, precision=lax.Pre...  3.7 us
    div x4, local copies, waits for them, and re-layouts, window_spectra(): normalized = window_data / jnp.sqrt(window_power + epsilon)  3.64 us
  transfers between devices with their start and end apart: 7, of which 5 were waited for; matrix products, arithmetic and copies ran while one was open for 7% of the time, Pallas kernels for 0%

commit v1 on v0

v1 whole, which is shorter than its diff:
```python
import math

import jax
import jax.numpy as jnp
import numpy as np
from jax import lax
from jax.experimental import pallas as pl
from jax.experimental.pallas import tpu as pltpu
from jax.sharding import PartitionSpec as P

NFFT = 1024
BINS = 32
FIRST_BIN = 16
STEPS = 4
LANES = 128
HALO = 4
GROUP = 8

epsilon = 1e-05

f32 = jnp.float32
bf16 = jnp.bfloat16


def dot(a, b):
    return lax.dot_general(a, b, (((1,), (0,)), ((), ())), preferred_element_type=f32)


def dot_t(a, b):
    return lax.dot_general(a, b, (((1,), (1,)), ((), ())), preferred_element_type=f32)


def halves(values):
    high = values.astype(bf16)
    low = (values - high.astype(f32)).astype(bf16)
    return high, low


def dft_table():
    sample = np.arange(NFFT)[:, None]
    bins = FIRST_BIN + np.arange(BINS)[None, :]
    angle = (sample * bins % NFFT) * (2.0 * math.pi / NFFT)
    scale = 1.0 / math.sqrt(NFFT)
    real = (np.cos(angle) * scale).reshape(NFFT, BINS // GROUP, GROUP)
    imag = (-np.sin(angle) * scale).reshape(NFFT, BINS // GROUP, GROUP)
    table = np.concatenate([real, imag], axis=2).reshape(NFFT, 2 * BINS).astype(np.float32)
    high = table.astype(jnp.bfloat16)
    low = (table - high.astype(np.float32)).astype(jnp.bfloat16)
    return np.concatenate([high, low], axis=1)


def rounded_halves(values):
    high = lax.reduce_precision(values, exponent_bits=8, mantissa_bits=7)
    return high.astype(bf16), (values - high).astype(bf16)


def toeplitz(fir_taps):
    source = jnp.arange(2 * LANES, dtype=jnp.int32)[:, None]
    target = jnp.arange(LANES, dtype=jnp.int32)[None, :]
    lag = (target + LANES - source)[:, :, None]
    slots = jnp.arange(fir_taps.shape[0], dtype=jnp.int32)
    taps = jnp.sum(jnp.where(lag == slots, fir_taps, 0.0), axis=2)
    return jnp.concatenate(rounded_halves(taps), axis=1)


def mixing(spatial, rows):
    span = spatial.shape[0]
    offset = (jnp.arange(rows + span - 1, dtype=jnp.int32)[None, :] - jnp.arange(rows, dtype=jnp.int32)[:, None])[:, :, None]
    return jnp.sum(jnp.where(offset == jnp.arange(span, dtype=jnp.int32), spatial, 0.0), axis=2)


def filtered(mixed_ref, first, count, rows, toeplitz_ref):
    parts = []
    for block in range(count):
        start = pl.multiple_of((first + block) * LANES, LANES)
        parts.append(mixed_ref[:, pl.ds(start, 2 * LANES)])
    out = dot(jnp.concatenate(parts, axis=0), toeplitz_ref[...])
    out = out[:, :LANES] + out[:, LANES:]
    out = out.reshape(count, 2, rows, LANES)
    return out[:, 0] + out[:, 1]


def windowed(band, first_window, rows, split_ref, scale_ref):
    per = NFFT // LANES
    count = band.shape[0] // per
    squares = band * band
    for window in range(count):
        total = squares[window * per]
        for block in range(1, per):
            total = total + squares[window * per + block]
        power = jnp.sum(total, axis=1, keepdims=True) * (1.0 / NFFT)
        scale_ref[first_window + window] = jnp.broadcast_to(1.0 / jnp.sqrt(power + epsilon), (rows, LANES))
    high = band.astype(bf16).astype(f32)
    low = band - high
    both = jnp.concatenate([high, low], axis=1).astype(bf16)
    for window in range(count):
        for block in range(per):
            split_ref[first_window + window, :, block * LANES : (block + 1) * LANES] = both[window * per + block]


def spectra_of(split_ref, scale_ref, dft_ref, rows):
    windows = split_ref.shape[0]
    out = dot(split_ref[...].reshape(windows * 2 * rows, NFFT), dft_ref[...])
    out = out + pltpu.roll(out, LANES // 2, 1)
    out = out.reshape(windows, 2, rows, LANES)
    return (out[:, 0] + out[:, 1]) * scale_ref[...]


def own_kernel(strain_ref, history_ref, mix_ref, toeplitz_ref, dft_ref, edge_ref, spectra_ref, mixed_ref, split_ref, scale_ref):
    rows, samples = strain_ref.shape

    def mix(columns):
        out = dot(mix_ref[...], columns)
        high, low = halves(out[:rows] + out[rows:])
        return jnp.concatenate([high, low], axis=0)

    mixed_ref[:, :LANES] = mix(history_ref[...])
    step = 4 * NFFT

    def mix_step(i, _):
        start = pl.multiple_of(i * step, step)
        mixed_ref[:, pl.ds(pl.multiple_of(start + LANES, LANES), step)] = mix(strain_ref[:, pl.ds(start, step)])
        return 0

    lax.fori_loop(0, samples // step, mix_step, 0)
    count = step // LANES
    near = lax.broadcasted_iota(jnp.int32, (count, rows // 2, LANES), 1) < HALO

    def filter_step(i, _):
        band = filtered(mixed_ref, i * count, count, rows, toeplitz_ref)
        edge_ref[pl.ds(i * count, count)] = jnp.where(near, band[:, : rows // 2], band[:, rows // 2 :])
        windowed(band, i * (step // NFFT), rows, split_ref, scale_ref)
        return 0

    lax.fori_loop(0, samples // step, filter_step, 0)
    spectra_ref[...] = spectra_of(split_ref, scale_ref, dft_ref, rows)


def edge_kernel(
    before_ref, after_ref, edge_ref, own_ref, mix_ref, toeplitz_ref, dft_ref, out_ref, mixed_ref, split_ref, scale_ref
):
    rows = 2 * HALO
    width = before_ref.shape[1]
    step = 4 * NFFT

    def mix(start, size):
        near = before_ref[:, pl.ds(start, size)].astype(f32)
        far = after_ref[:, pl.ds(start, size)].astype(f32)
        out = dot(mix_ref[...], jnp.concatenate([near, far], axis=0).astype(bf16))
        out = out[:rows] + out[rows:]
        high = out.astype(bf16).astype(f32)
        mixed_ref[:, pl.ds(start, size)] = jnp.concatenate([high, out - high], axis=0).astype(bf16)

    mix(0, LANES)
    lax.fori_loop(0, width // step, lambda i, _: (mix(pl.multiple_of(i * step + LANES, LANES), step), 0)[1], 0)
    count = step // LANES

    def filter_step(i, _):
        band = filtered(mixed_ref, i * count, count, rows, toeplitz_ref) + edge_ref[pl.ds(i * count, count)]
        windowed(band, i * (step // NFFT), rows, split_ref, scale_ref)
        return 0

    lax.fori_loop(0, width // step, filter_step, 0)
    edges = spectra_of(split_ref, scale_ref, dft_ref, rows)
    near = lax.broadcasted_iota(jnp.int32, edges.shape, 1) < HALO
    own = own_ref[...]
    first = jnp.where(near, edges, own[:, :rows])
    second = jnp.where(near, own[:, rows:], edges)
    spectra = jnp.concatenate([first, second], axis=1)
    width_group = 2 * GROUP
    across = LANES // width_group
    slot = lax.broadcasted_iota(jnp.int32, spectra.shape[1:], 1) // width_group
    for group in range(out_ref.shape[0]):
        for outer in range(out_ref.shape[1]):
            tile = jnp.zeros(spectra.shape[1:], f32)
            for inner in range(across):
                shift = (inner - group) * width_group % LANES
                value = spectra[outer * across + inner]
                if shift:
                    value = pltpu.roll(value, shift, 1)
                tile = jnp.where(slot == inner, value, tile)
            out_ref[group, outer] = tile.astype(bf16)


def left_kernel(own_ref, left_ref):
    parts, rows, _ = own_ref.shape
    lane = lax.broadcasted_iota(jnp.int32, (GROUP, LANES), 1)
    mask = lane % GROUP == lax.broadcasted_iota(jnp.int32, (GROUP, LANES), 0)
    real_lane = lax.broadcasted_iota(jnp.int32, (rows, LANES), 1) % (2 * GROUP) < GROUP

    for part in range(parts):
        value = own_ref[part].astype(f32)
        turned = jnp.where(real_lane, pltpu.roll(value, LANES - GROUP, 1), -pltpu.roll(value, GROUP, 1))
        for half, source in enumerate((value, turned)):
            spread = [jnp.where(mask, jnp.broadcast_to(source[c : c + 1], (GROUP, LANES)), 0.0) for c in range(rows)]
            left_ref[half, :, part * LANES : (part + 1) * LANES] = jnp.concatenate(spread, axis=0).astype(bf16)


def tile_kernel(scale, left_ref, *refs):
    partner_refs, out_ref = refs[:-1], refs[-1]
    parts, rows, _ = partner_refs[0].shape
    right = jnp.concatenate(
        [jnp.concatenate([ref[part] for part in range(parts)], axis=1) for ref in partner_refs], axis=0
    )
    real = dot_t(left_ref[0], right) * scale
    imag = dot_t(left_ref[1], right) * scale
    for c in range(rows):
        for s in range(len(partner_refs)):
            a = real[c * GROUP : (c + 1) * GROUP, s * rows : (s + 1) * rows]
            b = imag[c * GROUP : (c + 1) * GROUP, s * rows : (s + 1) * rows]
            out_ref[c, s] = jnp.concatenate([a, b], axis=1)


def call(kernel, out_shape, scratch=(), flops=0, bytes_accessed=0):
    return pl.pallas_call(
        kernel,
        out_shape=out_shape,
        scratch_shapes=list(scratch),
        compiler_params=pltpu.CompilerParams(vmem_limit_bytes=32 * 2**20),
        cost_estimate=pl.CostEstimate(flops=flops, bytes_accessed=bytes_accessed, transcendentals=0),
    )


def per_device(strain, fir_taps, spatial):
    rows, samples = strain.shape
    windows = samples // NFFT
    blocks = samples // LANES
    rep = lax.axis_size("rep")
    chan = lax.axis_size("chan")
    history = lax.ppermute(strain[:, samples - LANES :], "rep", [(i, i + 1) for i in range(rep - 1)])
    tail = jnp.concatenate([history[rows - HALO :], strain[rows - HALO :]], axis=1)
    head = jnp.concatenate([history[:HALO], strain[:HALO]], axis=1)
    before = lax.ppermute(tail, "chan", [(i, i + 1) for i in range(chan - 1)])
    after = lax.ppermute(head, "chan", [(i + 1, i) for i in range(chan - 1)])

    filter_matrix = toeplitz(fir_taps)
    table = jnp.asarray(dft_table())
    mix = mixing(spatial, rows)
    own_mix = jnp.concatenate(rounded_halves(mix[:, HALO : HALO + rows]), axis=0)
    edge_rows = jnp.concatenate([mix[:HALO], mix[rows - HALO :]], axis=0)
    edge_mix = jnp.concatenate([edge_rows[:, :HALO], edge_rows[:, HALO + rows :]], axis=1)
    edge_mix = jnp.concatenate(rounded_halves(edge_mix), axis=0)

    edge, own = call(
        own_kernel,
        (jax.ShapeDtypeStruct((blocks, 2 * HALO, LANES), f32), jax.ShapeDtypeStruct((windows, rows, LANES), f32)),
        [
            pltpu.VMEM((2 * rows, LANES + samples), bf16),
            pltpu.VMEM((windows, 2 * rows, NFFT), bf16),
            pltpu.VMEM((windows, rows, LANES), f32),
        ],
        flops=2 * 2 * rows * samples * 512,
        bytes_accessed=4 * 2**20,
    )(strain, history, own_mix, filter_matrix, table)
    pieces = call(
        edge_kernel,
        jax.ShapeDtypeStruct((rep, windows * 2 * GROUP // LANES, rows, LANES), bf16),
        [
            pltpu.VMEM((4 * HALO, LANES + samples), bf16),
            pltpu.VMEM((windows, 4 * HALO, NFFT), bf16),
            pltpu.VMEM((windows, 2 * HALO, LANES), f32),
        ],
        flops=2 * 2 * rows * samples * 256,
        bytes_accessed=2 * 2**20,
    )(before, after, edge, own, edge_mix, filter_matrix, table)
    gathered = lax.all_to_all(pieces, "rep", split_axis=0, concat_axis=0, tiled=True)
    gathered = gathered.reshape(-1, rows, LANES)
    partners = [gathered]
    for step in range(1, STEPS + 1):
        partners.append(lax.ppermute(gathered, "chan", [((i + step) % chan, i) for i in range(chan)]))
    parts = gathered.shape[0]
    left = call(
        left_kernel,
        jax.ShapeDtypeStruct((2, rows * GROUP, parts * LANES), bf16),
        flops=2**20,
        bytes_accessed=2**20,
    )(gathered)
    scale = 1.0 / (windows * rep)
    return call(
        lambda *refs: tile_kernel(scale, *refs),
        jax.ShapeDtypeStruct((rows, STEPS + 1, BINS // rep, 2 * rows), f32),
        flops=2**24,
        bytes_accessed=2**20,
    )(left, *partners)


def solution(mesh):
    in_specs = (P("chan", "rep"), P(), P())
    out_specs = P("chan", None, "rep", None)
    return jax.shard_map(
        per_device, mesh=mesh, in_specs=in_specs, out_specs=out_specs, check_vma=False
    )
```

time: 84.9 us -> 47.9 us (0.56)
  Pallas kernels: 0 us -> 12.1 us
  other arithmetic: 13.3 us -> 2.11 us
  matrix products: 10.3 us -> 0 us
  starting transfers between devices: 28.5 us -> 18.9 us
  local copies, waits for them, and re-layouts: 11.4 us -> 2.21 us
  waiting for transfers between devices: 14.2 us -> 5.01 us
    pallas_call x0 -> x4, Pallas kernels: none -> 12.1 us  [the longest x1 5.77 us: per_device(): call(own_kernel, (jax.ShapeDtypeStruct((blocks, 2 * HALO, LANES), f32), j...]
    dot_general x23 -> x0, matrix products: 10.3 us -> none  [the longest x1 3.7 us: window_spectra(): jnp.einsum('cbj,ji->cbi', time_blocks[:, 1:], taps_now, precision=lax.Pre...]
    ppermute x7, starting transfers between devices: 28.5 us -> 18.9 us  [the longest x4 11.1 us: per_device(): lax.ppermute(gathered, 'chan', [((i + step) % chan, i) for i in range(cha...]
    ppermute x7, waiting for transfers between devices: 14.2 us -> 5.01 us  [the longest x1 3.47 us: per_device(): after = lax.ppermute(head, 'chan', [(i + 1, i) for i in range(chan - 1)])]
    add x3 -> x1, other arithmetic: 8.85 us -> 0.01 us  [toeplitz(): lag = (target + LANES - source)[:, :, None]]
    div x4 -> x0, local copies, waits for them, and re-layouts: 3.64 us -> none  [window_spectra(): normalized = window_data / jnp.sqrt(window_power + epsilon)]
    div x1 -> x0, other arithmetic: 1.85 us -> none  [window_spectra(): normalized = window_data / jnp.sqrt(window_power + epsilon)]
    reshape x1 -> x0, local copies, waits for them, and re-layouts: 1.72 us -> none  [window_spectra(): time_blocks = mixed_rows.reshape(row_count, -1, 128)]
  transfers between devices with their start and end apart: 7 -> 7, of which waited for: 5 -> 2; matrix products, arithmetic and copies ran while one was open for 7% -> 7% of each run, Pallas kernels for 0% -> 13%
where the time goes in v1:
time: 47.9 us; the launch traced here: 47.4 us
  starting transfers between devices  18.9 us (39%)
  Pallas kernels  12.1 us (25%)
  blocking collectives  6.85 us (14%)
  waiting for transfers between devices  5.01 us (10%)
  local copies, waits for them, and re-layouts  2.21 us (5%)
  other arithmetic  2.11 us (4%)
    ppermute x4, starting transfers between devices, per_device(): lax.ppermute(gathered, 'chan', [((i + step) % chan, i) for i in range(cha...  11.1 us
    all_to_all x1, blocking collectives, per_device(): lax.all_to_all(pieces, 'rep', split_axis=0, concat_axis=0, tiled=True)  6.85 us
    pallas_call x1, Pallas kernels, per_device(): call(own_kernel, (jax.ShapeDtypeStruct((blocks, 2 * HALO, LANES), f32), j...  5.77 us
    pallas_call x1, Pallas kernels, per_device(): call(edge_kernel, jax.ShapeDtypeStruct((rep, windows * 2 * GROUP // LANES...  4.68 us
    ppermute x1, starting transfers between devices, per_device(): before = lax.ppermute(tail, 'chan', [(i, i + 1) for i in range(chan - 1)])  4.24 us
    ppermute x1, waiting for transfers between devices, per_device(): after = lax.ppermute(head, 'chan', [(i + 1, i) for i in range(chan - 1)])  3.47 us
    ppermute x1, starting transfers between devices, per_device(): lax.ppermute(strain[:, samples - LANES:], 'rep', [(i, i + 1) for i in ran...  2.34 us
    ppermute x4, waiting for transfers between devices, per_device(): lax.ppermute(gathered, 'chan', [((i + step) % chan, i) for i in range(cha...  1.54 us
  transfers between devices with their start and end apart: 7, of which 2 were waited for; matrix products, arithmetic and copies ran while one was open for 7% of the time, Pallas kernels for 13%

profile of v1, /device:TPU:0, one launch (start us, length us, event | category | flops | bytes accessed | tf_op | source)
XLA Modules:
  0.0 47.4 jit_solution(18051748543611075717)
XLA Ops:
  0.0 0.7 %slice.30 = bf16[16,128]{1,0:T(8,128)(2,1)S(1)} slice(bf16[16,32768]{1,0:T(8,128)(2,1)} %strain_ref.1), slice={[0:16], [32640:32768]} | slice | bytes 8192 | tf_op jit(solution)/shard_map/slice | solution.py:230
  0.7 2.3 %collective-permute-start = (bf16[16,128]{1,0:T(8,128)(2,1)S(1)}, bf16[16,128]{1,0:T(8,128)(2,1)S(1)}, u32[]{:S(2)}, u32[]{:S(2)}) collective-permute-start(bf16[16,128]{1,0:T(8,128)(2,1)S(1)} %slice.30), channel_id=1, source_target_pairs={{0,1},{1,2},{2,3},{4,5},{5,6},{6,7},{8,9},{9,10},{10,11},{12,13},{... | collective-permute-start | bytes 12296 | tf_op jit(solution)/shard_map/ppermute | solution.py:230
  3.1 0.7 %select_reduce_fusion.1 = f32[16,24]{1,0:T(8,128)S(1)} fusion(f32[9]{0:T(128)} %param.6, s32[16,24]{1,0:T(8,128)S(1)} %iota_subtract_fusion.1), kind=kLoop, calls=%fused_computation.9 | loop fusion | flops 9984 | bytes 3108 | tf_op jit(solution)/shard_map/reduce_sum | solution.py:69
  3.8 0.1 reduce-precision_convert_fusion.1
  3.9 1.4 %fusion.3 = (bf16[4,32768]{1,0:T(4,128)(2,1)S(1)}, bf16[4,32768]{1,0:T(4,128)(2,1)S(1)}) fusion(bf16[16,32768]{1,0:T(8,128)(2,1)} %strain_ref.1), kind=kLoop, calls=%fused_computation.23 | loop fusion | bytes 1048576 | tf_op jit(solution)/shard_map/slice | solution.py:232
  5.3 0.0 copy-start
  5.3 0.0 copy-start.1
  5.4 0.1 fusion.5
  5.5 0.9 %select_reduce_fusion = f32[256,128]{1,0:T(8,128)S(1)} fusion(f32[60]{0:T(128)S(1)} %copy-done.2, s32[256,128]{1,0:T(8,128)S(1)} %iota_subtract_fusion), kind=kLoop, calls=%fused_computation | loop fusion | flops 5865472 | bytes 262384 | tf_op jit(solution)/shard_map/reduce_sum | solution.py:62
  6.4 0.1 reduce-precision_convert_fusion.2
  6.5 0.1 pad_maximum_fusion
  6.6 4.2 %collective-permute-start.1 = (bf16[4,32896]{1,0:T(4,128)(2,1)S(1)}, bf16[4,32896]{1,0:T(4,128)(2,1)S(1)}, u32[]{:S(2)}, u32[]{:S(2)}) collective-permute-start(bf16[4,32896]{1,0:T(4,128)(2,1)S(1)} %pad_maximum_fusion), channel_id=1, source_target_pairs={{0,4},{4,8},{8,12},{12,16},{16,20},{20,24},{24,28},{1,5},{5,9},{9,... | collective-permute-start | bytes 789512 | tf_op jit(solution)/shard_map/ppermute | solution.py:233
  10.9 0.1 pad_maximum_fusion.1
  11.0 1.3 %collective-permute-start.2 = (bf16[4,32896]{1,0:T(4,128)(2,1)S(1)}, bf16[4,32896]{1,0:T(4,128)(2,1)S(1)}, u32[]{:S(2)}, u32[]{:S(2)}) collective-permute-start(bf16[4,32896]{1,0:T(4,128)(2,1)S(1)} %pad_maximum_fusion.1), channel_id=1, source_target_pairs={{4,0},{8,4},{12,8},{16,12},{20,16},{24,20},{28,24},{5,1},{9,5},{13... | collective-permute-start | bytes 789512 | tf_op jit(solution)/shard_map/ppermute | solution.py:234
  12.3 5.8 %shard_map.46 = (f32[256,8,128]{2,1,0:T(8,128)S(1)}, f32[32,16,128]{2,1,0:T(8,128)S(1)}) custom-call(bf16[16,32768]{1,0:T(8,128)(2,1)S(1)} %copy-done, bf16[16,128]{1,0:T(8,128)(2,1)S(1)} %collective-permute-done.history_ref, bf16[32,16]{1,0:T(8,128)(2,1)S(1)} %pad_maximum_fusion.3.mix_ref, bf16[256,256]{1,0:T(8,128)(2,1)S(1)} %pad_maximum_fusion.2.toeplitz_ref, ...), custom_call_target="tpu_custom_call" | custom-call | flops 1073741824 | bytes 4194304 | tf_op jit(solution)/shard_map/pallas_call | solution.py:244
  18.1 3.5 %collective-permute-done.2.after_ref = bf16[4,32896]{1,0:T(4,128)(2,1)S(1)} collective-permute-done((bf16[4,32896]{1,0:T(4,128)(2,1)S(1)}, bf16[4,32896]{1,0:T(4,128)(2,1)S(1)}, u32[]{:S(2)}, u32[]{:S(2)}) %collective-permute-start.2) | collective-permute-done | bytes 263200 | tf_op jit(solution)/shard_map/ppermute | solution.py:234
  21.6 4.7 %shard_map.47 = bf16[4,4,16,128]{3,2,1,0:T(8,128)(2,1)S(1)} custom-call(bf16[4,32896]{1,0:T(4,128)(2,1)S(1)} %collective-permute-done.1.before_ref, bf16[4,32896]{1,0:T(4,128)(2,1)S(1)} %collective-permute-done.2.after_ref, f32[256,8,128]{2,1,0:T(8,128)S(1)} %get-tuple-element.7.edge_ref, f32[32,16,128]{2,1,0:T(8,128)S(1)} %get-tuple-element.8.own_ref, ...), custom_call_target="tpu_custom_call" | custom-call | flops 536870912 | bytes 2097152 | tf_op jit(solution)/shard_map/pallas_call | solution.py:255
  26.3 6.8 %all_to_all.5 = bf16[4,4,16,128]{3,2,1,0:T(8,128)(2,1)S(1)} all-to-all(bf16[4,4,16,128]{3,2,1,0:T(8,128)(2,1)S(1)} %shard_map.47), channel_id=1, replica_groups=mesh['chan'=8,'rep'=4] {'rep'}, dimensions={0} | all-to-all | bytes 131072 | tf_op jit(solution)/shard_map/all_to_all | solution.py:266
  33.1 5.7 %collective-permute-start.6 = (bf16[16,16,128]{2,1,0:T(8,128)(2,1)S(1)}, bf16[16,16,128]{2,1,0:T(8,128)(2,1)S(1)}, u32[]{:S(2)}, u32[]{:S(2)}) collective-permute-start(bf16[16,16,128]{2,1,0:T(8,128)(2,1)S(1)} %bitcast.1), channel_id=1, source_target_pairs={{16,0},{20,4},{24,8},{28,12},{0,16},{4,20},{8,24},{12,28},{17,1},{... | collective-permute-start | bytes 196616 | tf_op jit(solution)/shard_map/ppermute | solution.py:270
  38.8 2.9 %collective-permute-start.4 = (bf16[16,16,128]{2,1,0:T(8,128)(2,1)S(1)}, bf16[16,16,128]{2,1,0:T(8,128)(2,1)S(1)}, u32[]{:S(2)}, u32[]{:S(2)}) collective-permute-start(bf16[16,16,128]{2,1,0:T(8,128)(2,1)S(1)} %bitcast.3), channel_id=1, source_target_pairs={{8,0},{12,4},{16,8},{20,12},{24,16},{28,20},{0,24},{4,28},{9,1},{1... | collective-permute-start | bytes 196616 | tf_op jit(solution)/shard_map/ppermute | solution.py:270
  41.7 2.5 %collective-permute-start.3 = (bf16[16,16,128]{2,1,0:T(8,128)(2,1)S(1)}, bf16[16,16,128]{2,1,0:T(8,128)(2,1)S(1)}, u32[]{:S(2)}, u32[]{:S(2)}) collective-permute-start(bf16[16,16,128]{2,1,0:T(8,128)(2,1)S(1)} %bitcast.4), channel_id=1, source_target_pairs={{4,0},{8,4},{12,8},{16,12},{20,16},{24,20},{28,24},{0,28},{5,1},{9... | collective-permute-start | bytes 196616 | tf_op jit(solution)/shard_map/ppermute | solution.py:270
  44.2 0.3 shard_map.48.refs_0_
  44.6 1.5 %collective-permute-done.3.refs_2_ = bf16[16,16,128]{2,1,0:T(8,128)(2,1)S(1)} collective-permute-done((bf16[16,16,128]{2,1,0:T(8,128)(2,1)S(1)}, bf16[16,16,128]{2,1,0:T(8,128)(2,1)S(1)}, u32[]{:S(2)}, u32[]{:S(2)}) %collective-permute-start.3) | collective-permute-done | bytes 65568 | tf_op jit(solution)/shard_map/ppermute | solution.py:270
  46.1 1.3 %shard_map.49 = f32[16,5,8,32]{3,2,1,0:T(8,128)} custom-call(bf16[2,128,2048]{2,1,0:T(8,128)(2,1)S(1)} %shard_map.48.refs_0_, bf16[16,16,128]{2,1,0:T(8,128)(2,1)S(1)} %bitcast.6, bf16[16,16,128]{2,1,0:T(8,128)(2,1)S(1)} %collective-permute-done.3.refs_2_, bf16[16,16,128]{2,1,0:T(8,128)(2,1)S(1)} %collective-permute-done.4.refs_3_, ...), custom_call_target="tpu_custom_call" | custom-call | flops 16777216 | bytes 1048576 | tf_op jit(solution)/shard_map/pallas_call | solution.py:279
  (20 shorter events, 0.1 us)
Async XLA Ops:
  0.0 5.5 %copy-start.2 = (f32[60]{0:T(128)S(1)}, f32[60]{0:T(128)}, u32[]{:S(2)}) copy-start(f32[60]{0:T(128)} %param.5) | copy-start | bytes 724
  0.7 5.8 %collective-permute-start = (bf16[16,128]{1,0:T(8,128)(2,1)S(1)}, bf16[16,128]{1,0:T(8,128)(2,1)S(1)}, u32[]{:S(2)}, u32[]{:S(2)}) collective-permute-start(bf16[16,128]{1,0:T(8,128)(2,1)S(1)} %slice.30), channel_id=1, source_target_pairs={{0,1},{1,2},{2,3},{4,5},{5,6},{6,7},{8,9},{9,10},{10,11},{12,13},{... | collective-permute-start | bytes 12296 | tf_op jit(solution)/shard_map/ppermute | solution.py:230
  5.3 7.0 %copy-start = (bf16[16,32768]{1,0:T(8,128)(2,1)S(1)}, bf16[16,32768]{1,0:T(8,128)(2,1)}, u32[]{:S(2)}) copy-start(bf16[16,32768]{1,0:T(8,128)(2,1)} %strain_ref.1) | copy-start | bytes 3145732
  5.3 7.0 %copy-start.1 = (bf16[1024,128]{1,0:T(8,128)(2,1)S(1)}, bf16[1024,128]{1,0:T(8,128)(2,1)}, u32[]{:S(2)}) copy-start(bf16[1024,128]{1,0:T(8,128)(2,1)} %constant.6.clone.dft_ref) | copy-start | bytes 786436
  6.6 11.5 %collective-permute-start.1 = (bf16[4,32896]{1,0:T(4,128)(2,1)S(1)}, bf16[4,32896]{1,0:T(4,128)(2,1)S(1)}, u32[]{:S(2)}, u32[]{:S(2)}) collective-permute-start(bf16[4,32896]{1,0:T(4,128)(2,1)S(1)} %pad_maximum_fusion), channel_id=1, source_target_pairs={{0,4},{4,8},{8,12},{12,16},{16,20},{20,24},{24,28},{1,5},{5,9},{9,... | collective-permute-start | bytes 789512 | tf_op jit(solution)/shard_map/ppermute | solution.py:233
  11.0 10.6 %collective-permute-start.2 = (bf16[4,32896]{1,0:T(4,128)(2,1)S(1)}, bf16[4,32896]{1,0:T(4,128)(2,1)S(1)}, u32[]{:S(2)}, u32[]{:S(2)}) collective-permute-start(bf16[4,32896]{1,0:T(4,128)(2,1)S(1)} %pad_maximum_fusion.1), channel_id=1, source_target_pairs={{4,0},{8,4},{12,8},{16,12},{20,16},{24,20},{28,24},{5,1},{9,5},{13... | collective-permute-start | bytes 789512 | tf_op jit(solution)/shard_map/ppermute | solution.py:234
  33.1 11.4 %collective-permute-start.6 = (bf16[16,16,128]{2,1,0:T(8,128)(2,1)S(1)}, bf16[16,16,128]{2,1,0:T(8,128)(2,1)S(1)}, u32[]{:S(2)}, u32[]{:S(2)}) collective-permute-start(bf16[16,16,128]{2,1,0:T(8,128)(2,1)S(1)} %bitcast.1), channel_id=1, source_target_pairs={{16,0},{20,4},{24,8},{28,12},{0,16},{4,20},{8,24},{12,28},{17,1},{... | collective-permute-start | bytes 196616 | tf_op jit(solution)/shard_map/ppermute | solution.py:270
  38.8 5.8 %collective-permute-start.5 = (bf16[16,16,128]{2,1,0:T(8,128)(2,1)S(1)}, bf16[16,16,128]{2,1,0:T(8,128)(2,1)S(1)}, u32[]{:S(2)}, u32[]{:S(2)}) collective-permute-start(bf16[16,16,128]{2,1,0:T(8,128)(2,1)S(1)} %bitcast.2), channel_id=1, source_target_pairs={{12,0},{16,4},{20,8},{24,12},{28,16},{0,20},{4,24},{8,28},{13,1},{... | collective-permute-start | bytes 196616 | tf_op jit(solution)/shard_map/ppermute | solution.py:270
  38.8 5.8 %collective-permute-start.4 = (bf16[16,16,128]{2,1,0:T(8,128)(2,1)S(1)}, bf16[16,16,128]{2,1,0:T(8,128)(2,1)S(1)}, u32[]{:S(2)}, u32[]{:S(2)}) collective-permute-start(bf16[16,16,128]{2,1,0:T(8,128)(2,1)S(1)} %bitcast.3), channel_id=1, source_target_pairs={{8,0},{12,4},{16,8},{20,12},{24,16},{28,20},{0,24},{4,28},{9,1},{1... | collective-permute-start | bytes 196616 | tf_op jit(solution)/shard_map/ppermute | solution.py:270
  41.7 4.4 %collective-permute-start.3 = (bf16[16,16,128]{2,1,0:T(8,128)(2,1)S(1)}, bf16[16,16,128]{2,1,0:T(8,128)(2,1)S(1)}, u32[]{:S(2)}, u32[]{:S(2)}) collective-permute-start(bf16[16,16,128]{2,1,0:T(8,128)(2,1)S(1)} %bitcast.4), channel_id=1, source_target_pairs={{4,0},{8,4},{12,8},{16,12},{20,16},{24,20},{28,24},{0,28},{5,1},{9... | collective-permute-start | bytes 196616 | tf_op jit(solution)/shard_map/ppermute | solution.py:270

commit v2 on v1

--- a/solution.py
+++ b/solution.py
@@ -115,7 +115,7 @@
         return jnp.concatenate([high, low], axis=0)
 
     mixed_ref[:, :LANES] = mix(history_ref[...])
-    step = 4 * NFFT
+    step = samples // 2
 
     def mix_step(i, _):
         start = pl.multiple_of(i * step, step)
@@ -141,7 +141,7 @@
 ):
     rows = 2 * HALO
     width = before_ref.shape[1]
-    step = 4 * NFFT
+    step = width // LANES * LANES - LANES
 
     def mix(start, size):
         near = before_ref[:, pl.ds(start, size)].astype(f32)
@@ -230,6 +230,7 @@
     history = lax.ppermute(strain[:, samples - LANES :], "rep", [(i, i + 1) for i in range(rep - 1)])
     tail = jnp.concatenate([history[rows - HALO :], strain[rows - HALO :]], axis=1)
     head = jnp.concatenate([history[:HALO], strain[:HALO]], axis=1)
+    tail, head, fir_taps, spatial = lax.optimization_barrier((tail, head, fir_taps, spatial))
     before = lax.ppermute(tail, "chan", [(i, i + 1) for i in range(chan - 1)])
     after = lax.ppermute(head, "chan", [(i + 1, i) for i in range(chan - 1)])
 

time: 47.9 us -> 44.6 us (0.931)
  Pallas kernels: 12.1 us -> 7.18 us
  waiting for transfers between devices: 5.01 us -> 7.95 us
  other arithmetic: 2.11 us -> 1.45 us
    ppermute x1, waiting for transfers between devices: 0.01 us -> 6.4 us  [per_device(): before = lax.ppermute(tail, 'chan', [(i, i + 1) for i in range(chan - 1)])]
    ppermute x1, waiting for transfers between devices: 3.47 us -> 0.01 us  [per_device(): after = lax.ppermute(head, 'chan', [(i + 1, i) for i in range(chan - 1)])]
    pallas_call x1, Pallas kernels: 4.68 us -> 2 us  [per_device(): call(edge_kernel, jax.ShapeDtypeStruct((rep, windows * 2 * GROUP // LANES...]
    pallas_call x1, Pallas kernels: 5.77 us -> 3.52 us  [per_device(): call(own_kernel, (jax.ShapeDtypeStruct((blocks, 2 * HALO, LANES), f32), j...]
    reduce_sum x1, other arithmetic: 0.74 us -> 0.08 us  [mixing(): jnp.sum(jnp.where(offset == jnp.arange(span, dtype=jnp.int32), spatial, 0...]
  transfers between devices with their start and end apart: 7 -> 7, of which waited for: 2 -> 2; matrix products, arithmetic and copies ran while one was open for 7% -> 4% of each run, Pallas kernels for 13% -> 9%
where the time goes in v2:
time: 44.6 us; the launch traced here: 44.1 us
  starting transfers between devices  18.6 us (42%)
  waiting for transfers between devices  7.95 us (18%)
  Pallas kernels  7.18 us (16%)
  blocking collectives  6.5 us (15%)
  local copies, waits for them, and re-layouts  2.21 us (5%)
  other arithmetic  1.45 us (3%)
    ppermute x4, starting transfers between devices, per_device(): lax.ppermute(gathered, 'chan', [((i + step) % chan, i) for i in range(cha...  10.8 us
    all_to_all x1, blocking collectives, per_device(): lax.all_to_all(pieces, 'rep', split_axis=0, concat_axis=0, tiled=True)  6.5 us
    ppermute x1, waiting for transfers between devices, per_device(): before = lax.ppermute(tail, 'chan', [(i, i + 1) for i in range(chan - 1)])  6.4 us
    ppermute x1, starting transfers between devices, per_device(): before = lax.ppermute(tail, 'chan', [(i, i + 1) for i in range(chan - 1)])  4.23 us
    pallas_call x1, Pallas kernels, per_device(): call(own_kernel, (jax.ShapeDtypeStruct((blocks, 2 * HALO, LANES), f32), j...  3.52 us
    ppermute x1, starting transfers between devices, per_device(): lax.ppermute(strain[:, samples - LANES:], 'rep', [(i, i + 1) for i in ran...  2.34 us
    pallas_call x1, Pallas kernels, per_device(): call(edge_kernel, jax.ShapeDtypeStruct((rep, windows * 2 * GROUP // LANES...  2 us
    ppermute x4, waiting for transfers between devices, per_device(): lax.ppermute(gathered, 'chan', [((i + step) % chan, i) for i in range(cha...  1.54 us
  transfers between devices with their start and end apart: 7, of which 2 were waited for; matrix products, arithmetic and copies ran while one was open for 4% of the time, Pallas kernels for 9%

profile of v2, /device:TPU:0, one launch (start us, length us, event | category | flops | bytes accessed | tf_op | source)
XLA Modules:
  0.0 44.1 jit_solution(17495922618049560699)
XLA Ops:
  0.0 0.7 %slice.30 = bf16[16,128]{1,0:T(8,128)(2,1)S(1)} slice(bf16[16,32768]{1,0:T(8,128)(2,1)} %strain_ref.1), slice={[0:16], [32640:32768]} | slice | bytes 8192 | tf_op jit(solution)/shard_map/slice | solution.py:230
  0.7 2.3 %collective-permute-start = (bf16[16,128]{1,0:T(8,128)(2,1)S(1)}, bf16[16,128]{1,0:T(8,128)(2,1)S(1)}, u32[]{:S(2)}, u32[]{:S(2)}) collective-permute-start(bf16[16,128]{1,0:T(8,128)(2,1)S(1)} %slice.30), channel_id=1, source_target_pairs={{0,1},{1,2},{2,3},{4,5},{5,6},{6,7},{8,9},{9,10},{10,11},{12,13},{... | collective-permute-start | bytes 12296 | tf_op jit(solution)/shard_map/ppermute | solution.py:230
  3.1 0.0 copy-start.3
  3.1 0.0 copy-start.2
  3.1 1.4 %fusion.3 = (bf16[4,32768]{1,0:T(4,128)(2,1)S(1)}, bf16[4,32768]{1,0:T(4,128)(2,1)S(1)}) fusion(bf16[16,32768]{1,0:T(8,128)(2,1)} %strain_ref.1), kind=kLoop, calls=%fused_computation.23 | loop fusion | bytes 1048576 | tf_op jit(solution)/shard_map/slice | solution.py:232
  4.5 0.0 copy-start.1
  4.6 0.2 pad_maximum_fusion
  4.8 0.1 select_reduce_fusion.1
  4.9 0.1 reduce-precision_convert_fusion.1
  5.0 0.9 %select_reduce_fusion = f32[256,128]{1,0:T(8,128)S(1)} fusion(f32[60]{0:T(128)S(1)} %copy-done.2, s32[256,128]{1,0:T(8,128)S(1)} %iota_subtract_fusion), kind=kLoop, calls=%fused_computation | loop fusion | flops 5865472 | bytes 262384 | tf_op jit(solution)/shard_map/reduce_sum | solution.py:62
  5.9 0.1 fusion.5
  6.0 4.2 %collective-permute-start.1 = (bf16[4,32896]{1,0:T(4,128)(2,1)S(1)}, bf16[4,32896]{1,0:T(4,128)(2,1)S(1)}, u32[]{:S(2)}, u32[]{:S(2)}) collective-permute-start(bf16[4,32896]{1,0:T(4,128)(2,1)S(1)} %get-tuple-element.11), channel_id=1, source_target_pairs={{0,4},{4,8},{8,12},{12,16},{16,20},{20,24},{24,28},{1,5},{5,9},{9,... | collective-permute-start | bytes 789512 | tf_op jit(solution)/shard_map/ppermute | solution.py:234
  10.3 1.3 %collective-permute-start.2 = (bf16[4,32896]{1,0:T(4,128)(2,1)S(1)}, bf16[4,32896]{1,0:T(4,128)(2,1)S(1)}, u32[]{:S(2)}, u32[]{:S(2)}) collective-permute-start(bf16[4,32896]{1,0:T(4,128)(2,1)S(1)} %get-tuple-element.12), channel_id=1, source_target_pairs={{4,0},{8,4},{12,8},{16,12},{20,16},{24,20},{28,24},{5,1},{9,5},{13... | collective-permute-start | bytes 789512 | tf_op jit(solution)/shard_map/ppermute | solution.py:235
  11.6 3.5 %shard_map.46 = (f32[256,8,128]{2,1,0:T(8,128)S(1)}, f32[32,16,128]{2,1,0:T(8,128)S(1)}) custom-call(bf16[16,32768]{1,0:T(8,128)(2,1)S(1)} %copy-done, bf16[16,128]{1,0:T(8,128)(2,1)S(1)} %collective-permute-done.history_ref, bf16[32,16]{1,0:T(8,128)(2,1)S(1)} %pad_maximum_fusion.3.mix_ref, bf16[256,256]{1,0:T(8,128)(2,1)S(1)} %pad_maximum_fusion.2.toeplitz_ref, ...), custom_call_target="tpu_custom_call" | custom-call | flops 1073741824 | bytes 4194304 | tf_op jit(solution)/shard_map/pallas_call | solution.py:245
  15.1 0.1 reduce-precision_convert_fusion.2
  15.2 6.4 %collective-permute-done.1.before_ref = bf16[4,32896]{1,0:T(4,128)(2,1)S(1)} collective-permute-done((bf16[4,32896]{1,0:T(4,128)(2,1)S(1)}, bf16[4,32896]{1,0:T(4,128)(2,1)S(1)}, u32[]{:S(2)}, u32[]{:S(2)}) %collective-permute-start.1) | collective-permute-done | bytes 263200 | tf_op jit(solution)/shard_map/ppermute | solution.py:234
  21.6 2.0 %shard_map.47 = bf16[4,4,16,128]{3,2,1,0:T(8,128)(2,1)S(1)} custom-call(bf16[4,32896]{1,0:T(4,128)(2,1)S(1)} %collective-permute-done.1.before_ref, bf16[4,32896]{1,0:T(4,128)(2,1)S(1)} %collective-permute-done.2.after_ref, f32[256,8,128]{2,1,0:T(8,128)S(1)} %get-tuple-element.15.edge_ref, f32[32,16,128]{2,1,0:T(8,128)S(1)} %get-tuple-element.16.own_ref, ...), custom_call_target="tpu_custom_call" | custom-call | flops 536870912 | bytes 2097152 | tf_op jit(solution)/shard_map/pallas_call | solution.py:256
  23.6 6.5 %all_to_all.5 = bf16[4,4,16,128]{3,2,1,0:T(8,128)(2,1)S(1)} all-to-all(bf16[4,4,16,128]{3,2,1,0:T(8,128)(2,1)S(1)} %shard_map.47), channel_id=1, replica_groups=mesh['chan'=8,'rep'=4] {'rep'}, dimensions={0} | all-to-all | bytes 131072 | tf_op jit(solution)/shard_map/all_to_all | solution.py:267
  30.1 5.4 %collective-permute-start.6 = (bf16[16,16,128]{2,1,0:T(8,128)(2,1)S(1)}, bf16[16,16,128]{2,1,0:T(8,128)(2,1)S(1)}, u32[]{:S(2)}, u32[]{:S(2)}) collective-permute-start(bf16[16,16,128]{2,1,0:T(8,128)(2,1)S(1)} %bitcast.1), channel_id=1, source_target_pairs={{16,0},{20,4},{24,8},{28,12},{0,16},{4,20},{8,24},{12,28},{17,1},{... | collective-permute-start | bytes 196616 | tf_op jit(solution)/shard_map/ppermute | solution.py:271
  35.5 2.9 %collective-permute-start.4 = (bf16[16,16,128]{2,1,0:T(8,128)(2,1)S(1)}, bf16[16,16,128]{2,1,0:T(8,128)(2,1)S(1)}, u32[]{:S(2)}, u32[]{:S(2)}) collective-permute-start(bf16[16,16,128]{2,1,0:T(8,128)(2,1)S(1)} %bitcast.3), channel_id=1, source_target_pairs={{8,0},{12,4},{16,8},{20,12},{24,16},{28,20},{0,24},{4,28},{9,1},{1... | collective-permute-start | bytes 196616 | tf_op jit(solution)/shard_map/ppermute | solution.py:271
  38.4 2.5 %collective-permute-start.3 = (bf16[16,16,128]{2,1,0:T(8,128)(2,1)S(1)}, bf16[16,16,128]{2,1,0:T(8,128)(2,1)S(1)}, u32[]{:S(2)}, u32[]{:S(2)}) collective-permute-start(bf16[16,16,128]{2,1,0:T(8,128)(2,1)S(1)} %bitcast.4), channel_id=1, source_target_pairs={{4,0},{8,4},{12,8},{16,12},{20,16},{24,20},{28,24},{0,28},{5,1},{9... | collective-permute-start | bytes 196616 | tf_op jit(solution)/shard_map/ppermute | solution.py:271
  40.9 0.3 shard_map.48.refs_0_
  41.3 1.5 %collective-permute-done.3.refs_2_ = bf16[16,16,128]{2,1,0:T(8,128)(2,1)S(1)} collective-permute-done((bf16[16,16,128]{2,1,0:T(8,128)(2,1)S(1)}, bf16[16,16,128]{2,1,0:T(8,128)(2,1)S(1)}, u32[]{:S(2)}, u32[]{:S(2)}) %collective-permute-start.3) | collective-permute-done | bytes 65568 | tf_op jit(solution)/shard_map/ppermute | solution.py:271
  42.8 1.3 %shard_map.49 = f32[16,5,8,32]{3,2,1,0:T(8,128)} custom-call(bf16[2,128,2048]{2,1,0:T(8,128)(2,1)S(1)} %shard_map.48.refs_0_, bf16[16,16,128]{2,1,0:T(8,128)(2,1)S(1)} %bitcast.6, bf16[16,16,128]{2,1,0:T(8,128)(2,1)S(1)} %collective-permute-done.3.refs_2_, bf16[16,16,128]{2,1,0:T(8,128)(2,1)S(1)} %collective-permute-done.4.refs_3_, ...), custom_call_target="tpu_custom_call" | custom-call | flops 16777216 | bytes 1048576 | tf_op jit(solution)/shard_map/pallas_call | solution.py:280
  (21 shorter events, 0.1 us)
Async XLA Ops:
  0.7 3.9 %collective-permute-start = (bf16[16,128]{1,0:T(8,128)(2,1)S(1)}, bf16[16,128]{1,0:T(8,128)(2,1)S(1)}, u32[]{:S(2)}, u32[]{:S(2)}) collective-permute-start(bf16[16,128]{1,0:T(8,128)(2,1)S(1)} %slice.30), channel_id=1, source_target_pairs={{0,1},{1,2},{2,3},{4,5},{5,6},{6,7},{8,9},{9,10},{10,11},{12,13},{... | collective-permute-start | bytes 12296 | tf_op jit(solution)/shard_map/ppermute | solution.py:230
  3.1 1.8 %copy-start.3 = (f32[9]{0:T(128)S(1)}, f32[9]{0:T(128)}, u32[]{:S(2)}) copy-start(f32[9]{0:T(128)} %param.6) | copy-start | bytes 112
  3.1 1.9 %copy-start.2 = (f32[60]{0:T(128)S(1)}, f32[60]{0:T(128)}, u32[]{:S(2)}) copy-start(f32[60]{0:T(128)} %param.5) | copy-start | bytes 724
  4.5 7.1 %copy-start = (bf16[16,32768]{1,0:T(8,128)(2,1)S(1)}, bf16[16,32768]{1,0:T(8,128)(2,1)}, u32[]{:S(2)}) copy-start(bf16[16,32768]{1,0:T(8,128)(2,1)} %strain_ref.1) | copy-start | bytes 3145732
  4.5 7.1 %copy-start.1 = (bf16[1024,128]{1,0:T(8,128)(2,1)S(1)}, bf16[1024,128]{1,0:T(8,128)(2,1)}, u32[]{:S(2)}) copy-start(bf16[1024,128]{1,0:T(8,128)(2,1)} %constant.6.clone.dft_ref) | copy-start | bytes 786436
  6.0 15.6 %collective-permute-start.1 = (bf16[4,32896]{1,0:T(4,128)(2,1)S(1)}, bf16[4,32896]{1,0:T(4,128)(2,1)S(1)}, u32[]{:S(2)}, u32[]{:S(2)}) collective-permute-start(bf16[4,32896]{1,0:T(4,128)(2,1)S(1)} %get-tuple-element.11), channel_id=1, source_target_pairs={{0,4},{4,8},{8,12},{12,16},{16,20},{20,24},{24,28},{1,5},{5,9},{9,... | collective-permute-start | bytes 789512 | tf_op jit(solution)/shard_map/ppermute | solution.py:234
  10.3 11.4 %collective-permute-start.2 = (bf16[4,32896]{1,0:T(4,128)(2,1)S(1)}, bf16[4,32896]{1,0:T(4,128)(2,1)S(1)}, u32[]{:S(2)}, u32[]{:S(2)}) collective-permute-start(bf16[4,32896]{1,0:T(4,128)(2,1)S(1)} %get-tuple-element.12), channel_id=1, source_target_pairs={{4,0},{8,4},{12,8},{16,12},{20,16},{24,20},{28,24},{5,1},{9,5},{13... | collective-permute-start | bytes 789512 | tf_op jit(solution)/shard_map/ppermute | solution.py:235
  30.1 11.1 %collective-permute-start.6 = (bf16[16,16,128]{2,1,0:T(8,128)(2,1)S(1)}, bf16[16,16,128]{2,1,0:T(8,128)(2,1)S(1)}, u32[]{:S(2)}, u32[]{:S(2)}) collective-permute-start(bf16[16,16,128]{2,1,0:T(8,128)(2,1)S(1)} %bitcast.1), channel_id=1, source_target_pairs={{16,0},{20,4},{24,8},{28,12},{0,16},{4,20},{8,24},{12,28},{17,1},{... | collective-permute-start | bytes 196616 | tf_op jit(solution)/shard_map/ppermute | solution.py:271
  35.5 5.8 %collective-permute-start.5 = (bf16[16,16,128]{2,1,0:T(8,128)(2,1)S(1)}, bf16[16,16,128]{2,1,0:T(8,128)(2,1)S(1)}, u32[]{:S(2)}, u32[]{:S(2)}) collective-permute-start(bf16[16,16,128]{2,1,0:T(8,128)(2,1)S(1)} %bitcast.2), channel_id=1, source_target_pairs={{12,0},{16,4},{20,8},{24,12},{28,16},{0,20},{4,24},{8,28},{13,1},{... | collective-permute-start | bytes 196616 | tf_op jit(solution)/shard_map/ppermute | solution.py:271
  35.5 5.8 %collective-permute-start.4 = (bf16[16,16,128]{2,1,0:T(8,128)(2,1)S(1)}, bf16[16,16,128]{2,1,0:T(8,128)(2,1)S(1)}, u32[]{:S(2)}, u32[]{:S(2)}) collective-permute-start(bf16[16,16,128]{2,1,0:T(8,128)(2,1)S(1)} %bitcast.3), channel_id=1, source_target_pairs={{8,0},{12,4},{16,8},{20,12},{24,16},{28,20},{0,24},{4,28},{9,1},{1... | collective-permute-start | bytes 196616 | tf_op jit(solution)/shard_map/ppermute | solution.py:271
  38.4 4.4 %collective-permute-start.3 = (bf16[16,16,128]{2,1,0:T(8,128)(2,1)S(1)}, bf16[16,16,128]{2,1,0:T(8,128)(2,1)S(1)}, u32[]{:S(2)}, u32[]{:S(2)}) collective-permute-start(bf16[16,16,128]{2,1,0:T(8,128)(2,1)S(1)} %bitcast.4), channel_id=1, source_target_pairs={{4,0},{8,4},{12,8},{16,12},{20,16},{24,20},{28,24},{0,28},{5,1},{9... | collective-permute-start | bytes 196616 | tf_op jit(solution)/shard_map/ppermute | solution.py:271

commit v3 on v2

--- a/solution.py
+++ b/solution.py
@@ -137,30 +137,31 @@
 
 
 def edge_kernel(
-    before_ref, after_ref, edge_ref, own_ref, mix_ref, toeplitz_ref, dft_ref, out_ref, mixed_ref, split_ref, scale_ref
+    near_ref,
+    far_ref,
+    edge_ref,
+    own_ref,
+    mix_ref,
+    toeplitz_ref,
+    dft_ref,
+    out_ref,
+    mixed_ref,
+    split_ref,
+    scale_ref,
 ):
     rows = 2 * HALO
-    width = before_ref.shape[1]
-    step = width // LANES * LANES - LANES
-
-    def mix(start, size):
-        near = before_ref[:, pl.ds(start, size)].astype(f32)
-        far = after_ref[:, pl.ds(start, size)].astype(f32)
-        out = dot(mix_ref[...], jnp.concatenate([near, far], axis=0).astype(bf16))
+    step = near_ref.shape[1] - LANES
+
+    def mix(near, far):
+        both = jnp.concatenate([near.astype(f32), far.astype(f32)], axis=0).astype(bf16)
+        out = dot(mix_ref[...], both)
         out = out[:rows] + out[rows:]
         high = out.astype(bf16).astype(f32)
-        mixed_ref[:, pl.ds(start, size)] = jnp.concatenate([high, out - high], axis=0).astype(bf16)
-
-    mix(0, LANES)
-    lax.fori_loop(0, width // step, lambda i, _: (mix(pl.multiple_of(i * step + LANES, LANES), step), 0)[1], 0)
-    count = step // LANES
-
-    def filter_step(i, _):
-        band = filtered(mixed_ref, i * count, count, rows, toeplitz_ref) + edge_ref[pl.ds(i * count, count)]
-        windowed(band, i * (step // NFFT), rows, split_ref, scale_ref)
-        return 0
-
-    lax.fori_loop(0, width // step, filter_step, 0)
+        return jnp.concatenate([high, out - high], axis=0).astype(bf16)
+
+    mixed_ref[...] = mix(near_ref[...], far_ref[...])
+    band = filtered(mixed_ref, 0, step // LANES, rows, toeplitz_ref) + edge_ref[...]
+    windowed(band, 0, rows, split_ref, scale_ref)
     edges = spectra_of(split_ref, scale_ref, dft_ref, rows)
     near = lax.broadcasted_iota(jnp.int32, edges.shape, 1) < HALO
     own = own_ref[...]
@@ -227,19 +228,28 @@
     blocks = samples // LANES
     rep = lax.axis_size("rep")
     chan = lax.axis_size("chan")
+    even = lax.axis_index("chan") % 2 == 0
+    pairs_within = [(i, i ^ 1) for i in range(chan) if i ^ 1 < chan]
+    pairs_across = [(i, j) for i in range(chan) for j in (i + 1 if i % 2 else i - 1,) if 0 <= j < chan]
+
+    def rims(block):
+        head, tail = block[:HALO], block[rows - HALO :]
+        return jnp.where(even, tail, head), jnp.where(even, head, tail)
+
     history = lax.ppermute(strain[:, samples - LANES :], "rep", [(i, i + 1) for i in range(rep - 1)])
-    tail = jnp.concatenate([history[rows - HALO :], strain[rows - HALO :]], axis=1)
-    head = jnp.concatenate([history[:HALO], strain[:HALO]], axis=1)
-    tail, head, fir_taps, spatial = lax.optimization_barrier((tail, head, fir_taps, spatial))
-    before = lax.ppermute(tail, "chan", [(i, i + 1) for i in range(chan - 1)])
-    after = lax.ppermute(head, "chan", [(i + 1, i) for i in range(chan - 1)])
+    now = lax.optimization_barrier(rims(strain))
+    within, across = (jnp.concatenate(pair, axis=1) for pair in zip(rims(history), now))
+    within, across, fir_taps, spatial = lax.optimization_barrier((within, across, fir_taps, spatial))
+    near = lax.ppermute(within, "chan", pairs_within)
+    far = lax.ppermute(across, "chan", pairs_across)
 
     filter_matrix = toeplitz(fir_taps)
     table = jnp.asarray(dft_table())
     mix = mixing(spatial, rows)
     own_mix = jnp.concatenate(rounded_halves(mix[:, HALO : HALO + rows]), axis=0)
     edge_rows = jnp.concatenate([mix[:HALO], mix[rows - HALO :]], axis=0)
-    edge_mix = jnp.concatenate([edge_rows[:, :HALO], edge_rows[:, HALO + rows :]], axis=1)
+    before_mix, after_mix = edge_rows[:, :HALO], edge_rows[:, HALO + rows :]
+    edge_mix = jnp.concatenate([jnp.where(even, after_mix, before_mix), jnp.where(even, before_mix, after_mix)], axis=1)
     edge_mix = jnp.concatenate(rounded_halves(edge_mix), axis=0)
 
     edge, own = call(
@@ -263,7 +273,7 @@
         ],
         flops=2 * 2 * rows * samples * 256,
         bytes_accessed=2 * 2**20,
-    )(before, after, edge, own, edge_mix, filter_matrix, table)
+    )(near, far, edge, own, edge_mix, filter_matrix, table)
     gathered = lax.all_to_all(pieces, "rep", split_axis=0, concat_axis=0, tiled=True)
     gathered = gathered.reshape(-1, rows, LANES)
     partners = [gathered]

time: 44.6 us -> 41 us (0.919)
  starting transfers between devices: 18.6 us -> 14.3 us
  other arithmetic: 1.45 us -> 3.03 us
  local copies, waits for them, and re-layouts: 2.21 us -> 0.72 us
  waiting for transfers between devices: 7.95 us -> 8.75 us
    ppermute x2, starting transfers between devices: 5.52 us -> 2.99 us  [the longest x1 2.33 us: per_device(): near = lax.ppermute(within, 'chan', pairs_within)]
    ppermute x4, starting transfers between devices: 10.8 us -> 8.98 us  [per_device(): lax.ppermute(gathered, 'chan', [((i + step) % chan, i) for i in range(cha...]
    select_n x0 -> x3, other arithmetic: none -> 1.58 us  [the longest x2 1.51 us: rims(): return (jnp.where(even, tail, head), jnp.where(even, head, tail))]
    slice x3 -> x0, local copies, waits for them, and re-layouts: 1.49 us -> none  [the longest x2 1.42 us: per_device(): head = jnp.concatenate([history[:HALO], strain[:HALO]], axis=1)]
    ppermute x2, waiting for transfers between devices: 6.41 us -> 7.2 us  [the longest x1 7.2 us: per_device(): near = lax.ppermute(within, 'chan', pairs_within)]
  transfers between devices with their start and end apart: 7 -> 7, of which waited for: 2 -> 3; matrix products, arithmetic and copies ran while one was open for 4% -> 4% of each run, Pallas kernels for 9% -> 9%
where the time goes in v3:
time: 41 us; the launch traced here: 40.7 us
  starting transfers between devices  14.3 us (35%)
  waiting for transfers between devices  8.75 us (21%)
  Pallas kernels  7.18 us (18%)
  blocking collectives  6.49 us (16%)
  other arithmetic  3.03 us (7%)
  local copies, waits for them, and re-layouts  0.72 us (2%)
    ppermute x4, starting transfers between devices, per_device(): lax.ppermute(gathered, 'chan', [((i + step) % chan, i) for i in range(cha...  8.98 us
    ppermute x1, waiting for transfers between devices, per_device(): near = lax.ppermute(within, 'chan', pairs_within)  7.2 us
    all_to_all x1, blocking collectives, per_device(): lax.all_to_all(pieces, 'rep', split_axis=0, concat_axis=0, tiled=True)  6.49 us
    pallas_call x1, Pallas kernels, per_device(): call(own_kernel, (jax.ShapeDtypeStruct((blocks, 2 * HALO, LANES), f32), j...  3.53 us
    ppermute x1, starting transfers between devices, per_device(): lax.ppermute(strain[:, samples - LANES:], 'rep', [(i, i + 1) for i in ran...  2.34 us
    ppermute x1, starting transfers between devices, per_device(): near = lax.ppermute(within, 'chan', pairs_within)  2.33 us
    pallas_call x1, Pallas kernels, per_device(): call(edge_kernel, jax.ShapeDtypeStruct((rep, windows * 2 * GROUP // LANES...  2 us
    ppermute x4, waiting for transfers between devices, per_device(): lax.ppermute(gathered, 'chan', [((i + step) % chan, i) for i in range(cha...  1.54 us
  transfers between devices with their start and end apart: 7, of which 3 were waited for; matrix products, arithmetic and copies ran while one was open for 4% of the time, Pallas kernels for 9%

profile of v3, /device:TPU:0, one launch (start us, length us, event | category | flops | bytes accessed | tf_op | source)
XLA Modules:
  0.0 40.7 jit_solution(14709776430893582444)
XLA Ops:
  0.0 0.7 %slice.30 = bf16[16,128]{1,0:T(8,128)(2,1)S(1)} slice(bf16[16,32768]{1,0:T(8,128)(2,1)} %strain_ref.1), slice={[0:16], [32640:32768]} | slice | bytes 8192 | tf_op jit(solution)/shard_map/slice | solution.py:239
  0.7 2.3 %collective-permute-start = (bf16[16,128]{1,0:T(8,128)(2,1)S(1)}, bf16[16,128]{1,0:T(8,128)(2,1)S(1)}, u32[]{:S(2)}, u32[]{:S(2)}) collective-permute-start(bf16[16,128]{1,0:T(8,128)(2,1)S(1)} %slice.30), channel_id=1, source_target_pairs={{0,1},{1,2},{2,3},{4,5},{5,6},{6,7},{8,9},{9,10},{10,11},{12,13},{... | collective-permute-start | bytes 12296 | tf_op jit(solution)/shard_map/ppermute | solution.py:239
  3.1 1.5 %broadcast_select_fusion = (bf16[4,32768]{1,0:T(4,128)(2,1)S(1)}, bf16[4,32768]{1,0:T(4,128)(2,1)S(1)}) fusion(pred[]{:T(512)S(6)} %eq.16, bf16[16,32768]{1,0:T(8,128)(2,1)} %strain_ref.1), kind=kLoop, calls=%fused_computation.4 | loop fusion | flops 262144 | bytes 1048577 | tf_op jit(solution)/shard_map/jit(_where)/select_n | solution.py:237
  4.6 0.0 copy-start.1
  4.7 0.2 pad_maximum_fusion
  4.9 0.1 select_reduce_fusion.1
  5.0 0.1 reduce-precision_convert_fusion.1
  5.1 0.9 %select_reduce_fusion = f32[256,128]{1,0:T(8,128)S(1)} fusion(f32[60]{0:T(128)S(1)} %copy-done.2, s32[256,128]{1,0:T(8,128)S(1)} %iota_subtract_fusion), kind=kLoop, calls=%fused_computation | loop fusion | flops 5865472 | bytes 262384 | tf_op jit(solution)/shard_map/reduce_sum | solution.py:62
  6.0 0.1 slice_select_fusion.1
  6.1 2.3 %collective-permute-start.1 = (bf16[4,32896]{1,0:T(4,128)(2,1)S(1)}, bf16[4,32896]{1,0:T(4,128)(2,1)S(1)}, u32[]{:S(2)}, u32[]{:S(2)}) collective-permute-start(bf16[4,32896]{1,0:T(4,128)(2,1)S(1)} %get-tuple-element.15), channel_id=1, source_target_pairs={{0,4},{4,0},{8,12},{12,8},{16,20},{20,16},{24,28},{28,24},{1,5},{5... | collective-permute-start | bytes 789512 | tf_op jit(solution)/shard_map/ppermute | solution.py:243
  8.4 0.7 %collective-permute-start.2 = (bf16[4,32896]{1,0:T(4,128)(2,1)S(1)}, bf16[4,32896]{1,0:T(4,128)(2,1)S(1)}, u32[]{:S(2)}, u32[]{:S(2)}) collective-permute-start(bf16[4,32896]{1,0:T(4,128)(2,1)S(1)} %get-tuple-element.16), channel_id=1, source_target_pairs={{4,8},{8,4},{12,16},{16,12},{20,24},{24,20},{5,9},{9,5},{13,17},{1... | collective-permute-start | bytes 789512 | tf_op jit(solution)/shard_map/ppermute | solution.py:244
  9.2 3.5 %shard_map.46 = (f32[256,8,128]{2,1,0:T(8,128)S(1)}, f32[32,16,128]{2,1,0:T(8,128)S(1)}) custom-call(bf16[16,32768]{1,0:T(8,128)(2,1)S(1)} %copy-done, bf16[16,128]{1,0:T(8,128)(2,1)S(1)} %collective-permute-done.history_ref, bf16[32,16]{1,0:T(8,128)(2,1)S(1)} %pad_maximum_fusion.3.mix_ref, bf16[256,256]{1,0:T(8,128)(2,1)S(1)} %pad_maximum_fusion.2.toeplitz_ref, ...), custom_call_target="tpu_custom_call" | custom-call | flops 1073741824 | bytes 4194304 | tf_op jit(solution)/shard_map/pallas_call | solution.py:255
  12.7 0.1 reduce-precision_convert_fusion.2
  12.8 7.2 %collective-permute-done.1.near_ref = bf16[4,32896]{1,0:T(4,128)(2,1)S(1)} collective-permute-done((bf16[4,32896]{1,0:T(4,128)(2,1)S(1)}, bf16[4,32896]{1,0:T(4,128)(2,1)S(1)}, u32[]{:S(2)}, u32[]{:S(2)}) %collective-permute-start.1) | collective-permute-done | bytes 263200 | tf_op jit(solution)/shard_map/ppermute | solution.py:243
  20.0 2.0 %shard_map.47 = bf16[4,4,16,128]{3,2,1,0:T(8,128)(2,1)S(1)} custom-call(bf16[4,32896]{1,0:T(4,128)(2,1)S(1)} %collective-permute-done.1.near_ref, bf16[4,32896]{1,0:T(4,128)(2,1)S(1)} %collective-permute-done.2.far_ref, f32[256,8,128]{2,1,0:T(8,128)S(1)} %get-tuple-element.19.edge_ref, f32[32,16,128]{2,1,0:T(8,128)S(1)} %get-tuple-element.20.own_ref, ...), custom_call_target="tpu_custom_call" | custom-call | flops 536870912 | bytes 2097152 | tf_op jit(solution)/shard_map/pallas_call | solution.py:266
  22.0 6.5 %all_to_all.5 = bf16[4,4,16,128]{3,2,1,0:T(8,128)(2,1)S(1)} all-to-all(bf16[4,4,16,128]{3,2,1,0:T(8,128)(2,1)S(1)} %shard_map.47), channel_id=1, replica_groups=mesh['chan'=8,'rep'=4] {'rep'}, dimensions={0} | all-to-all | bytes 131072 | tf_op jit(solution)/shard_map/all_to_all | solution.py:277
  28.5 3.6 %collective-permute-start.6 = (bf16[16,16,128]{2,1,0:T(8,128)(2,1)S(1)}, bf16[16,16,128]{2,1,0:T(8,128)(2,1)S(1)}, u32[]{:S(2)}, u32[]{:S(2)}) collective-permute-start(bf16[16,16,128]{2,1,0:T(8,128)(2,1)S(1)} %bitcast.1), channel_id=1, source_target_pairs={{16,0},{20,4},{24,8},{28,12},{0,16},{4,20},{8,24},{12,28},{17,1},{... | collective-permute-start | bytes 196616 | tf_op jit(solution)/shard_map/ppermute | solution.py:281
  32.1 1.3 %collective-permute-start.5 = (bf16[16,16,128]{2,1,0:T(8,128)(2,1)S(1)}, bf16[16,16,128]{2,1,0:T(8,128)(2,1)S(1)}, u32[]{:S(2)}, u32[]{:S(2)}) collective-permute-start(bf16[16,16,128]{2,1,0:T(8,128)(2,1)S(1)} %bitcast.2), channel_id=1, source_target_pairs={{12,0},{16,4},{20,8},{24,12},{28,16},{0,20},{4,24},{8,28},{13,1},{... | collective-permute-start | bytes 196616 | tf_op jit(solution)/shard_map/ppermute | solution.py:281
  33.3 1.5 %collective-permute-start.4 = (bf16[16,16,128]{2,1,0:T(8,128)(2,1)S(1)}, bf16[16,16,128]{2,1,0:T(8,128)(2,1)S(1)}, u32[]{:S(2)}, u32[]{:S(2)}) collective-permute-start(bf16[16,16,128]{2,1,0:T(8,128)(2,1)S(1)} %bitcast.3), channel_id=1, source_target_pairs={{8,0},{12,4},{16,8},{20,12},{24,16},{28,20},{0,24},{4,28},{9,1},{1... | collective-permute-start | bytes 196616 | tf_op jit(solution)/shard_map/ppermute | solution.py:281
  34.8 2.6 %collective-permute-start.3 = (bf16[16,16,128]{2,1,0:T(8,128)(2,1)S(1)}, bf16[16,16,128]{2,1,0:T(8,128)(2,1)S(1)}, u32[]{:S(2)}, u32[]{:S(2)}) collective-permute-start(bf16[16,16,128]{2,1,0:T(8,128)(2,1)S(1)} %bitcast.4), channel_id=1, source_target_pairs={{4,0},{8,4},{12,8},{16,12},{20,16},{24,20},{28,24},{0,28},{5,1},{9... | collective-permute-start | bytes 196616 | tf_op jit(solution)/shard_map/ppermute | solution.py:281
  37.5 0.3 shard_map.48.refs_0_
  37.8 1.3 %collective-permute-done.4.refs_3_ = bf16[16,16,128]{2,1,0:T(8,128)(2,1)S(1)} collective-permute-done((bf16[16,16,128]{2,1,0:T(8,128)(2,1)S(1)}, bf16[16,16,128]{2,1,0:T(8,128)(2,1)S(1)}, u32[]{:S(2)}, u32[]{:S(2)}) %collective-permute-start.4) | collective-permute-done | bytes 65568 | tf_op jit(solution)/shard_map/ppermute | solution.py:281
  39.2 0.2 collective-permute-done.3.refs_2_
  39.4 1.3 %shard_map.49 = f32[16,5,8,32]{3,2,1,0:T(8,128)} custom-call(bf16[2,128,2048]{2,1,0:T(8,128)(2,1)S(1)} %shard_map.48.refs_0_, bf16[16,16,128]{2,1,0:T(8,128)(2,1)S(1)} %bitcast.6, bf16[16,16,128]{2,1,0:T(8,128)(2,1)S(1)} %collective-permute-done.3.refs_2_, bf16[16,16,128]{2,1,0:T(8,128)(2,1)S(1)} %collective-permute-done.4.refs_3_, ...), custom_call_target="tpu_custom_call" | custom-call | flops 16777216 | bytes 1048576 | tf_op jit(solution)/shard_map/pallas_call | solution.py:290
  (21 shorter events, 0.1 us)
Async XLA Ops:
  0.7 4.0 %collective-permute-start = (bf16[16,128]{1,0:T(8,128)(2,1)S(1)}, bf16[16,128]{1,0:T(8,128)(2,1)S(1)}, u32[]{:S(2)}, u32[]{:S(2)}) collective-permute-start(bf16[16,128]{1,0:T(8,128)(2,1)S(1)} %slice.30), channel_id=1, source_target_pairs={{0,1},{1,2},{2,3},{4,5},{5,6},{6,7},{8,9},{9,10},{10,11},{12,13},{... | collective-permute-start | bytes 12296 | tf_op jit(solution)/shard_map/ppermute | solution.py:239
  3.1 1.8 %copy-start.3 = (f32[9]{0:T(128)S(1)}, f32[9]{0:T(128)}, u32[]{:S(2)}) copy-start(f32[9]{0:T(128)} %param.6) | copy-start | bytes 112
  3.1 2.0 %copy-start.2 = (f32[60]{0:T(128)S(1)}, f32[60]{0:T(128)}, u32[]{:S(2)}) copy-start(f32[60]{0:T(128)} %param.5) | copy-start | bytes 724
  4.6 4.5 %copy-start = (bf16[16,32768]{1,0:T(8,128)(2,1)S(1)}, bf16[16,32768]{1,0:T(8,128)(2,1)}, u32[]{:S(2)}) copy-start(bf16[16,32768]{1,0:T(8,128)(2,1)} %strain_ref.1) | copy-start | bytes 3145732
  4.6 4.5 %copy-start.1 = (bf16[1024,128]{1,0:T(8,128)(2,1)S(1)}, bf16[1024,128]{1,0:T(8,128)(2,1)}, u32[]{:S(2)}) copy-start(bf16[1024,128]{1,0:T(8,128)(2,1)} %constant.26.clone.dft_ref) | copy-start | bytes 786436
  6.1 13.9 %collective-permute-start.1 = (bf16[4,32896]{1,0:T(4,128)(2,1)S(1)}, bf16[4,32896]{1,0:T(4,128)(2,1)S(1)}, u32[]{:S(2)}, u32[]{:S(2)}) collective-permute-start(bf16[4,32896]{1,0:T(4,128)(2,1)S(1)} %get-tuple-element.15), channel_id=1, source_target_pairs={{0,4},{4,0},{8,12},{12,8},{16,20},{20,16},{24,28},{28,24},{1,5},{5... | collective-permute-start | bytes 789512 | tf_op jit(solution)/shard_map/ppermute | solution.py:243
  8.4 11.6 %collective-permute-start.2 = (bf16[4,32896]{1,0:T(4,128)(2,1)S(1)}, bf16[4,32896]{1,0:T(4,128)(2,1)S(1)}, u32[]{:S(2)}, u32[]{:S(2)}) collective-permute-start(bf16[4,32896]{1,0:T(4,128)(2,1)S(1)} %get-tuple-element.16), channel_id=1, source_target_pairs={{4,8},{8,4},{12,16},{16,12},{20,24},{24,20},{5,9},{9,5},{13,17},{1... | collective-permute-start | bytes 789512 | tf_op jit(solution)/shard_map/ppermute | solution.py:244
  28.5 9.3 %collective-permute-start.6 = (bf16[16,16,128]{2,1,0:T(8,128)(2,1)S(1)}, bf16[16,16,128]{2,1,0:T(8,128)(2,1)S(1)}, u32[]{:S(2)}, u32[]{:S(2)}) collective-permute-start(bf16[16,16,128]{2,1,0:T(8,128)(2,1)S(1)} %bitcast.1), channel_id=1, source_target_pairs={{16,0},{20,4},{24,8},{28,12},{0,16},{4,20},{8,24},{12,28},{17,1},{... | collective-permute-start | bytes 196616 | tf_op jit(solution)/shard_map/ppermute | solution.py:281
  32.1 5.8 %collective-permute-start.5 = (bf16[16,16,128]{2,1,0:T(8,128)(2,1)S(1)}, bf16[16,16,128]{2,1,0:T(8,128)(2,1)S(1)}, u32[]{:S(2)}, u32[]{:S(2)}) collective-permute-start(bf16[16,16,128]{2,1,0:T(8,128)(2,1)S(1)} %bitcast.2), channel_id=1, source_target_pairs={{12,0},{16,4},{20,8},{24,12},{28,16},{0,20},{4,24},{8,28},{13,1},{... | collective-permute-start | bytes 196616 | tf_op jit(solution)/shard_map/ppermute | solution.py:281
  33.3 5.8 %collective-permute-start.4 = (bf16[16,16,128]{2,1,0:T(8,128)(2,1)S(1)}, bf16[16,16,128]{2,1,0:T(8,128)(2,1)S(1)}, u32[]{:S(2)}, u32[]{:S(2)}) collective-permute-start(bf16[16,16,128]{2,1,0:T(8,128)(2,1)S(1)} %bitcast.3), channel_id=1, source_target_pairs={{8,0},{12,4},{16,8},{20,12},{24,16},{28,20},{0,24},{4,28},{9,1},{1... | collective-permute-start | bytes 196616 | tf_op jit(solution)/shard_map/ppermute | solution.py:281
  34.8 4.5 %collective-permute-start.3 = (bf16[16,16,128]{2,1,0:T(8,128)(2,1)S(1)}, bf16[16,16,128]{2,1,0:T(8,128)(2,1)S(1)}, u32[]{:S(2)}, u32[]{:S(2)}) collective-permute-start(bf16[16,16,128]{2,1,0:T(8,128)(2,1)S(1)} %bitcast.4), channel_id=1, source_target_pairs={{4,0},{8,4},{12,8},{16,12},{20,16},{24,20},{28,24},{0,28},{5,1},{9... | collective-permute-start | bytes 196616 | tf_op jit(solution)/shard_map/ppermute | solution.py:281

commit v4 on v3

--- a/solution.py
+++ b/solution.py
@@ -171,7 +171,10 @@
     width_group = 2 * GROUP
     across = LANES // width_group
     slot = lax.broadcasted_iota(jnp.int32, spectra.shape[1:], 1) // width_group
-    for group in range(out_ref.shape[0]):
+    groups = out_ref.shape[0]
+    here = lax.axis_index("rep")
+    for group in range(groups):
+        place = jnp.bitwise_xor(group, here) if groups & (groups - 1) == 0 else lax.rem(group - here + groups, groups)
         for outer in range(out_ref.shape[1]):
             tile = jnp.zeros(spectra.shape[1:], f32)
             for inner in range(across):
@@ -180,7 +183,7 @@
                 if shift:
                     value = pltpu.roll(value, shift, 1)
                 tile = jnp.where(slot == inner, value, tile)
-            out_ref[group, outer] = tile.astype(bf16)
+            out_ref[place, outer] = tile.astype(bf16)
 
 
 def left_kernel(own_ref, left_ref):
@@ -274,8 +277,11 @@
         flops=2 * 2 * rows * samples * 256,
         bytes_accessed=2 * 2**20,
     )(near, far, edge, own, edge_mix, filter_matrix, table)
-    gathered = lax.all_to_all(pieces, "rep", split_axis=0, concat_axis=0, tiled=True)
-    gathered = gathered.reshape(-1, rows, LANES)
+    arrived = [pieces[0]]
+    for step in range(1, rep):
+        to = [(i, i ^ step if rep & (rep - 1) == 0 else (i + step) % rep) for i in range(rep)]
+        arrived.append(lax.ppermute(pieces[step], "rep", to))
+    gathered = jnp.concatenate(arrived, axis=0)
     partners = [gathered]
     for step in range(1, STEPS + 1):
         partners.append(lax.ppermute(gathered, "chan", [((i + step) % chan, i) for i in range(chan)]))

time: 41 us -> 38.9 us (0.949)
  blocking collectives: 6.49 us -> 0 us
  starting transfers between devices: 14.3 us -> 16.8 us
  waiting for transfers between devices: 8.75 us -> 10.7 us
    all_to_all x1 -> x0, blocking collectives: 6.49 us -> none  [per_device(): lax.all_to_all(pieces, 'rep', split_axis=0, concat_axis=0, tiled=True)]
    ppermute x0 -> x3, starting transfers between devices: none -> 2.61 us  [per_device(): arrived.append(lax.ppermute(pieces[step], 'rep', to))]
    ppermute x0 -> x3, waiting for transfers between devices: none -> 1.89 us  [per_device(): arrived.append(lax.ppermute(pieces[step], 'rep', to))]
  transfers between devices with their start and end apart: 7 -> 10, of which waited for: 3 -> 5; matrix products, arithmetic and copies ran while one was open for 4% -> 4% of each run, Pallas kernels for 9% -> 10%
where the time goes in v4:
time: 38.9 us; the launch traced here: 38.7 us
  starting transfers between devices  16.8 us (43%)
  waiting for transfers between devices  10.7 us (28%)
  Pallas kernels  7.18 us (18%)
  other arithmetic  3.04 us (8%)
  local copies, waits for them, and re-layouts  0.73 us (2%)
    ppermute x4, starting transfers between devices, per_device(): lax.ppermute(gathered, 'chan', [((i + step) % chan, i) for i in range(cha...  8.89 us
    ppermute x1, waiting for transfers between devices, per_device(): near = lax.ppermute(within, 'chan', pairs_within)  7.2 us
    pallas_call x1, Pallas kernels, per_device(): call(own_kernel, (jax.ShapeDtypeStruct((blocks, 2 * HALO, LANES), f32), j...  3.53 us
    ppermute x3, starting transfers between devices, per_device(): arrived.append(lax.ppermute(pieces[step], 'rep', to))  2.61 us
    ppermute x1, starting transfers between devices, per_device(): lax.ppermute(strain[:, samples - LANES:], 'rep', [(i, i + 1) for i in ran...  2.34 us
    ppermute x1, starting transfers between devices, per_device(): near = lax.ppermute(within, 'chan', pairs_within)  2.33 us
    pallas_call x1, Pallas kernels, per_device(): call(edge_kernel, jax.ShapeDtypeStruct((rep, windows * 2 * GROUP // LANES...  2 us
    ppermute x3, waiting for transfers between devices, per_device(): arrived.append(lax.ppermute(pieces[step], 'rep', to))  1.89 us
  transfers between devices with their start and end apart: 10, of which 5 were waited for; matrix products, arithmetic and copies ran while one was open for 4% of the time, Pallas kernels for 10%

profile of v4, /device:TPU:0, one launch (start us, length us, event | category | flops | bytes accessed | tf_op | source)
XLA Modules:
  0.0 38.7 jit_solution(11441639719581443172)
XLA Ops:
  0.0 0.7 %slice.42 = bf16[16,128]{1,0:T(8,128)(2,1)S(1)} slice(bf16[16,32768]{1,0:T(8,128)(2,1)} %strain_ref.1), slice={[0:16], [32640:32768]} | slice | bytes 8192 | tf_op jit(solution)/shard_map/slice | solution.py:242
  0.7 2.3 %collective-permute-start = (bf16[16,128]{1,0:T(8,128)(2,1)S(1)}, bf16[16,128]{1,0:T(8,128)(2,1)S(1)}, u32[]{:S(2)}, u32[]{:S(2)}) collective-permute-start(bf16[16,128]{1,0:T(8,128)(2,1)S(1)} %slice.42), channel_id=1, source_target_pairs={{0,1},{1,2},{2,3},{4,5},{5,6},{6,7},{8,9},{9,10},{10,11},{12,13},{... | collective-permute-start | bytes 12296 | tf_op jit(solution)/shard_map/ppermute | solution.py:242
  3.1 1.5 %broadcast_select_fusion = (bf16[4,32768]{1,0:T(4,128)(2,1)S(1)}, bf16[4,32768]{1,0:T(4,128)(2,1)S(1)}) fusion(pred[]{:T(512)S(6)} %eq.16, bf16[16,32768]{1,0:T(8,128)(2,1)} %strain_ref.1), kind=kLoop, calls=%fused_computation.4 | loop fusion | flops 262144 | bytes 1048577 | tf_op jit(solution)/shard_map/jit(_where)/select_n | solution.py:240
  4.7 0.2 pad_maximum_fusion
  4.9 0.1 select_reduce_fusion.1
  5.0 0.1 reduce-precision_convert_fusion.1
  5.1 0.9 %select_reduce_fusion = f32[256,128]{1,0:T(8,128)S(1)} fusion(f32[60]{0:T(128)S(1)} %copy-done.2, s32[256,128]{1,0:T(8,128)S(1)} %iota_subtract_fusion), kind=kLoop, calls=%fused_computation | loop fusion | flops 5865472 | bytes 262384 | tf_op jit(solution)/shard_map/reduce_sum | solution.py:62
  6.1 2.3 %collective-permute-start.1 = (bf16[4,32896]{1,0:T(4,128)(2,1)S(1)}, bf16[4,32896]{1,0:T(4,128)(2,1)S(1)}, u32[]{:S(2)}, u32[]{:S(2)}) collective-permute-start(bf16[4,32896]{1,0:T(4,128)(2,1)S(1)} %get-tuple-element.15), channel_id=1, source_target_pairs={{0,4},{4,0},{8,12},{12,8},{16,20},{20,16},{24,28},{28,24},{1,5},{5... | collective-permute-start | bytes 789512 | tf_op jit(solution)/shard_map/ppermute | solution.py:246
  8.4 0.7 %collective-permute-start.2 = (bf16[4,32896]{1,0:T(4,128)(2,1)S(1)}, bf16[4,32896]{1,0:T(4,128)(2,1)S(1)}, u32[]{:S(2)}, u32[]{:S(2)}) collective-permute-start(bf16[4,32896]{1,0:T(4,128)(2,1)S(1)} %get-tuple-element.16), channel_id=1, source_target_pairs={{4,8},{8,4},{12,16},{16,12},{20,24},{24,20},{5,9},{9,5},{13,17},{1... | collective-permute-start | bytes 789512 | tf_op jit(solution)/shard_map/ppermute | solution.py:247
  9.2 3.5 %shard_map.46 = (f32[256,8,128]{2,1,0:T(8,128)S(1)}, f32[32,16,128]{2,1,0:T(8,128)S(1)}) custom-call(bf16[16,32768]{1,0:T(8,128)(2,1)S(1)} %copy-done, bf16[16,128]{1,0:T(8,128)(2,1)S(1)} %collective-permute-done.history_ref, bf16[32,16]{1,0:T(8,128)(2,1)S(1)} %pad_maximum_fusion.4.mix_ref, bf16[256,256]{1,0:T(8,128)(2,1)S(1)} %pad_maximum_fusion.2.toeplitz_ref, ...), custom_call_target="tpu_custom_call" | custom-call | flops 1073741824 | bytes 4194304 | tf_op jit(solution)/shard_map/pallas_call | solution.py:258
  12.7 0.1 reduce-precision_convert_fusion.2
  12.8 7.2 %collective-permute-done.1.near_ref = bf16[4,32896]{1,0:T(4,128)(2,1)S(1)} collective-permute-done((bf16[4,32896]{1,0:T(4,128)(2,1)S(1)}, bf16[4,32896]{1,0:T(4,128)(2,1)S(1)}, u32[]{:S(2)}, u32[]{:S(2)}) %collective-permute-start.1) | collective-permute-done | bytes 263200 | tf_op jit(solution)/shard_map/ppermute | solution.py:246
  20.0 2.0 %shard_map.47 = bf16[4,4,16,128]{3,2,1,0:T(8,128)(2,1)S(1)} custom-call(bf16[4,32896]{1,0:T(4,128)(2,1)S(1)} %collective-permute-done.1.near_ref, bf16[4,32896]{1,0:T(4,128)(2,1)S(1)} %collective-permute-done.2.far_ref, f32[256,8,128]{2,1,0:T(8,128)S(1)} %get-tuple-element.19.edge_ref, f32[32,16,128]{2,1,0:T(8,128)S(1)} %get-tuple-element.20.own_ref, ...), custom_call_target="tpu_custom_call" | custom-call | flops 536870912 | bytes 2097152 | tf_op jit(solution)/shard_map/pallas_call | solution.py:269
  22.1 2.5 %collective-permute-start.4 = (bf16[4,16,128]{2,1,0:T(8,128)(2,1)S(1)}, bf16[4,16,128]{2,1,0:T(8,128)(2,1)S(1)}, u32[]{:S(2)}, u32[]{:S(2)}) collective-permute-start(bf16[4,16,128]{2,1,0:T(8,128)(2,1)S(1)} %get-tuple-element.27), channel_id=1, source_target_pairs={{0,2},{1,3},{2,0},{3,1},{4,6},{5,7},{6,4},{7,5},{8,10},{9,11},{10,... | collective-permute-start | bytes 49160 | tf_op jit(solution)/shard_map/ppermute | solution.py:283
  24.6 0.6 %collective-permute-done.5 = bf16[4,16,128]{2,1,0:T(8,128)(2,1)S(1)} collective-permute-done((bf16[4,16,128]{2,1,0:T(8,128)(2,1)S(1)}, bf16[4,16,128]{2,1,0:T(8,128)(2,1)S(1)}, u32[]{:S(2)}, u32[]{:S(2)}) %collective-permute-start.5) | collective-permute-done | bytes 16416 | tf_op jit(solution)/shard_map/ppermute | solution.py:283
  25.3 1.3 %collective-permute-done.4 = bf16[4,16,128]{2,1,0:T(8,128)(2,1)S(1)} collective-permute-done((bf16[4,16,128]{2,1,0:T(8,128)(2,1)S(1)}, bf16[4,16,128]{2,1,0:T(8,128)(2,1)S(1)}, u32[]{:S(2)}, u32[]{:S(2)}) %collective-permute-start.4) | collective-permute-done | bytes 16416 | tf_op jit(solution)/shard_map/ppermute | solution.py:283
  26.5 3.5 %collective-permute-start.9 = (bf16[16,16,128]{2,1,0:T(8,128)(2,1)S(1)}, bf16[16,16,128]{2,1,0:T(8,128)(2,1)S(1)}, u32[]{:S(2)}, u32[]{:S(2)}) collective-permute-start(bf16[16,16,128]{2,1,0:T(8,128)(2,1)S(1)} %pad_maximum_fusion.3.own_ref.refs_1_), channel_id=1, source_target_pairs={{16,0},{20,4},{24,8},{28,12},{0,16},{4,20},{8,24},{12,28},{17,1},{... | collective-permute-start | bytes 196616 | tf_op jit(solution)/shard_map/ppermute | solution.py:287
  30.0 1.3 %collective-permute-start.8 = (bf16[16,16,128]{2,1,0:T(8,128)(2,1)S(1)}, bf16[16,16,128]{2,1,0:T(8,128)(2,1)S(1)}, u32[]{:S(2)}, u32[]{:S(2)}) collective-permute-start(bf16[16,16,128]{2,1,0:T(8,128)(2,1)S(1)} %pad_maximum_fusion.3.own_ref.refs_1_), channel_id=1, source_target_pairs={{12,0},{16,4},{20,8},{24,12},{28,16},{0,20},{4,24},{8,28},{13,1},{... | collective-permute-start | bytes 196616 | tf_op jit(solution)/shard_map/ppermute | solution.py:287
  31.3 1.8 %collective-permute-start.7 = (bf16[16,16,128]{2,1,0:T(8,128)(2,1)S(1)}, bf16[16,16,128]{2,1,0:T(8,128)(2,1)S(1)}, u32[]{:S(2)}, u32[]{:S(2)}) collective-permute-start(bf16[16,16,128]{2,1,0:T(8,128)(2,1)S(1)} %pad_maximum_fusion.3.own_ref.refs_1_), channel_id=1, source_target_pairs={{8,0},{12,4},{16,8},{20,12},{24,16},{28,20},{0,24},{4,28},{9,1},{1... | collective-permute-start | bytes 196616 | tf_op jit(solution)/shard_map/ppermute | solution.py:287
  33.1 2.3 %collective-permute-start.6 = (bf16[16,16,128]{2,1,0:T(8,128)(2,1)S(1)}, bf16[16,16,128]{2,1,0:T(8,128)(2,1)S(1)}, u32[]{:S(2)}, u32[]{:S(2)}) collective-permute-start(bf16[16,16,128]{2,1,0:T(8,128)(2,1)S(1)} %pad_maximum_fusion.3.own_ref.refs_1_), channel_id=1, source_target_pairs={{4,0},{8,4},{12,8},{16,12},{20,16},{24,20},{28,24},{0,28},{5,1},{9... | collective-permute-start | bytes 196616 | tf_op jit(solution)/shard_map/ppermute | solution.py:287
  35.4 0.3 shard_map.48.refs_0_
  35.8 1.0 %collective-permute-done.7.refs_3_ = bf16[16,16,128]{2,1,0:T(8,128)(2,1)S(1)} collective-permute-done((bf16[16,16,128]{2,1,0:T(8,128)(2,1)S(1)}, bf16[16,16,128]{2,1,0:T(8,128)(2,1)S(1)}, u32[]{:S(2)}, u32[]{:S(2)}) %collective-permute-start.7) | collective-permute-done | bytes 65568 | tf_op jit(solution)/shard_map/ppermute | solution.py:287
  36.8 0.6 %collective-permute-done.6.refs_2_ = bf16[16,16,128]{2,1,0:T(8,128)(2,1)S(1)} collective-permute-done((bf16[16,16,128]{2,1,0:T(8,128)(2,1)S(1)}, bf16[16,16,128]{2,1,0:T(8,128)(2,1)S(1)}, u32[]{:S(2)}, u32[]{:S(2)}) %collective-permute-start.6) | collective-permute-done | bytes 65568 | tf_op jit(solution)/shard_map/ppermute | solution.py:287
  37.4 1.3 %shard_map.49 = f32[16,5,8,32]{3,2,1,0:T(8,128)} custom-call(bf16[2,128,2048]{2,1,0:T(8,128)(2,1)S(1)} %shard_map.48.refs_0_, bf16[16,16,128]{2,1,0:T(8,128)(2,1)S(1)} %pad_maximum_fusion.3.own_ref.refs_1_, bf16[16,16,128]{2,1,0:T(8,128)(2,1)S(1)} %collective-permute-done.6.refs_2_, bf16[16,16,128]{2,1,0:T(8,128)(2,1)S(1)} %collective-permute-done.7.refs_3_, ...), custom_call_target="tpu_custom_call" | custom-call | flops 16777216 | bytes 1048576 | tf_op jit(solution)/shard_map/pallas_call | solution.py:296
  (28 shorter events, 0.3 us)
Async XLA Ops:
  0.7 4.0 %collective-permute-start = (bf16[16,128]{1,0:T(8,128)(2,1)S(1)}, bf16[16,128]{1,0:T(8,128)(2,1)S(1)}, u32[]{:S(2)}, u32[]{:S(2)}) collective-permute-start(bf16[16,128]{1,0:T(8,128)(2,1)S(1)} %slice.42), channel_id=1, source_target_pairs={{0,1},{1,2},{2,3},{4,5},{5,6},{6,7},{8,9},{9,10},{10,11},{12,13},{... | collective-permute-start | bytes 12296 | tf_op jit(solution)/shard_map/ppermute | solution.py:242
  3.1 1.8 %copy-start.3 = (f32[9]{0:T(128)S(1)}, f32[9]{0:T(128)}, u32[]{:S(2)}) copy-start(f32[9]{0:T(128)} %param.6) | copy-start | bytes 112
  3.1 2.0 %copy-start.2 = (f32[60]{0:T(128)S(1)}, f32[60]{0:T(128)}, u32[]{:S(2)}) copy-start(f32[60]{0:T(128)} %param.5) | copy-start | bytes 724
  4.6 4.5 %copy-start = (bf16[16,32768]{1,0:T(8,128)(2,1)S(1)}, bf16[16,32768]{1,0:T(8,128)(2,1)}, u32[]{:S(2)}) copy-start(bf16[16,32768]{1,0:T(8,128)(2,1)} %strain_ref.1) | copy-start | bytes 3145732
  4.6 4.5 %copy-start.1 = (bf16[1024,128]{1,0:T(8,128)(2,1)S(1)}, bf16[1024,128]{1,0:T(8,128)(2,1)}, u32[]{:S(2)}) copy-start(bf16[1024,128]{1,0:T(8,128)(2,1)} %constant.26.clone.dft_ref) | copy-start | bytes 786436
  6.1 13.9 %collective-permute-start.1 = (bf16[4,32896]{1,0:T(4,128)(2,1)S(1)}, bf16[4,32896]{1,0:T(4,128)(2,1)S(1)}, u32[]{:S(2)}, u32[]{:S(2)}) collective-permute-start(bf16[4,32896]{1,0:T(4,128)(2,1)S(1)} %get-tuple-element.15), channel_id=1, source_target_pairs={{0,4},{4,0},{8,12},{12,8},{16,20},{20,16},{24,28},{28,24},{1,5},{5... | collective-permute-start | bytes 789512 | tf_op jit(solution)/shard_map/ppermute | solution.py:246
  8.4 11.6 %collective-permute-start.2 = (bf16[4,32896]{1,0:T(4,128)(2,1)S(1)}, bf16[4,32896]{1,0:T(4,128)(2,1)S(1)}, u32[]{:S(2)}, u32[]{:S(2)}) collective-permute-start(bf16[4,32896]{1,0:T(4,128)(2,1)S(1)} %get-tuple-element.16), channel_id=1, source_target_pairs={{4,8},{8,4},{12,16},{16,12},{20,24},{24,20},{5,9},{9,5},{13,17},{1... | collective-permute-start | bytes 789512 | tf_op jit(solution)/shard_map/ppermute | solution.py:247
  22.0 3.2 %collective-permute-start.5 = (bf16[4,16,128]{2,1,0:T(8,128)(2,1)S(1)}, bf16[4,16,128]{2,1,0:T(8,128)(2,1)S(1)}, u32[]{:S(2)}, u32[]{:S(2)}) collective-permute-start(bf16[4,16,128]{2,1,0:T(8,128)(2,1)S(1)} %get-tuple-element.26), channel_id=1, source_target_pairs={{0,3},{1,2},{2,1},{3,0},{4,7},{5,6},{6,5},{7,4},{8,11},{9,10},{10,... | collective-permute-start | bytes 49160 | tf_op jit(solution)/shard_map/ppermute | solution.py:283
  22.1 4.4 %collective-permute-start.4 = (bf16[4,16,128]{2,1,0:T(8,128)(2,1)S(1)}, bf16[4,16,128]{2,1,0:T(8,128)(2,1)S(1)}, u32[]{:S(2)}, u32[]{:S(2)}) collective-permute-start(bf16[4,16,128]{2,1,0:T(8,128)(2,1)S(1)} %get-tuple-element.27), channel_id=1, source_target_pairs={{0,2},{1,3},{2,0},{3,1},{4,6},{5,7},{6,4},{7,5},{8,10},{9,11},{10,... | collective-permute-start | bytes 49160 | tf_op jit(solution)/shard_map/ppermute | solution.py:283
  24.6 1.9 %collective-permute-start.3 = (bf16[4,16,128]{2,1,0:T(8,128)(2,1)S(1)}, bf16[4,16,128]{2,1,0:T(8,128)(2,1)S(1)}, u32[]{:S(2)}, u32[]{:S(2)}) collective-permute-start(bf16[4,16,128]{2,1,0:T(8,128)(2,1)S(1)} %get-tuple-element.28), channel_id=1, source_target_pairs={{0,1},{1,0},{2,3},{3,2},{4,5},{5,4},{6,7},{7,6},{8,9},{9,8},{10,11... | collective-permute-start | bytes 49160 | tf_op jit(solution)/shard_map/ppermute | solution.py:283
  26.5 9.2 %collective-permute-start.9 = (bf16[16,16,128]{2,1,0:T(8,128)(2,1)S(1)}, bf16[16,16,128]{2,1,0:T(8,128)(2,1)S(1)}, u32[]{:S(2)}, u32[]{:S(2)}) collective-permute-start(bf16[16,16,128]{2,1,0:T(8,128)(2,1)S(1)} %pad_maximum_fusion.3.own_ref.refs_1_), channel_id=1, source_target_pairs={{16,0},{20,4},{24,8},{28,12},{0,16},{4,20},{8,24},{12,28},{17,1},{... | collective-permute-start | bytes 196616 | tf_op jit(solution)/shard_map/ppermute | solution.py:287
  30.0 5.8 %collective-permute-start.8 = (bf16[16,16,128]{2,1,0:T(8,128)(2,1)S(1)}, bf16[16,16,128]{2,1,0:T(8,128)(2,1)S(1)}, u32[]{:S(2)}, u32[]{:S(2)}) collective-permute-start(bf16[16,16,128]{2,1,0:T(8,128)(2,1)S(1)} %pad_maximum_fusion.3.own_ref.refs_1_), channel_id=1, source_target_pairs={{12,0},{16,4},{20,8},{24,12},{28,16},{0,20},{4,24},{8,28},{13,1},{... | collective-permute-start | bytes 196616 | tf_op jit(solution)/shard_map/ppermute | solution.py:287
  31.3 5.5 %collective-permute-start.7 = (bf16[16,16,128]{2,1,0:T(8,128)(2,1)S(1)}, bf16[16,16,128]{2,1,0:T(8,128)(2,1)S(1)}, u32[]{:S(2)}, u32[]{:S(2)}) collective-permute-start(bf16[16,16,128]{2,1,0:T(8,128)(2,1)S(1)} %pad_maximum_fusion.3.own_ref.refs_1_), channel_id=1, source_target_pairs={{8,0},{12,4},{16,8},{20,12},{24,16},{28,20},{0,24},{4,28},{9,1},{1... | collective-permute-start | bytes 196616 | tf_op jit(solution)/shard_map/ppermute | solution.py:287
  33.1 4.3 %collective-permute-start.6 = (bf16[16,16,128]{2,1,0:T(8,128)(2,1)S(1)}, bf16[16,16,128]{2,1,0:T(8,128)(2,1)S(1)}, u32[]{:S(2)}, u32[]{:S(2)}) collective-permute-start(bf16[16,16,128]{2,1,0:T(8,128)(2,1)S(1)} %pad_maximum_fusion.3.own_ref.refs_1_), channel_id=1, source_target_pairs={{4,0},{8,4},{12,8},{16,12},{20,16},{24,20},{28,24},{0,28},{5,1},{9... | collective-permute-start | bytes 196616 | tf_op jit(solution)/shard_map/ppermute | solution.py:287

commit v5 on v4

--- a/solution.py
+++ b/solution.py
@@ -49,24 +49,32 @@
     return np.concatenate([high, low], axis=1)
 
 
-def rounded_halves(values):
-    high = lax.reduce_precision(values, exponent_bits=8, mantissa_bits=7)
-    return high.astype(bf16), (values - high).astype(bf16)
-
-
-def toeplitz(fir_taps):
-    source = jnp.arange(2 * LANES, dtype=jnp.int32)[:, None]
-    target = jnp.arange(LANES, dtype=jnp.int32)[None, :]
-    lag = (target + LANES - source)[:, :, None]
-    slots = jnp.arange(fir_taps.shape[0], dtype=jnp.int32)
-    taps = jnp.sum(jnp.where(lag == slots, fir_taps, 0.0), axis=2)
-    return jnp.concatenate(rounded_halves(taps), axis=1)
-
-
-def mixing(spatial, rows):
-    span = spatial.shape[0]
-    offset = (jnp.arange(rows + span - 1, dtype=jnp.int32)[None, :] - jnp.arange(rows, dtype=jnp.int32)[:, None])[:, :, None]
-    return jnp.sum(jnp.where(offset == jnp.arange(span, dtype=jnp.int32), spatial, 0.0), axis=2)
+def toeplitz(taps_ref):
+    lane = lax.broadcasted_iota(jnp.int32, (LANES, LANES), 1)
+    row = lax.broadcasted_iota(jnp.int32, (LANES, LANES), 0)
+    taps = jnp.zeros((1, LANES), f32)
+    for k in range(taps_ref.shape[0]):
+        taps = jnp.where(lane[:1] == k, taps_ref[k], taps)
+    turned = pltpu.roll(jnp.broadcast_to(taps, (LANES, LANES)), 0, 1, stride=1, stride_axis=0)
+    parts = [jnp.where(lane < row, turned, 0.0), jnp.where(lane >= row, turned, 0.0)]
+    return jnp.concatenate(halves(jnp.concatenate(parts, axis=0)), axis=1)
+
+
+def mixing(spatial_ref, lag):
+    weight = jnp.zeros(lag.shape, f32)
+    for j in range(spatial_ref.shape[0]):
+        weight = jnp.where(lag == j, spatial_ref[j], weight)
+    high = weight.astype(bf16).astype(f32)
+    return jnp.concatenate([high, weight - high], axis=0).astype(bf16)
+
+
+def edge_lags(count):
+    shape = (2 * HALO, 2 * HALO)
+    target = lax.broadcasted_iota(jnp.int32, shape, 0)
+    target = jnp.where(target < HALO, target, target + count - 2 * HALO)
+    source = lax.broadcasted_iota(jnp.int32, shape, 1)
+    before = (source < HALO) == (lax.axis_index("chan") % 2 != 0)
+    return source % HALO + jnp.where(before, 0, count + HALO) - target
 
 
 def filtered(mixed_ref, first, count, rows, toeplitz_ref):
@@ -106,11 +114,28 @@
     return (out[:, 0] + out[:, 1]) * scale_ref[...]
 
 
-def own_kernel(strain_ref, history_ref, mix_ref, toeplitz_ref, dft_ref, edge_ref, spectra_ref, mixed_ref, split_ref, scale_ref):
+def own_kernel(
+    strain_ref,
+    history_ref,
+    taps_ref,
+    spatial_ref,
+    dft_ref,
+    edge_ref,
+    spectra_ref,
+    toeplitz_ref,
+    edge_mix_ref,
+    mixed_ref,
+    split_ref,
+    scale_ref,
+):
     rows, samples = strain_ref.shape
+    source = lax.broadcasted_iota(jnp.int32, (rows, rows), 1)
+    weights = mixing(spatial_ref, source + HALO - lax.broadcasted_iota(jnp.int32, (rows, rows), 0))
+    toeplitz_ref[...] = toeplitz(taps_ref)
+    edge_mix_ref[...] = mixing(spatial_ref, edge_lags(rows))
 
     def mix(columns):
-        out = dot(mix_ref[...], columns)
+        out = dot(weights, columns)
         high, low = halves(out[:rows] + out[rows:])
         return jnp.concatenate([high, low], axis=0)
 
@@ -151,10 +176,11 @@
 ):
     rows = 2 * HALO
     step = near_ref.shape[1] - LANES
+    weights = mix_ref[...]
 
     def mix(near, far):
         both = jnp.concatenate([near.astype(f32), far.astype(f32)], axis=0).astype(bf16)
-        out = dot(mix_ref[...], both)
+        out = dot(weights, both)
         out = out[:rows] + out[rows:]
         high = out.astype(bf16).astype(f32)
         return jnp.concatenate([high, out - high], axis=0).astype(bf16)
@@ -186,6 +212,25 @@
             out_ref[place, outer] = tile.astype(bf16)
 
 
+def rim_kernel(strain_ref, within_ref, across_ref, last_ref):
+    rows, samples = strain_ref.shape
+    even = lax.axis_index("chan") % 2 == 0
+    head, tail = strain_ref[:HALO], strain_ref[rows - HALO :]
+    within_ref[...] = jnp.where(even, tail, head)
+    across_ref[...] = jnp.where(even, head, tail)
+    last_ref[...] = strain_ref[:, samples - LANES :]
+
+
+def prefix_kernel(history_ref, within_ref, across_ref, near_ref, far_ref):
+    rows = history_ref.shape[0]
+    even = lax.axis_index("chan") % 2 == 0
+    head, tail = history_ref[:HALO], history_ref[rows - HALO :]
+    near_ref[:, :LANES] = jnp.where(even, tail, head)
+    near_ref[:, LANES:] = within_ref[...]
+    far_ref[:, :LANES] = jnp.where(even, head, tail)
+    far_ref[:, LANES:] = across_ref[...]
+
+
 def left_kernel(own_ref, left_ref):
     parts, rows, _ = own_ref.shape
     lane = lax.broadcasted_iota(jnp.int32, (GROUP, LANES), 1)
@@ -215,10 +260,12 @@
             out_ref[c, s] = jnp.concatenate([a, b], axis=1)
 
 
-def call(kernel, out_shape, scratch=(), flops=0, bytes_accessed=0):
+def call(kernel, out_shape, scratch=(), flops=0, bytes_accessed=0, places="v"):
+    whole = {"v": pl.BlockSpec(memory_space=pltpu.VMEM), "s": pl.BlockSpec(memory_space=pltpu.SMEM)}
     return pl.pallas_call(
         kernel,
         out_shape=out_shape,
+        in_specs=[whole[place] for place in places],
         scratch_shapes=list(scratch),
         compiler_params=pltpu.CompilerParams(vmem_limit_bytes=32 * 2**20),
         cost_estimate=pl.CostEstimate(flops=flops, bytes_accessed=bytes_accessed, transcendentals=0),
@@ -235,29 +282,24 @@
     pairs_within = [(i, i ^ 1) for i in range(chan) if i ^ 1 < chan]
     pairs_across = [(i, j) for i in range(chan) for j in (i + 1 if i % 2 else i - 1,) if 0 <= j < chan]
 
-    def rims(block):
-        head, tail = block[:HALO], block[rows - HALO :]
-        return jnp.where(even, tail, head), jnp.where(even, head, tail)
-
-    history = lax.ppermute(strain[:, samples - LANES :], "rep", [(i, i + 1) for i in range(rep - 1)])
-    now = lax.optimization_barrier(rims(strain))
-    within, across = (jnp.concatenate(pair, axis=1) for pair in zip(rims(history), now))
-    within, across, fir_taps, spatial = lax.optimization_barrier((within, across, fir_taps, spatial))
+    rim = jax.ShapeDtypeStruct((HALO, samples), bf16)
+    last = jax.ShapeDtypeStruct((rows, LANES), bf16)
+    within, across, last = call(rim_kernel, [rim, rim, last], bytes_accessed=2**20)(strain)
+    history = lax.ppermute(last, "rep", [(i, i + 1) for i in range(rep - 1)])
+    rim = jax.ShapeDtypeStruct((HALO, LANES + samples), bf16)
+    within, across = call(prefix_kernel, [rim, rim], bytes_accessed=2**20, places="vvv")(history, within, across)
     near = lax.ppermute(within, "chan", pairs_within)
     far = lax.ppermute(across, "chan", pairs_across)
 
-    filter_matrix = toeplitz(fir_taps)
     table = jnp.asarray(dft_table())
-    mix = mixing(spatial, rows)
-    own_mix = jnp.concatenate(rounded_halves(mix[:, HALO : HALO + rows]), axis=0)
-    edge_rows = jnp.concatenate([mix[:HALO], mix[rows - HALO :]], axis=0)
-    before_mix, after_mix = edge_rows[:, :HALO], edge_rows[:, HALO + rows :]
-    edge_mix = jnp.concatenate([jnp.where(even, after_mix, before_mix), jnp.where(even, before_mix, after_mix)], axis=1)
-    edge_mix = jnp.concatenate(rounded_halves(edge_mix), axis=0)
-
-    edge, own = call(
+    edge, own, filter_matrix, edge_mix = call(
         own_kernel,
-        (jax.ShapeDtypeStruct((blocks, 2 * HALO, LANES), f32), jax.ShapeDtypeStruct((windows, rows, LANES), f32)),
+        [
+            jax.ShapeDtypeStruct((blocks, 2 * HALO, LANES), f32),
+            jax.ShapeDtypeStruct((windows, rows, LANES), f32),
+            jax.ShapeDtypeStruct((2 * LANES, 2 * LANES), bf16),
+            jax.ShapeDtypeStruct((4 * HALO, 2 * HALO), bf16),
+        ],
         [
             pltpu.VMEM((2 * rows, LANES + samples), bf16),
             pltpu.VMEM((windows, 2 * rows, NFFT), bf16),
@@ -265,7 +307,8 @@
         ],
         flops=2 * 2 * rows * samples * 512,
         bytes_accessed=4 * 2**20,
-    )(strain, history, own_mix, filter_matrix, table)
+        places="vvssv",
+    )(strain, history, fir_taps, spatial, table)
     pieces = call(
         edge_kernel,
         jax.ShapeDtypeStruct((rep, windows * 2 * GROUP // LANES, rows, LANES), bf16),
@@ -276,6 +319,7 @@
         ],
         flops=2 * 2 * rows * samples * 256,
         bytes_accessed=2 * 2**20,
+        places="v" * 7,
     )(near, far, edge, own, edge_mix, filter_matrix, table)
     arrived = [pieces[0]]
     for step in range(1, rep):
@@ -298,6 +342,7 @@
         jax.ShapeDtypeStruct((rows, STEPS + 1, BINS // rep, 2 * rows), f32),
         flops=2**24,
         bytes_accessed=2**20,
+        places="v" * (STEPS + 2),
     )(left, *partners)
 
 

time: 38.9 us -> 38.5 us (0.990)
  the two profiles are of different devices: /device:TPU:0 before, /device:TPU:27 now
where the time goes in v5:
time: 38.5 us; the launch traced here: 38.3 us
  waiting for transfers between devices  16.3 us (42%)
  starting transfers between devices  12.8 us (33%)
  Pallas kernels  7.9 us (21%)
  local copies, waits for them, and re-layouts  1.25 us (3%)
    ppermute x4, waiting for transfers between devices, per_device(): lax.ppermute(gathered, 'chan', [((i + step) % chan, i) for i in range(cha...  7.78 us
    ppermute x1, waiting for transfers between devices, per_device(): near = lax.ppermute(within, 'chan', pairs_within)  6.24 us
    ppermute x4, starting transfers between devices, per_device(): lax.ppermute(gathered, 'chan', [((i + step) % chan, i) for i in range(cha...  5.73 us
    pallas_call x1, Pallas kernels, per_device(): call(own_kernel, [jax.ShapeDtypeStruct((blocks, 2 * HALO, LANES), f32), j...  4.07 us
    ppermute x1, starting transfers between devices, per_device(): history = lax.ppermute(last, 'rep', [(i, i + 1) for i in range(rep - 1)])  3.84 us
    ppermute x3, starting transfers between devices, per_device(): arrived.append(lax.ppermute(pieces[step], 'rep', to))  2.21 us
    pallas_call x1, Pallas kernels, per_device(): call(edge_kernel, jax.ShapeDtypeStruct((rep, windows * 2 * GROUP // LANES...  1.99 us
    ppermute x3, waiting for transfers between devices, per_device(): arrived.append(lax.ppermute(pieces[step], 'rep', to))  1.52 us
  transfers between devices with their start and end apart: 10, of which 5 were waited for; matrix products, arithmetic and copies ran while one was open for 0% of the time, Pallas kernels for 12%

profile of v5, /device:TPU:27, one launch (start us, length us, event | category | flops | bytes accessed | tf_op | source)
XLA Modules:
  0.0 38.3 jit_solution(7530957090437305422)
XLA Ops:
  0.0 1.2 %copy-done = bf16[16,32768]{1,0:T(8,128)(2,1)S(1)} copy-done((bf16[16,32768]{1,0:T(8,128)(2,1)S(1)}, bf16[16,32768]{1,0:T(8,128)(2,1)}, u32[]{:S(2)}) %copy-start) | copy-done | bytes 1048600
  1.2 0.1 shard_map.46
  1.4 3.8 %collective-permute-start = (bf16[16,128]{1,0:T(8,128)(2,1)S(1)}, bf16[16,128]{1,0:T(8,128)(2,1)S(1)}, u32[]{:S(2)}, u32[]{:S(2)}) collective-permute-start(bf16[16,128]{1,0:T(8,128)(2,1)S(1)} %get-tuple-element.14), channel_id=1, source_target_pairs={{0,1},{1,2},{2,3},{4,5},{5,6},{6,7},{8,9},{9,10},{10,11},{12,13},{... | collective-permute-start | bytes 12296 | tf_op jit(solution)/shard_map/ppermute | solution.py:288
  5.2 0.7 %collective-permute-done.history_ref = bf16[16,128]{1,0:T(8,128)(2,1)S(1)} collective-permute-done((bf16[16,128]{1,0:T(8,128)(2,1)S(1)}, bf16[16,128]{1,0:T(8,128)(2,1)S(1)}, u32[]{:S(2)}, u32[]{:S(2)}) %collective-permute-start) | collective-permute-done | bytes 4128 | tf_op jit(solution)/shard_map/ppermute | solution.py:288
  6.0 0.0 copy-start.3
  6.0 0.0 copy-start.4
  6.0 0.3 collective-permute-start.1
  6.3 0.7 %collective-permute-start.2 = (bf16[4,32896]{1,0:T(4,128)(2,1)S(1)}, bf16[4,32896]{1,0:T(4,128)(2,1)S(1)}, u32[]{:S(2)}, u32[]{:S(2)}) collective-permute-start(bf16[4,32896]{1,0:T(4,128)(2,1)S(1)} %get-tuple-element.18), channel_id=1, source_target_pairs={{4,8},{8,4},{12,16},{16,12},{20,24},{24,20},{5,9},{9,5},{13,17},{1... | collective-permute-start | bytes 789512 | tf_op jit(solution)/shard_map/ppermute | solution.py:292
  7.1 4.1 %shard_map.48 = (f32[256,8,128]{2,1,0:T(8,128)S(1)}, f32[32,16,128]{2,1,0:T(8,128)S(1)}, bf16[256,256]{1,0:T(8,128)(2,1)S(1)}, bf16[16,8]{1,0:T(8,128)(2,1)S(1)}) custom-call(bf16[16,32768]{1,0:T(8,128)(2,1)S(1)} %copy-done.1, bf16[16,128]{1,0:T(8,128)(2,1)S(1)} %collective-permute-done.history_ref, f32[60]{0:T(128)S(1)} %copy-done.3, f32[9]{0:T(128)S(1)} %copy-done.4, ...), custom_call_target="tpu_custom_call" | custom-call | flops 1073741824 | bytes 4194304 | tf_op jit(solution)/shard_map/pallas_call | solution.py:295
  11.1 6.2 %collective-permute-done.1.near_ref = bf16[4,32896]{1,0:T(4,128)(2,1)S(1)} collective-permute-done((bf16[4,32896]{1,0:T(4,128)(2,1)S(1)}, bf16[4,32896]{1,0:T(4,128)(2,1)S(1)}, u32[]{:S(2)}, u32[]{:S(2)}) %collective-permute-start.1) | collective-permute-done | bytes 263200 | tf_op jit(solution)/shard_map/ppermute | solution.py:291
  17.4 0.0 collective-permute-done.2.far_ref
  17.4 2.0 %shard_map.49 = bf16[4,4,16,128]{3,2,1,0:T(8,128)(2,1)S(1)} custom-call(bf16[4,32896]{1,0:T(4,128)(2,1)S(1)} %collective-permute-done.1.near_ref, bf16[4,32896]{1,0:T(4,128)(2,1)S(1)} %collective-permute-done.2.far_ref, f32[256,8,128]{2,1,0:T(8,128)S(1)} %get-tuple-element.19.edge_ref, f32[32,16,128]{2,1,0:T(8,128)S(1)} %get-tuple-element.20.own_ref, ...), custom_call_target="tpu_custom_call" | custom-call | flops 536870912 | bytes 2097152 | tf_op jit(solution)/shard_map/pallas_call | solution.py:312
  19.4 1.1 %collective-permute-start.5 = (bf16[4,16,128]{2,1,0:T(8,128)(2,1)S(1)}, bf16[4,16,128]{2,1,0:T(8,128)(2,1)S(1)}, u32[]{:S(2)}, u32[]{:S(2)}) collective-permute-start(bf16[4,16,128]{2,1,0:T(8,128)(2,1)S(1)} %get-tuple-element.24), channel_id=1, source_target_pairs={{0,3},{1,2},{2,1},{3,0},{4,7},{5,6},{6,5},{7,4},{8,11},{9,10},{10,... | collective-permute-start | bytes 49160 | tf_op jit(solution)/shard_map/ppermute | solution.py:327
  20.5 0.0 collective-permute-start.4
  20.5 1.1 %collective-permute-start.3 = (bf16[4,16,128]{2,1,0:T(8,128)(2,1)S(1)}, bf16[4,16,128]{2,1,0:T(8,128)(2,1)S(1)}, u32[]{:S(2)}, u32[]{:S(2)}) collective-permute-start(bf16[4,16,128]{2,1,0:T(8,128)(2,1)S(1)} %get-tuple-element.26), channel_id=1, source_target_pairs={{0,1},{1,0},{2,3},{3,2},{4,5},{5,4},{6,7},{7,6},{8,9},{9,8},{10,11... | collective-permute-start | bytes 49160 | tf_op jit(solution)/shard_map/ppermute | solution.py:327
  21.6 1.0 %collective-permute-done.5 = bf16[4,16,128]{2,1,0:T(8,128)(2,1)S(1)} collective-permute-done((bf16[4,16,128]{2,1,0:T(8,128)(2,1)S(1)}, bf16[4,16,128]{2,1,0:T(8,128)(2,1)S(1)}, u32[]{:S(2)}, u32[]{:S(2)}) %collective-permute-start.5) | collective-permute-done | bytes 16416 | tf_op jit(solution)/shard_map/ppermute | solution.py:327
  22.6 0.5 %collective-permute-done.4 = bf16[4,16,128]{2,1,0:T(8,128)(2,1)S(1)} collective-permute-done((bf16[4,16,128]{2,1,0:T(8,128)(2,1)S(1)}, bf16[4,16,128]{2,1,0:T(8,128)(2,1)S(1)}, u32[]{:S(2)}, u32[]{:S(2)}) %collective-permute-start.4) | collective-permute-done | bytes 16416 | tf_op jit(solution)/shard_map/ppermute | solution.py:327
  23.1 2.1 %collective-permute-start.9 = (bf16[16,16,128]{2,1,0:T(8,128)(2,1)S(1)}, bf16[16,16,128]{2,1,0:T(8,128)(2,1)S(1)}, u32[]{:S(2)}, u32[]{:S(2)}) collective-permute-start(bf16[16,16,128]{2,1,0:T(8,128)(2,1)S(1)} %pad_maximum_fusion.own_ref.refs_1_), channel_id=1, source_target_pairs={{16,0},{20,4},{24,8},{28,12},{0,16},{4,20},{8,24},{12,28},{17,1},{... | collective-permute-start | bytes 196616 | tf_op jit(solution)/shard_map/ppermute | solution.py:331
  25.2 0.2 collective-permute-start.8
  25.4 2.4 %collective-permute-start.7 = (bf16[16,16,128]{2,1,0:T(8,128)(2,1)S(1)}, bf16[16,16,128]{2,1,0:T(8,128)(2,1)S(1)}, u32[]{:S(2)}, u32[]{:S(2)}) collective-permute-start(bf16[16,16,128]{2,1,0:T(8,128)(2,1)S(1)} %pad_maximum_fusion.own_ref.refs_1_), channel_id=1, source_target_pairs={{8,0},{12,4},{16,8},{20,12},{24,16},{28,20},{0,24},{4,28},{9,1},{1... | collective-permute-start | bytes 196616 | tf_op jit(solution)/shard_map/ppermute | solution.py:331
  27.8 1.1 %collective-permute-start.6 = (bf16[16,16,128]{2,1,0:T(8,128)(2,1)S(1)}, bf16[16,16,128]{2,1,0:T(8,128)(2,1)S(1)}, u32[]{:S(2)}, u32[]{:S(2)}) collective-permute-start(bf16[16,16,128]{2,1,0:T(8,128)(2,1)S(1)} %pad_maximum_fusion.own_ref.refs_1_), channel_id=1, source_target_pairs={{4,0},{8,4},{12,8},{16,12},{20,16},{24,20},{28,24},{0,28},{5,1},{9... | collective-permute-start | bytes 196616 | tf_op jit(solution)/shard_map/ppermute | solution.py:331
  28.9 0.3 shard_map.50.refs_0_
  29.2 7.8 %collective-permute-done.8.refs_4_ = bf16[16,16,128]{2,1,0:T(8,128)(2,1)S(1)} collective-permute-done((bf16[16,16,128]{2,1,0:T(8,128)(2,1)S(1)}, bf16[16,16,128]{2,1,0:T(8,128)(2,1)S(1)}, u32[]{:S(2)}, u32[]{:S(2)}) %collective-permute-start.8) | collective-permute-done | bytes 65568 | tf_op jit(solution)/shard_map/ppermute | solution.py:331
  37.0 1.3 %shard_map.51 = f32[16,5,8,32]{3,2,1,0:T(8,128)} custom-call(bf16[2,128,2048]{2,1,0:T(8,128)(2,1)S(1)} %shard_map.50.refs_0_, bf16[16,16,128]{2,1,0:T(8,128)(2,1)S(1)} %pad_maximum_fusion.own_ref.refs_1_, bf16[16,16,128]{2,1,0:T(8,128)(2,1)S(1)} %collective-permute-done.6.refs_2_, bf16[16,16,128]{2,1,0:T(8,128)(2,1)S(1)} %collective-permute-done.7.refs_3_, ...), custom_call_target="tpu_custom_call" | custom-call | flops 16777216 | bytes 1048576 | tf_op jit(solution)/shard_map/pallas_call | solution.py:340
  (14 shorter events, 0.1 us)
Async XLA Ops:
  0.0 1.2 %copy-start = (bf16[16,32768]{1,0:T(8,128)(2,1)S(1)}, bf16[16,32768]{1,0:T(8,128)(2,1)}, u32[]{:S(2)}) copy-start(bf16[16,32768]{1,0:T(8,128)(2,1)} %strain_ref.3) | copy-start | bytes 3145732
  1.2 5.8 %copy-start.1 = (bf16[16,32768]{1,0:T(8,128)(2,1)S(1)}, bf16[16,32768]{1,0:T(8,128)(2,1)}, u32[]{:S(2)}) copy-start(bf16[16,32768]{1,0:T(8,128)(2,1)} %strain_ref.3) | copy-start | bytes 3145732
  1.4 4.6 %collective-permute-start = (bf16[16,128]{1,0:T(8,128)(2,1)S(1)}, bf16[16,128]{1,0:T(8,128)(2,1)S(1)}, u32[]{:S(2)}, u32[]{:S(2)}) collective-permute-start(bf16[16,128]{1,0:T(8,128)(2,1)S(1)} %get-tuple-element.14), channel_id=1, source_target_pairs={{0,1},{1,2},{2,3},{4,5},{5,6},{6,7},{8,9},{9,10},{10,11},{12,13},{... | collective-permute-start | bytes 12296 | tf_op jit(solution)/shard_map/ppermute | solution.py:288
  6.0 1.1 %copy-start.2 = (bf16[1024,128]{1,0:T(8,128)(2,1)S(1)}, bf16[1024,128]{1,0:T(8,128)(2,1)}, u32[]{:S(2)}) copy-start(bf16[1024,128]{1,0:T(8,128)(2,1)} %constant.2.clone.dft_ref) | copy-start | bytes 786436
  6.0 1.0 %copy-start.3 = (f32[60]{0:T(128)S(1)}, f32[60]{0:T(128)}, u32[]{:S(2)}) copy-start(f32[60]{0:T(128)} %taps_ref.1) | copy-start | bytes 724
  6.0 1.0 %copy-start.4 = (f32[9]{0:T(128)S(1)}, f32[9]{0:T(128)}, u32[]{:S(2)}) copy-start(f32[9]{0:T(128)} %spatial_ref.1) | copy-start | bytes 112
  6.0 11.3 %collective-permute-start.1 = (bf16[4,32896]{1,0:T(4,128)(2,1)S(1)}, bf16[4,32896]{1,0:T(4,128)(2,1)S(1)}, u32[]{:S(2)}, u32[]{:S(2)}) collective-permute-start(bf16[4,32896]{1,0:T(4,128)(2,1)S(1)} %get-tuple-element.17), channel_id=1, source_target_pairs={{0,4},{4,0},{8,12},{12,8},{16,20},{20,16},{24,28},{28,24},{1,5},{5... | collective-permute-start | bytes 789512 | tf_op jit(solution)/shard_map/ppermute | solution.py:291
  6.3 11.0 %collective-permute-start.2 = (bf16[4,32896]{1,0:T(4,128)(2,1)S(1)}, bf16[4,32896]{1,0:T(4,128)(2,1)S(1)}, u32[]{:S(2)}, u32[]{:S(2)}) collective-permute-start(bf16[4,32896]{1,0:T(4,128)(2,1)S(1)} %get-tuple-element.18), channel_id=1, source_target_pairs={{4,8},{8,4},{12,16},{16,12},{20,24},{24,20},{5,9},{9,5},{13,17},{1... | collective-permute-start | bytes 789512 | tf_op jit(solution)/shard_map/ppermute | solution.py:292
  19.4 3.2 %collective-permute-start.5 = (bf16[4,16,128]{2,1,0:T(8,128)(2,1)S(1)}, bf16[4,16,128]{2,1,0:T(8,128)(2,1)S(1)}, u32[]{:S(2)}, u32[]{:S(2)}) collective-permute-start(bf16[4,16,128]{2,1,0:T(8,128)(2,1)S(1)} %get-tuple-element.24), channel_id=1, source_target_pairs={{0,3},{1,2},{2,1},{3,0},{4,7},{5,6},{6,5},{7,4},{8,11},{9,10},{10,... | collective-permute-start | bytes 49160 | tf_op jit(solution)/shard_map/ppermute | solution.py:327
  20.5 2.6 %collective-permute-start.4 = (bf16[4,16,128]{2,1,0:T(8,128)(2,1)S(1)}, bf16[4,16,128]{2,1,0:T(8,128)(2,1)S(1)}, u32[]{:S(2)}, u32[]{:S(2)}) collective-permute-start(bf16[4,16,128]{2,1,0:T(8,128)(2,1)S(1)} %get-tuple-element.25), channel_id=1, source_target_pairs={{0,2},{1,3},{2,0},{3,1},{4,6},{5,7},{6,4},{7,5},{8,10},{9,11},{10,... | collective-permute-start | bytes 49160 | tf_op jit(solution)/shard_map/ppermute | solution.py:327
  20.5 2.6 %collective-permute-start.3 = (bf16[4,16,128]{2,1,0:T(8,128)(2,1)S(1)}, bf16[4,16,128]{2,1,0:T(8,128)(2,1)S(1)}, u32[]{:S(2)}, u32[]{:S(2)}) collective-permute-start(bf16[4,16,128]{2,1,0:T(8,128)(2,1)S(1)} %get-tuple-element.26), channel_id=1, source_target_pairs={{0,1},{1,0},{2,3},{3,2},{4,5},{5,4},{6,7},{7,6},{8,9},{9,8},{10,11... | collective-permute-start | bytes 49160 | tf_op jit(solution)/shard_map/ppermute | solution.py:327
  23.1 6.1 %collective-permute-start.9 = (bf16[16,16,128]{2,1,0:T(8,128)(2,1)S(1)}, bf16[16,16,128]{2,1,0:T(8,128)(2,1)S(1)}, u32[]{:S(2)}, u32[]{:S(2)}) collective-permute-start(bf16[16,16,128]{2,1,0:T(8,128)(2,1)S(1)} %pad_maximum_fusion.own_ref.refs_1_), channel_id=1, source_target_pairs={{16,0},{20,4},{24,8},{28,12},{0,16},{4,20},{8,24},{12,28},{17,1},{... | collective-permute-start | bytes 196616 | tf_op jit(solution)/shard_map/ppermute | solution.py:331
  25.2 11.8 %collective-permute-start.8 = (bf16[16,16,128]{2,1,0:T(8,128)(2,1)S(1)}, bf16[16,16,128]{2,1,0:T(8,128)(2,1)S(1)}, u32[]{:S(2)}, u32[]{:S(2)}) collective-permute-start(bf16[16,16,128]{2,1,0:T(8,128)(2,1)S(1)} %pad_maximum_fusion.own_ref.refs_1_), channel_id=1, source_target_pairs={{12,0},{16,4},{20,8},{24,12},{28,16},{0,20},{4,24},{8,28},{13,1},{... | collective-permute-start | bytes 196616 | tf_op jit(solution)/shard_map/ppermute | solution.py:331
  25.4 11.6 %collective-permute-start.7 = (bf16[16,16,128]{2,1,0:T(8,128)(2,1)S(1)}, bf16[16,16,128]{2,1,0:T(8,128)(2,1)S(1)}, u32[]{:S(2)}, u32[]{:S(2)}) collective-permute-start(bf16[16,16,128]{2,1,0:T(8,128)(2,1)S(1)} %pad_maximum_fusion.own_ref.refs_1_), channel_id=1, source_target_pairs={{8,0},{12,4},{16,8},{20,12},{24,16},{28,20},{0,24},{4,28},{9,1},{1... | collective-permute-start | bytes 196616 | tf_op jit(solution)/shard_map/ppermute | solution.py:331
  27.8 9.2 %collective-permute-start.6 = (bf16[16,16,128]{2,1,0:T(8,128)(2,1)S(1)}, bf16[16,16,128]{2,1,0:T(8,128)(2,1)S(1)}, u32[]{:S(2)}, u32[]{:S(2)}) collective-permute-start(bf16[16,16,128]{2,1,0:T(8,128)(2,1)S(1)} %pad_maximum_fusion.own_ref.refs_1_), channel_id=1, source_target_pairs={{4,0},{8,4},{12,8},{16,12},{20,16},{24,20},{28,24},{0,28},{5,1},{9... | collective-permute-start | bytes 196616 | tf_op jit(solution)/shard_map/ppermute | solution.py:331

commit v6 on v5

--- a/solution.py
+++ b/solution.py
@@ -68,13 +68,24 @@
     return jnp.concatenate([high, weight - high], axis=0).astype(bf16)
 
 
+def received_row(source, count):
+    before = (source < HALO) == (lax.axis_index("chan") % 2 != 0)
+    return source % HALO + jnp.where(before, -HALO, count)
+
+
 def edge_lags(count):
     shape = (2 * HALO, 2 * HALO)
     target = lax.broadcasted_iota(jnp.int32, shape, 0)
     target = jnp.where(target < HALO, target, target + count - 2 * HALO)
+    return received_row(lax.broadcasted_iota(jnp.int32, shape, 1), count) + HALO - target
+
+
+def tail_lags(count):
+    shape = (count, 2 * count)
     source = lax.broadcasted_iota(jnp.int32, shape, 1)
-    before = (source < HALO) == (lax.axis_index("chan") % 2 != 0)
-    return source % HALO + jnp.where(before, 0, count + HALO) - target
+    row = jnp.where(source < count, source, received_row(source - count, count))
+    lag = row + HALO - lax.broadcasted_iota(jnp.int32, shape, 0)
+    return jnp.where(source < count + 2 * HALO, lag, -1)
 
 
 def filtered(mixed_ref, first, count, rows, toeplitz_ref):
@@ -116,14 +127,15 @@
 
 def own_kernel(
     strain_ref,
-    history_ref,
     taps_ref,
     spatial_ref,
     dft_ref,
     edge_ref,
     spectra_ref,
+    first_ref,
     toeplitz_ref,
     edge_mix_ref,
+    tail_mix_ref,
     mixed_ref,
     split_ref,
     scale_ref,
@@ -133,13 +145,14 @@
     weights = mixing(spatial_ref, source + HALO - lax.broadcasted_iota(jnp.int32, (rows, rows), 0))
     toeplitz_ref[...] = toeplitz(taps_ref)
     edge_mix_ref[...] = mixing(spatial_ref, edge_lags(rows))
+    tail_mix_ref[...] = mixing(spatial_ref, tail_lags(rows))
 
     def mix(columns):
         out = dot(weights, columns)
         high, low = halves(out[:rows] + out[rows:])
         return jnp.concatenate([high, low], axis=0)
 
-    mixed_ref[:, :LANES] = mix(history_ref[...])
+    mixed_ref[:, :LANES] = jnp.zeros((2 * rows, LANES), bf16)
     step = samples // 2
 
     def mix_step(i, _):
@@ -155,10 +168,26 @@
         band = filtered(mixed_ref, i * count, count, rows, toeplitz_ref)
         edge_ref[pl.ds(i * count, count)] = jnp.where(near, band[:, : rows // 2], band[:, rows // 2 :])
         windowed(band, i * (step // NFFT), rows, split_ref, scale_ref)
+
+        @pl.when(i == 0)
+        def _():
+            first_ref[...] = band[: NFFT // LANES]
+
         return 0
 
     lax.fori_loop(0, samples // step, filter_step, 0)
     spectra_ref[...] = spectra_of(split_ref, scale_ref, dft_ref, rows)
+
+
+def whole_block(edges, own):
+    rows = edges.shape[1]
+    near = lax.broadcasted_iota(jnp.int32, edges.shape, 1) < HALO
+    return jnp.concatenate([jnp.where(near, edges, own[:, :rows]), jnp.where(near, own[:, rows:], edges)], axis=1)
+
+
+def place_of(group, groups):
+    here = lax.axis_index("rep")
+    return jnp.bitwise_xor(group, here) if groups & (groups - 1) == 0 else lax.rem(group - here + groups, groups)
 
 
 def edge_kernel(
@@ -170,12 +199,13 @@
     toeplitz_ref,
     dft_ref,
     out_ref,
+    first_ref,
     mixed_ref,
     split_ref,
     scale_ref,
 ):
     rows = 2 * HALO
-    step = near_ref.shape[1] - LANES
+    step = near_ref.shape[1]
     weights = mix_ref[...]
 
     def mix(near, far):
@@ -185,22 +215,19 @@
         high = out.astype(bf16).astype(f32)
         return jnp.concatenate([high, out - high], axis=0).astype(bf16)
 
-    mixed_ref[...] = mix(near_ref[...], far_ref[...])
+    mixed_ref[:, :LANES] = jnp.zeros((2 * rows, LANES), bf16)
+    mixed_ref[:, LANES:] = mix(near_ref[...], far_ref[...])
     band = filtered(mixed_ref, 0, step // LANES, rows, toeplitz_ref) + edge_ref[...]
+    first_ref[...] = band[: NFFT // LANES]
     windowed(band, 0, rows, split_ref, scale_ref)
     edges = spectra_of(split_ref, scale_ref, dft_ref, rows)
-    near = lax.broadcasted_iota(jnp.int32, edges.shape, 1) < HALO
-    own = own_ref[...]
-    first = jnp.where(near, edges, own[:, :rows])
-    second = jnp.where(near, own[:, rows:], edges)
-    spectra = jnp.concatenate([first, second], axis=1)
+    spectra = whole_block(edges, own_ref[...])
     width_group = 2 * GROUP
     across = LANES // width_group
     slot = lax.broadcasted_iota(jnp.int32, spectra.shape[1:], 1) // width_group
     groups = out_ref.shape[0]
-    here = lax.axis_index("rep")
     for group in range(groups):
-        place = jnp.bitwise_xor(group, here) if groups & (groups - 1) == 0 else lax.rem(group - here + groups, groups)
+        place = place_of(group, groups)
         for outer in range(out_ref.shape[1]):
             tile = jnp.zeros(spectra.shape[1:], f32)
             for inner in range(across):
@@ -212,23 +239,45 @@
             out_ref[place, outer] = tile.astype(bf16)
 
 
-def rim_kernel(strain_ref, within_ref, across_ref, last_ref):
-    rows, samples = strain_ref.shape
+def first_kernel(
+    odd_ref, even_ref, mix_ref, toeplitz_ref, dft_ref, own_ref, edge_ref, pieces_ref, out_ref, split_ref, scale_ref
+):
+    rows = own_ref.shape[1]
+    here = lax.axis_index("rep")
+    tail = jnp.where(here % 2 == 1, odd_ref[...], even_ref[...])
+    mixed = dot(mix_ref[...], jnp.where(here == 0, jnp.zeros_like(tail), tail))
+    mixed = jnp.concatenate(halves(mixed[:rows] + mixed[rows:]), axis=0)
+    spill = dot(mixed, toeplitz_ref[:LANES, :])
+    spill = spill[:, :LANES] + spill[:, LANES:]
+    spill = spill[:rows] + spill[rows:]
+    band = whole_block(edge_ref[...], own_ref[...])
+    first = lax.broadcasted_iota(jnp.int32, band.shape, 0) == 0
+    windowed(jnp.where(first, band + spill, band), 0, rows, split_ref, scale_ref)
+    spectra = spectra_of(split_ref, scale_ref, dft_ref, rows)[0]
+    width_group = 2 * GROUP
+    groups = out_ref.shape[0]
+    out_ref[...] = pieces_ref[...]
+    here = lax.broadcasted_iota(jnp.int32, spectra.shape, 1) < width_group
+    for group in range(groups):
+        place = place_of(group, groups)
+        value = pltpu.roll(spectra, LANES - group * width_group, 1) if group else spectra
+        out_ref[place, 0] = jnp.where(here, value, pieces_ref[place, 0].astype(f32)).astype(bf16)
+
+
+def rim_kernel(strain_ref, within_ref, across_ref):
+    rows = strain_ref.shape[0]
     even = lax.axis_index("chan") % 2 == 0
     head, tail = strain_ref[:HALO], strain_ref[rows - HALO :]
     within_ref[...] = jnp.where(even, tail, head)
     across_ref[...] = jnp.where(even, head, tail)
-    last_ref[...] = strain_ref[:, samples - LANES :]
-
-
-def prefix_kernel(history_ref, within_ref, across_ref, near_ref, far_ref):
-    rows = history_ref.shape[0]
-    even = lax.axis_index("chan") % 2 == 0
-    head, tail = history_ref[:HALO], history_ref[rows - HALO :]
-    near_ref[:, :LANES] = jnp.where(even, tail, head)
-    near_ref[:, LANES:] = within_ref[...]
-    far_ref[:, :LANES] = jnp.where(even, head, tail)
-    far_ref[:, LANES:] = across_ref[...]
+
+
+def tail_kernel(strain_ref, near_ref, far_ref, tail_ref):
+    rows, samples = strain_ref.shape
+    last = slice(samples - LANES, samples)
+    received = [near_ref[:, last].astype(f32), far_ref[:, last].astype(f32), jnp.zeros((rows - 2 * HALO, LANES), f32)]
+    tail_ref[:rows] = strain_ref[:, last]
+    tail_ref[rows:] = jnp.concatenate(received, axis=0).astype(bf16)
 
 
 def left_kernel(own_ref, left_ref):
@@ -246,7 +295,7 @@
 
 
 def tile_kernel(scale, left_ref, *refs):
-    partner_refs, out_ref = refs[:-1], refs[-1]
+    partner_refs, out_ref = refs[-2::-1], refs[-1]
     parts, rows, _ = partner_refs[0].shape
     right = jnp.concatenate(
         [jnp.concatenate([ref[part] for part in range(parts)], axis=1) for ref in partner_refs], axis=0
@@ -283,22 +332,20 @@
     pairs_across = [(i, j) for i in range(chan) for j in (i + 1 if i % 2 else i - 1,) if 0 <= j < chan]
 
     rim = jax.ShapeDtypeStruct((HALO, samples), bf16)
-    last = jax.ShapeDtypeStruct((rows, LANES), bf16)
-    within, across, last = call(rim_kernel, [rim, rim, last], bytes_accessed=2**20)(strain)
-    history = lax.ppermute(last, "rep", [(i, i + 1) for i in range(rep - 1)])
-    rim = jax.ShapeDtypeStruct((HALO, LANES + samples), bf16)
-    within, across = call(prefix_kernel, [rim, rim], bytes_accessed=2**20, places="vvv")(history, within, across)
+    within, across = call(rim_kernel, [rim, rim], bytes_accessed=2**20)(strain)
     near = lax.ppermute(within, "chan", pairs_within)
     far = lax.ppermute(across, "chan", pairs_across)
 
     table = jnp.asarray(dft_table())
-    edge, own, filter_matrix, edge_mix = call(
+    edge, own, own_first, filter_matrix, edge_mix, tail_mix = call(
         own_kernel,
         [
             jax.ShapeDtypeStruct((blocks, 2 * HALO, LANES), f32),
             jax.ShapeDtypeStruct((windows, rows, LANES), f32),
+            jax.ShapeDtypeStruct((NFFT // LANES, rows, LANES), f32),
             jax.ShapeDtypeStruct((2 * LANES, 2 * LANES), bf16),
             jax.ShapeDtypeStruct((4 * HALO, 2 * HALO), bf16),
+            jax.ShapeDtypeStruct((2 * rows, 2 * rows), bf16),
         ],
         [
             pltpu.VMEM((2 * rows, LANES + samples), bf16),
@@ -307,11 +354,18 @@
         ],
         flops=2 * 2 * rows * samples * 512,
         bytes_accessed=4 * 2**20,
-        places="vvssv",
-    )(strain, history, fir_taps, spatial, table)
-    pieces = call(
+        places="vssv",
+    )(strain, fir_taps, spatial, table)
+    tail = jax.ShapeDtypeStruct((2 * rows, LANES), bf16)
+    tail = call(tail_kernel, tail, places="vvv")(strain, near, far)
+    if rep == 4:
+        tails = [lax.ppermute(tail, "rep", [(i, i ^ turn) for i in range(rep)]) for turn in (1, 3)]
+    else:
+        tails = [lax.ppermute(tail, "rep", [(i, i + 1) for i in range(rep - 1)])] * 2
+    pieces = jax.ShapeDtypeStruct((rep, windows * 2 * GROUP // LANES, rows, LANES), bf16)
+    pieces_made, edge_first = call(
         edge_kernel,
-        jax.ShapeDtypeStruct((rep, windows * 2 * GROUP // LANES, rows, LANES), bf16),
+        [pieces, jax.ShapeDtypeStruct((NFFT // LANES, 2 * HALO, LANES), f32)],
         [
             pltpu.VMEM((4 * HALO, LANES + samples), bf16),
             pltpu.VMEM((windows, 4 * HALO, NFFT), bf16),
@@ -321,6 +375,14 @@
         bytes_accessed=2 * 2**20,
         places="v" * 7,
     )(near, far, edge, own, edge_mix, filter_matrix, table)
+    pieces = call(
+        first_kernel,
+        pieces,
+        [pltpu.VMEM((1, 2 * rows, NFFT), bf16), pltpu.VMEM((1, rows, LANES), f32)],
+        flops=2**22,
+        bytes_accessed=2**19,
+        places="v" * 8,
+    )(*tails, tail_mix, filter_matrix, table, own_first, edge_first, pieces_made)
     arrived = [pieces[0]]
     for step in range(1, rep):
         to = [(i, i ^ step if rep & (rep - 1) == 0 else (i + step) % rep) for i in range(rep)]
@@ -343,7 +405,7 @@
         flops=2**24,
         bytes_accessed=2**20,
         places="v" * (STEPS + 2),
-    )(left, *partners)
+    )(left, *partners[::-1])
 
 
 def solution(mesh):

time: 38.5 us -> 37.2 us (0.966)
  the two profiles are of different devices: /device:TPU:27 before, /device:TPU:0 now
where the time goes in v6:
time: 37.2 us; the launch traced here: 37.1 us
  starting transfers between devices  16.3 us (44%)
  waiting for transfers between devices  10.8 us (29%)
  Pallas kernels  8.47 us (23%)
  local copies, waits for them, and re-layouts  1.25 us (3%)
    ppermute x4, starting transfers between devices, per_device(): lax.ppermute(gathered, 'chan', [((i + step) % chan, i) for i in range(cha...  9.04 us
    ppermute x1, waiting for transfers between devices, per_device(): near = lax.ppermute(within, 'chan', pairs_within)  6.37 us
    pallas_call x1, Pallas kernels, per_device(): call(own_kernel, [jax.ShapeDtypeStruct((blocks, 2 * HALO, LANES), f32), j...  4.1 us
    ppermute x1, starting transfers between devices, per_device(): near = lax.ppermute(within, 'chan', pairs_within)  3 us
    ppermute x3, waiting for transfers between devices, per_device(): arrived.append(lax.ppermute(pieces[step], 'rep', to))  2.92 us
    pallas_call x1, Pallas kernels, per_device(): call(edge_kernel, [pieces, jax.ShapeDtypeStruct((NFFT // LANES, 2 * HALO,...  2.01 us
    ppermute x3, starting transfers between devices, per_device(): arrived.append(lax.ppermute(pieces[step], 'rep', to))  1.93 us
    ppermute x2, starting transfers between devices, per_device(): lax.ppermute(tail, 'rep', [(i, i ^ turn) for i in range(rep)])  1.71 us
  transfers between devices with their start and end apart: 11, of which 4 were waited for; matrix products, arithmetic and copies ran while one was open for 0% of the time, Pallas kernels for 17%

profile of v6, /device:TPU:0, one launch (start us, length us, event | category | flops | bytes accessed | tf_op | source)
XLA Modules:
  0.0 37.1 jit_solution(8747116634488761931)
XLA Ops:
  0.0 1.2 %copy-done = bf16[16,32768]{1,0:T(8,128)(2,1)S(1)} copy-done((bf16[16,32768]{1,0:T(8,128)(2,1)S(1)}, bf16[16,32768]{1,0:T(8,128)(2,1)}, u32[]{:S(2)}) %copy-start) | copy-done | bytes 1048600
  1.2 0.1 shard_map.46
  1.4 0.0 copy-start.2
  1.4 0.0 copy-start.3
  1.4 3.0 %collective-permute-start = (bf16[4,32768]{1,0:T(4,128)(2,1)S(1)}, bf16[4,32768]{1,0:T(4,128)(2,1)S(1)}, u32[]{:S(2)}, u32[]{:S(2)}) collective-permute-start(bf16[4,32768]{1,0:T(4,128)(2,1)S(1)} %get-tuple-element.15), channel_id=1, source_target_pairs={{0,4},{4,0},{8,12},{12,8},{16,20},{20,16},{24,28},{28,24},{1,5},{5... | collective-permute-start | bytes 786440 | tf_op jit(solution)/shard_map/ppermute | solution.py:336
  4.4 0.7 %collective-permute-start.1 = (bf16[4,32768]{1,0:T(4,128)(2,1)S(1)}, bf16[4,32768]{1,0:T(4,128)(2,1)S(1)}, u32[]{:S(2)}, u32[]{:S(2)}) collective-permute-start(bf16[4,32768]{1,0:T(4,128)(2,1)S(1)} %get-tuple-element.16), channel_id=1, source_target_pairs={{4,8},{8,4},{12,16},{16,12},{20,24},{24,20},{5,9},{9,5},{13,17},{1... | collective-permute-start | bytes 786440 | tf_op jit(solution)/shard_map/ppermute | solution.py:337
  5.1 4.1 %shard_map.48 = (f32[256,8,128]{2,1,0:T(8,128)S(1)}, f32[32,16,128]{2,1,0:T(8,128)S(1)}, f32[8,16,128]{2,1,0:T(8,128)S(1)}, bf16[256,256]{1,0:T(8,128)(2,1)S(1)}...) custom-call(bf16[16,32768]{1,0:T(8,128)(2,1)S(1)} %copy-done, f32[60]{0:T(128)S(1)} %copy-done.2, f32[9]{0:T(128)S(1)} %copy-done.3, ...), custom_call_target="tpu_custom_call" | custom-call | flops 1073741824 | bytes 4194304 | tf_op jit(solution)/shard_map/pallas_call | solution.py:340
  9.2 6.4 %collective-permute-done.near_ref = bf16[4,32768]{1,0:T(4,128)(2,1)S(1)} collective-permute-done((bf16[4,32768]{1,0:T(4,128)(2,1)S(1)}, bf16[4,32768]{1,0:T(4,128)(2,1)S(1)}, u32[]{:S(2)}, u32[]{:S(2)}) %collective-permute-start) | collective-permute-done | bytes 262176 | tf_op jit(solution)/shard_map/ppermute | solution.py:336
  15.6 0.1 collective-permute-start.2
  15.7 1.6 %collective-permute-start.3 = (bf16[32,128]{1,0:T(8,128)(2,1)S(1)}, bf16[32,128]{1,0:T(8,128)(2,1)S(1)}, u32[]{:S(2)}, u32[]{:S(2)}) collective-permute-start(bf16[32,128]{1,0:T(8,128)(2,1)S(1)} %shard_map.47), channel_id=1, source_target_pairs={{0,3},{1,2},{2,1},{3,0},{4,7},{5,6},{6,5},{7,4},{8,11},{9,10},{10,... | collective-permute-start | bytes 24584 | tf_op jit(solution)/shard_map/ppermute | solution.py:362
  17.3 2.0 %shard_map.49 = (bf16[4,4,16,128]{3,2,1,0:T(8,128)(2,1)S(1)}, f32[8,8,128]{2,1,0:T(8,128)S(1)}) custom-call(bf16[4,32768]{1,0:T(4,128)(2,1)S(1)} %collective-permute-done.near_ref, bf16[4,32768]{1,0:T(4,128)(2,1)S(1)} %collective-permute-done.1.far_ref, f32[256,8,128]{2,1,0:T(8,128)S(1)} %get-tuple-element.20.edge_ref, ...), custom_call_target="tpu_custom_call" | custom-call | flops 536870912 | bytes 2097152 | tf_op jit(solution)/shard_map/pallas_call | solution.py:366
  19.4 0.5 %shard_map.50 = bf16[4,4,16,128]{3,2,1,0:T(8,128)(2,1)S(1)} custom-call(bf16[32,128]{1,0:T(8,128)(2,1)S(1)} %collective-permute-done.2.odd_ref, bf16[32,128]{1,0:T(8,128)(2,1)S(1)} %collective-permute-done.3.even_ref, bf16[32,32]{1,0:T(8,128)(2,1)S(1)} %get-tuple-element.17.mix_ref, bf16[256,256]{1,0:T(8,128)(2,1)S(1)} %get-tuple-element.18.toeplitz_ref, ...), custom_call_target="tpu_custom_call" | custom-call | flops 4194304 | bytes 524288 | tf_op jit(solution)/shard_map/pallas_call | solution.py:378
  19.9 1.1 %collective-permute-start.6 = (bf16[4,16,128]{2,1,0:T(8,128)(2,1)S(1)}, bf16[4,16,128]{2,1,0:T(8,128)(2,1)S(1)}, u32[]{:S(2)}, u32[]{:S(2)}) collective-permute-start(bf16[4,16,128]{2,1,0:T(8,128)(2,1)S(1)} %get-tuple-element.26), channel_id=1, source_target_pairs={{0,3},{1,2},{2,1},{3,0},{4,7},{5,6},{6,5},{7,4},{8,11},{9,10},{10,... | collective-permute-start | bytes 49160 | tf_op jit(solution)/shard_map/ppermute | solution.py:389
  21.0 0.7 %collective-permute-start.5 = (bf16[4,16,128]{2,1,0:T(8,128)(2,1)S(1)}, bf16[4,16,128]{2,1,0:T(8,128)(2,1)S(1)}, u32[]{:S(2)}, u32[]{:S(2)}) collective-permute-start(bf16[4,16,128]{2,1,0:T(8,128)(2,1)S(1)} %get-tuple-element.27), channel_id=1, source_target_pairs={{0,2},{1,3},{2,0},{3,1},{4,6},{5,7},{6,4},{7,5},{8,10},{9,11},{10,... | collective-permute-start | bytes 49160 | tf_op jit(solution)/shard_map/ppermute | solution.py:389
  21.7 0.2 collective-permute-start.4
  21.9 1.3 %collective-permute-done.6 = bf16[4,16,128]{2,1,0:T(8,128)(2,1)S(1)} collective-permute-done((bf16[4,16,128]{2,1,0:T(8,128)(2,1)S(1)}, bf16[4,16,128]{2,1,0:T(8,128)(2,1)S(1)}, u32[]{:S(2)}, u32[]{:S(2)}) %collective-permute-start.6) | collective-permute-done | bytes 16416 | tf_op jit(solution)/shard_map/ppermute | solution.py:389
  23.2 1.6 %collective-permute-done.5 = bf16[4,16,128]{2,1,0:T(8,128)(2,1)S(1)} collective-permute-done((bf16[4,16,128]{2,1,0:T(8,128)(2,1)S(1)}, bf16[4,16,128]{2,1,0:T(8,128)(2,1)S(1)}, u32[]{:S(2)}, u32[]{:S(2)}) %collective-permute-start.5) | collective-permute-done | bytes 16416 | tf_op jit(solution)/shard_map/ppermute | solution.py:389
  24.8 3.6 %collective-permute-start.7 = (bf16[16,16,128]{2,1,0:T(8,128)(2,1)S(1)}, bf16[16,16,128]{2,1,0:T(8,128)(2,1)S(1)}, u32[]{:S(2)}, u32[]{:S(2)}) collective-permute-start(bf16[16,16,128]{2,1,0:T(8,128)(2,1)S(1)} %pad_maximum_fusion.own_ref.refs_5_), channel_id=1, source_target_pairs={{16,0},{20,4},{24,8},{28,12},{0,16},{4,20},{8,24},{12,28},{17,1},{... | collective-permute-start | bytes 196616 | tf_op jit(solution)/shard_map/ppermute | solution.py:393
  28.4 1.3 %collective-permute-start.8 = (bf16[16,16,128]{2,1,0:T(8,128)(2,1)S(1)}, bf16[16,16,128]{2,1,0:T(8,128)(2,1)S(1)}, u32[]{:S(2)}, u32[]{:S(2)}) collective-permute-start(bf16[16,16,128]{2,1,0:T(8,128)(2,1)S(1)} %pad_maximum_fusion.own_ref.refs_5_), channel_id=1, source_target_pairs={{12,0},{16,4},{20,8},{24,12},{28,16},{0,20},{4,24},{8,28},{13,1},{... | collective-permute-start | bytes 196616 | tf_op jit(solution)/shard_map/ppermute | solution.py:393
  29.7 1.7 %collective-permute-start.9 = (bf16[16,16,128]{2,1,0:T(8,128)(2,1)S(1)}, bf16[16,16,128]{2,1,0:T(8,128)(2,1)S(1)}, u32[]{:S(2)}, u32[]{:S(2)}) collective-permute-start(bf16[16,16,128]{2,1,0:T(8,128)(2,1)S(1)} %pad_maximum_fusion.own_ref.refs_5_), channel_id=1, source_target_pairs={{8,0},{12,4},{16,8},{20,12},{24,16},{28,20},{0,24},{4,28},{9,1},{1... | collective-permute-start | bytes 196616 | tf_op jit(solution)/shard_map/ppermute | solution.py:393
  31.3 2.5 %collective-permute-start.10 = (bf16[16,16,128]{2,1,0:T(8,128)(2,1)S(1)}, bf16[16,16,128]{2,1,0:T(8,128)(2,1)S(1)}, u32[]{:S(2)}, u32[]{:S(2)}) collective-permute-start(bf16[16,16,128]{2,1,0:T(8,128)(2,1)S(1)} %pad_maximum_fusion.own_ref.refs_5_), channel_id=1, source_target_pairs={{4,0},{8,4},{12,8},{16,12},{20,16},{24,20},{28,24},{0,28},{5,1},{9... | collective-permute-start | bytes 196616 | tf_op jit(solution)/shard_map/ppermute | solution.py:393
  33.8 0.3 shard_map.51.refs_0_
  34.2 1.5 %collective-permute-done.10.refs_4_ = bf16[16,16,128]{2,1,0:T(8,128)(2,1)S(1)} collective-permute-done((bf16[16,16,128]{2,1,0:T(8,128)(2,1)S(1)}, bf16[16,16,128]{2,1,0:T(8,128)(2,1)S(1)}, u32[]{:S(2)}, u32[]{:S(2)}) %collective-permute-start.10) | collective-permute-done | bytes 65568 | tf_op jit(solution)/shard_map/ppermute | solution.py:393
  35.7 1.3 %shard_map.52 = f32[16,5,8,32]{3,2,1,0:T(8,128)} custom-call(bf16[2,128,2048]{2,1,0:T(8,128)(2,1)S(1)} %shard_map.51.refs_0_, bf16[16,16,128]{2,1,0:T(8,128)(2,1)S(1)} %collective-permute-done.7.refs_1_, bf16[16,16,128]{2,1,0:T(8,128)(2,1)S(1)} %collective-permute-done.8.refs_2_, bf16[16,16,128]{2,1,0:T(8,128)(2,1)S(1)} %collective-permute-done.9.refs_3_, ...), custom_call_target="tpu_custom_call" | custom-call | flops 16777216 | bytes 1048576 | tf_op jit(solution)/shard_map/pallas_call | solution.py:402
  (15 shorter events, 0.1 us)
Async XLA Ops:
  0.0 1.2 %copy-start = (bf16[16,32768]{1,0:T(8,128)(2,1)S(1)}, bf16[16,32768]{1,0:T(8,128)(2,1)}, u32[]{:S(2)}) copy-start(bf16[16,32768]{1,0:T(8,128)(2,1)} %strain_ref.5) | copy-start | bytes 3145732
  1.2 3.9 %copy-start.1 = (bf16[1024,128]{1,0:T(8,128)(2,1)S(1)}, bf16[1024,128]{1,0:T(8,128)(2,1)}, u32[]{:S(2)}) copy-start(bf16[1024,128]{1,0:T(8,128)(2,1)} %constant.2.clone.dft_ref) | copy-start | bytes 786436
  1.4 3.7 %copy-start.2 = (f32[60]{0:T(128)S(1)}, f32[60]{0:T(128)}, u32[]{:S(2)}) copy-start(f32[60]{0:T(128)} %taps_ref.1) | copy-start | bytes 724
  1.4 3.7 %copy-start.3 = (f32[9]{0:T(128)S(1)}, f32[9]{0:T(128)}, u32[]{:S(2)}) copy-start(f32[9]{0:T(128)} %spatial_ref.1) | copy-start | bytes 112
  1.4 14.2 %collective-permute-start = (bf16[4,32768]{1,0:T(4,128)(2,1)S(1)}, bf16[4,32768]{1,0:T(4,128)(2,1)S(1)}, u32[]{:S(2)}, u32[]{:S(2)}) collective-permute-start(bf16[4,32768]{1,0:T(4,128)(2,1)S(1)} %get-tuple-element.15), channel_id=1, source_target_pairs={{0,4},{4,0},{8,12},{12,8},{16,20},{20,16},{24,28},{28,24},{1,5},{5... | collective-permute-start | bytes 786440 | tf_op jit(solution)/shard_map/ppermute | solution.py:336
  4.4 11.2 %collective-permute-start.1 = (bf16[4,32768]{1,0:T(4,128)(2,1)S(1)}, bf16[4,32768]{1,0:T(4,128)(2,1)S(1)}, u32[]{:S(2)}, u32[]{:S(2)}) collective-permute-start(bf16[4,32768]{1,0:T(4,128)(2,1)S(1)} %get-tuple-element.16), channel_id=1, source_target_pairs={{4,8},{8,4},{12,16},{16,12},{20,24},{24,20},{5,9},{9,5},{13,17},{1... | collective-permute-start | bytes 786440 | tf_op jit(solution)/shard_map/ppermute | solution.py:337
  15.6 3.7 %collective-permute-start.2 = (bf16[32,128]{1,0:T(8,128)(2,1)S(1)}, bf16[32,128]{1,0:T(8,128)(2,1)S(1)}, u32[]{:S(2)}, u32[]{:S(2)}) collective-permute-start(bf16[32,128]{1,0:T(8,128)(2,1)S(1)} %shard_map.47), channel_id=1, source_target_pairs={{0,1},{1,0},{2,3},{3,2},{4,5},{5,4},{6,7},{7,6},{8,9},{9,8},{10,11... | collective-permute-start | bytes 24584 | tf_op jit(solution)/shard_map/ppermute | solution.py:362
  15.7 3.7 %collective-permute-start.3 = (bf16[32,128]{1,0:T(8,128)(2,1)S(1)}, bf16[32,128]{1,0:T(8,128)(2,1)S(1)}, u32[]{:S(2)}, u32[]{:S(2)}) collective-permute-start(bf16[32,128]{1,0:T(8,128)(2,1)S(1)} %shard_map.47), channel_id=1, source_target_pairs={{0,3},{1,2},{2,1},{3,0},{4,7},{5,6},{6,5},{7,4},{8,11},{9,10},{10,... | collective-permute-start | bytes 24584 | tf_op jit(solution)/shard_map/ppermute | solution.py:362
  19.9 3.2 %collective-permute-start.6 = (bf16[4,16,128]{2,1,0:T(8,128)(2,1)S(1)}, bf16[4,16,128]{2,1,0:T(8,128)(2,1)S(1)}, u32[]{:S(2)}, u32[]{:S(2)}) collective-permute-start(bf16[4,16,128]{2,1,0:T(8,128)(2,1)S(1)} %get-tuple-element.26), channel_id=1, source_target_pairs={{0,3},{1,2},{2,1},{3,0},{4,7},{5,6},{6,5},{7,4},{8,11},{9,10},{10,... | collective-permute-start | bytes 49160 | tf_op jit(solution)/shard_map/ppermute | solution.py:389
  21.0 3.7 %collective-permute-start.5 = (bf16[4,16,128]{2,1,0:T(8,128)(2,1)S(1)}, bf16[4,16,128]{2,1,0:T(8,128)(2,1)S(1)}, u32[]{:S(2)}, u32[]{:S(2)}) collective-permute-start(bf16[4,16,128]{2,1,0:T(8,128)(2,1)S(1)} %get-tuple-element.27), channel_id=1, source_target_pairs={{0,2},{1,3},{2,0},{3,1},{4,6},{5,7},{6,4},{7,5},{8,10},{9,11},{10,... | collective-permute-start | bytes 49160 | tf_op jit(solution)/shard_map/ppermute | solution.py:389
  21.7 3.1 %collective-permute-start.4 = (bf16[4,16,128]{2,1,0:T(8,128)(2,1)S(1)}, bf16[4,16,128]{2,1,0:T(8,128)(2,1)S(1)}, u32[]{:S(2)}, u32[]{:S(2)}) collective-permute-start(bf16[4,16,128]{2,1,0:T(8,128)(2,1)S(1)} %get-tuple-element.28), channel_id=1, source_target_pairs={{0,1},{1,0},{2,3},{3,2},{4,5},{5,4},{6,7},{7,6},{8,9},{9,8},{10,11... | collective-permute-start | bytes 49160 | tf_op jit(solution)/shard_map/ppermute | solution.py:389
  24.8 9.4 %collective-permute-start.7 = (bf16[16,16,128]{2,1,0:T(8,128)(2,1)S(1)}, bf16[16,16,128]{2,1,0:T(8,128)(2,1)S(1)}, u32[]{:S(2)}, u32[]{:S(2)}) collective-permute-start(bf16[16,16,128]{2,1,0:T(8,128)(2,1)S(1)} %pad_maximum_fusion.own_ref.refs_5_), channel_id=1, source_target_pairs={{16,0},{20,4},{24,8},{28,12},{0,16},{4,20},{8,24},{12,28},{17,1},{... | collective-permute-start | bytes 196616 | tf_op jit(solution)/shard_map/ppermute | solution.py:393
  28.4 5.8 %collective-permute-start.8 = (bf16[16,16,128]{2,1,0:T(8,128)(2,1)S(1)}, bf16[16,16,128]{2,1,0:T(8,128)(2,1)S(1)}, u32[]{:S(2)}, u32[]{:S(2)}) collective-permute-start(bf16[16,16,128]{2,1,0:T(8,128)(2,1)S(1)} %pad_maximum_fusion.own_ref.refs_5_), channel_id=1, source_target_pairs={{12,0},{16,4},{20,8},{24,12},{28,16},{0,20},{4,24},{8,28},{13,1},{... | collective-permute-start | bytes 196616 | tf_op jit(solution)/shard_map/ppermute | solution.py:393
  29.7 4.5 %collective-permute-start.9 = (bf16[16,16,128]{2,1,0:T(8,128)(2,1)S(1)}, bf16[16,16,128]{2,1,0:T(8,128)(2,1)S(1)}, u32[]{:S(2)}, u32[]{:S(2)}) collective-permute-start(bf16[16,16,128]{2,1,0:T(8,128)(2,1)S(1)} %pad_maximum_fusion.own_ref.refs_5_), channel_id=1, source_target_pairs={{8,0},{12,4},{16,8},{20,12},{24,16},{28,20},{0,24},{4,28},{9,1},{1... | collective-permute-start | bytes 196616 | tf_op jit(solution)/shard_map/ppermute | solution.py:393
  31.3 4.4 %collective-permute-start.10 = (bf16[16,16,128]{2,1,0:T(8,128)(2,1)S(1)}, bf16[16,16,128]{2,1,0:T(8,128)(2,1)S(1)}, u32[]{:S(2)}, u32[]{:S(2)}) collective-permute-start(bf16[16,16,128]{2,1,0:T(8,128)(2,1)S(1)} %pad_maximum_fusion.own_ref.refs_5_), channel_id=1, source_target_pairs={{4,0},{8,4},{12,8},{16,12},{20,16},{24,20},{28,24},{0,28},{5,1},{9... | collective-permute-start | bytes 196616 | tf_op jit(solution)/shard_map/ppermute | solution.py:393

commit v7 on v5

--- a/solution.py
+++ b/solution.py
@@ -68,13 +68,16 @@
     return jnp.concatenate([high, weight - high], axis=0).astype(bf16)
 
 
+def received_row(source, count):
+    before = (source < HALO) == (lax.axis_index("chan") % 2 != 0)
+    return source % HALO + jnp.where(before, -HALO, count)
+
+
 def edge_lags(count):
     shape = (2 * HALO, 2 * HALO)
     target = lax.broadcasted_iota(jnp.int32, shape, 0)
     target = jnp.where(target < HALO, target, target + count - 2 * HALO)
-    source = lax.broadcasted_iota(jnp.int32, shape, 1)
-    before = (source < HALO) == (lax.axis_index("chan") % 2 != 0)
-    return source % HALO + jnp.where(before, 0, count + HALO) - target
+    return received_row(lax.broadcasted_iota(jnp.int32, shape, 1), count) + HALO - target
 
 
 def filtered(mixed_ref, first, count, rows, toeplitz_ref):
@@ -106,6 +109,22 @@
             split_ref[first_window + window, :, block * LANES : (block + 1) * LANES] = both[window * per + block]
 
 
+def remainder(band):
+    squares = band * band
+    lane = lax.broadcasted_iota(jnp.int32, squares.shape[1:], 1)
+    total = jnp.where(lane < LANES // 2, 0.0, squares[0])
+    for block in range(1, NFFT // LANES):
+        total = total + squares[block]
+    return jnp.broadcast_to(jnp.sum(total, axis=1, keepdims=True), total.shape)
+
+
+def spill_of(mixed, toeplitz_ref):
+    rows = mixed.shape[0] // 2
+    out = dot(mixed, toeplitz_ref[:LANES, :])
+    out = out[:, :LANES] + out[:, LANES:]
+    return out[:rows] + out[rows:]
+
+
 def spectra_of(split_ref, scale_ref, dft_ref, rows):
     windows = split_ref.shape[0]
     out = dot(split_ref[...].reshape(windows * 2 * rows, NFFT), dft_ref[...])
@@ -116,12 +135,12 @@
 
 def own_kernel(
     strain_ref,
-    history_ref,
     taps_ref,
     spatial_ref,
     dft_ref,
     edge_ref,
     spectra_ref,
+    lead_ref,
     toeplitz_ref,
     edge_mix_ref,
     mixed_ref,
@@ -139,7 +158,7 @@
         high, low = halves(out[:rows] + out[rows:])
         return jnp.concatenate([high, low], axis=0)
 
-    mixed_ref[:, :LANES] = mix(history_ref[...])
+    mixed_ref[:, :LANES] = jnp.zeros((2 * rows, LANES), bf16)
     step = samples // 2
 
     def mix_step(i, _):
@@ -155,10 +174,29 @@
         band = filtered(mixed_ref, i * count, count, rows, toeplitz_ref)
         edge_ref[pl.ds(i * count, count)] = jnp.where(near, band[:, : rows // 2], band[:, rows // 2 :])
         windowed(band, i * (step // NFFT), rows, split_ref, scale_ref)
+
+        @pl.when(i == 0)
+        def _():
+            lead_ref[0] = band[0]
+            lead_ref[1] = remainder(band[: NFFT // LANES])
+            scale_ref[0] = jnp.ones((rows, LANES), f32)
+
         return 0
 
     lax.fori_loop(0, samples // step, filter_step, 0)
     spectra_ref[...] = spectra_of(split_ref, scale_ref, dft_ref, rows)
+    lead_ref[2] = spill_of(mixed_ref[:, samples:], toeplitz_ref)
+
+
+def whole_block(edges, own):
+    rows = edges.shape[1]
+    near = lax.broadcasted_iota(jnp.int32, edges.shape, 1) < HALO
+    return jnp.concatenate([jnp.where(near, edges, own[:, :rows]), jnp.where(near, own[:, rows:], edges)], axis=1)
+
+
+def place_of(group, groups):
+    here = lax.axis_index("rep")
+    return jnp.bitwise_xor(group, here) if groups & (groups - 1) == 0 else lax.rem(group - here + groups, groups)
 
 
 def edge_kernel(
@@ -166,6 +204,7 @@
     far_ref,
     edge_ref,
     own_ref,
+    lead_ref,
     mix_ref,
     toeplitz_ref,
     dft_ref,
@@ -175,60 +214,100 @@
     scale_ref,
 ):
     rows = 2 * HALO
-    step = near_ref.shape[1] - LANES
-    weights = mix_ref[...]
-
-    def mix(near, far):
-        both = jnp.concatenate([near.astype(f32), far.astype(f32)], axis=0).astype(bf16)
-        out = dot(weights, both)
-        out = out[:rows] + out[rows:]
-        high = out.astype(bf16).astype(f32)
-        return jnp.concatenate([high, out - high], axis=0).astype(bf16)
-
-    mixed_ref[...] = mix(near_ref[...], far_ref[...])
+    step = near_ref.shape[1]
+    both = jnp.concatenate([near_ref[...].astype(f32), far_ref[...].astype(f32)], axis=0).astype(bf16)
+    mixed = dot(mix_ref[...], both)
+    mixed = mixed[:rows] + mixed[rows:]
+    high = mixed.astype(bf16).astype(f32)
+    mixed_ref[:, :LANES] = jnp.zeros((2 * rows, LANES), bf16)
+    mixed_ref[:, LANES:] = jnp.concatenate([high, mixed - high], axis=0).astype(bf16)
     band = filtered(mixed_ref, 0, step // LANES, rows, toeplitz_ref) + edge_ref[...]
     windowed(band, 0, rows, split_ref, scale_ref)
+    scale_ref[0] = jnp.ones((rows, LANES), f32)
     edges = spectra_of(split_ref, scale_ref, dft_ref, rows)
-    near = lax.broadcasted_iota(jnp.int32, edges.shape, 1) < HALO
-    own = own_ref[...]
-    first = jnp.where(near, edges, own[:, :rows])
-    second = jnp.where(near, own[:, rows:], edges)
-    spectra = jnp.concatenate([first, second], axis=1)
-    width_group = 2 * GROUP
-    across = LANES // width_group
-    slot = lax.broadcasted_iota(jnp.int32, spectra.shape[1:], 1) // width_group
+    spectra = whole_block(edges, own_ref[...])
+
+    lead = whole_block(jnp.stack([band[0], remainder(band[: NFFT // LANES])]), lead_ref[:2])
+    spill = spill_of(mixed_ref[:, step:], toeplitz_ref)
+    near = lax.broadcasted_iota(jnp.int32, spill.shape, 0) < HALO
+    spill = lead_ref[2] + jnp.concatenate([jnp.where(near, spill, 0.0), jnp.where(near, 0.0, spill)], axis=0)
+    change = dot(jnp.concatenate(halves(spill), axis=0), dft_ref[:LANES, :])
+    change = change[: 2 * rows] + change[2 * rows :]
+    change = change + pltpu.roll(change, LANES // 2, 1)
+
+    def parted(values):
+        high = values.astype(bf16).astype(f32)
+        return high, values - high
+
+    width = 2 * GROUP
+    across = LANES // width
+    lane = lax.broadcasted_iota(jnp.int32, spectra.shape[1:], 1)
+    slot = lane // width
+    samples = parted(jnp.where(lane < LANES // 2, lead[0], pltpu.roll(spill, LANES // 2, 1)))
+    change = parted(change)
+    rest = parted(lead[1])
     groups = out_ref.shape[0]
+    for group in range(groups):
+        place = place_of(group, groups)
+
+        def moved(value, to):
+            shift = (to - group) * width % LANES
+            return pltpu.roll(value, shift, 1) if shift else value
+
+        for outer in range(out_ref.shape[1] - 3):
+            tile = moved(spectra[outer * across], 0)
+            for inner in range(1, across):
+                tile = jnp.where(slot == inner, moved(spectra[outer * across + inner], inner), tile)
+            out_ref[place, outer] = tile.astype(bf16)
+        extra = [parted(moved(spectra[0], 0))[1], moved(change[0], 1), moved(change[1], 2), *rest]
+        tile = extra[0]
+        for inner in range(1, len(extra)):
+            tile = jnp.where(slot == inner, extra[inner], tile)
+        for index, value in enumerate((*samples, tile)):
+            out_ref[place, out_ref.shape[1] - 3 + index] = value.astype(bf16)
+
+
+def merge_kernel(pieces_ref, *refs):
+    out_ref = refs[-1]
+    parts = [pieces_ref.at[0], *refs[:-1]]
+    count = pieces_ref.shape[1] - 3
+    groups = len(parts)
     here = lax.axis_index("rep")
-    for group in range(groups):
-        place = jnp.bitwise_xor(group, here) if groups & (groups - 1) == 0 else lax.rem(group - here + groups, groups)
-        for outer in range(out_ref.shape[1]):
-            tile = jnp.zeros(spectra.shape[1:], f32)
-            for inner in range(across):
-                shift = (inner - group) * width_group % LANES
-                value = spectra[outer * across + inner]
-                if shift:
-                    value = pltpu.roll(value, shift, 1)
-                tile = jnp.where(slot == inner, value, tile)
-            out_ref[place, outer] = tile.astype(bf16)
-
-
-def rim_kernel(strain_ref, within_ref, across_ref, last_ref):
-    rows, samples = strain_ref.shape
+    lane = lax.broadcasted_iota(jnp.int32, pieces_ref.shape[2:], 1)
+    width = 2 * GROUP
+    reps, leads, spills, rests, raws, changes = [], [], [], [], [], []
+    for step, part in enumerate(parts):
+        reps.append(jnp.bitwise_xor(here, step) if groups & (groups - 1) == 0 else lax.rem(here - step + groups, groups))
+        samples = part[count].astype(f32) + part[count + 1].astype(f32)
+        extra = part[count + 2].astype(f32)
+        leads.append(jnp.where(lane < LANES // 2, samples, 0.0))
+        spills.append(jnp.where(lane < LANES // 2, pltpu.roll(samples, LANES // 2, 1), 0.0))
+        raws.append(part[0].astype(f32))
+        changes.append(pltpu.roll(extra, LANES - width, 1) + pltpu.roll(extra, LANES - 2 * width, 1))
+        rests.append(extra[:, 3 * width : 3 * width + 1] + extra[:, 4 * width : 4 * width + 1])
+        raws[-1] = jnp.where(lane < width, raws[-1] + extra, raws[-1])
+    for step, part in enumerate(parts):
+        spill = jnp.zeros_like(leads[step])
+        change = jnp.zeros_like(leads[step])
+        for other in range(groups):
+            if other != step:
+                before = reps[other] == reps[step] - 1
+                spill = jnp.where(before, spills[other], spill)
+                change = jnp.where(before, changes[other], change)
+        lead = leads[step] + spill
+        power = (rests[step] + jnp.sum(lead * lead, axis=1, keepdims=True)) * (1.0 / NFFT)
+        first = (raws[step] + change) * (1.0 / jnp.sqrt(power + epsilon))
+        out_ref[step * count] = jnp.where(lane < width, first, raws[step]).astype(bf16)
+        for index in range(1, count):
+            out_ref[step * count + index] = part[index]
+
+
+def rim_kernel(strain_ref, within_ref, across_ref):
+    rows = strain_ref.shape[0]
     even = lax.axis_index("chan") % 2 == 0
     head, tail = strain_ref[:HALO], strain_ref[rows - HALO :]
     within_ref[...] = jnp.where(even, tail, head)
     across_ref[...] = jnp.where(even, head, tail)
-    last_ref[...] = strain_ref[:, samples - LANES :]
-
-
-def prefix_kernel(history_ref, within_ref, across_ref, near_ref, far_ref):
-    rows = history_ref.shape[0]
-    even = lax.axis_index("chan") % 2 == 0
-    head, tail = history_ref[:HALO], history_ref[rows - HALO :]
-    near_ref[:, :LANES] = jnp.where(even, tail, head)
-    near_ref[:, LANES:] = within_ref[...]
-    far_ref[:, :LANES] = jnp.where(even, head, tail)
-    far_ref[:, LANES:] = across_ref[...]
 
 
 def left_kernel(own_ref, left_ref):
@@ -283,20 +362,17 @@
     pairs_across = [(i, j) for i in range(chan) for j in (i + 1 if i % 2 else i - 1,) if 0 <= j < chan]
 
     rim = jax.ShapeDtypeStruct((HALO, samples), bf16)
-    last = jax.ShapeDtypeStruct((rows, LANES), bf16)
-    within, across, last = call(rim_kernel, [rim, rim, last], bytes_accessed=2**20)(strain)
-    history = lax.ppermute(last, "rep", [(i, i + 1) for i in range(rep - 1)])
-    rim = jax.ShapeDtypeStruct((HALO, LANES + samples), bf16)
-    within, across = call(prefix_kernel, [rim, rim], bytes_accessed=2**20, places="vvv")(history, within, across)
+    within, across = call(rim_kernel, [rim, rim], bytes_accessed=2**20)(strain)
     near = lax.ppermute(within, "chan", pairs_within)
     far = lax.ppermute(across, "chan", pairs_across)
 
     table = jnp.asarray(dft_table())
-    edge, own, filter_matrix, edge_mix = call(
+    edge, own, lead, filter_matrix, edge_mix = call(
         own_kernel,
         [
             jax.ShapeDtypeStruct((blocks, 2 * HALO, LANES), f32),
             jax.ShapeDtypeStruct((windows, rows, LANES), f32),
+            jax.ShapeDtypeStruct((3, rows, LANES), f32),
             jax.ShapeDtypeStruct((2 * LANES, 2 * LANES), bf16),
             jax.ShapeDtypeStruct((4 * HALO, 2 * HALO), bf16),
         ],
@@ -307,11 +383,12 @@
         ],
         flops=2 * 2 * rows * samples * 512,
         bytes_accessed=4 * 2**20,
-        places="vvssv",
-    )(strain, history, fir_taps, spatial, table)
+        places="vssv",
+    )(strain, fir_taps, spatial, table)
+    count = windows * 2 * GROUP // LANES
     pieces = call(
         edge_kernel,
-        jax.ShapeDtypeStruct((rep, windows * 2 * GROUP // LANES, rows, LANES), bf16),
+        jax.ShapeDtypeStruct((rep, count + 3, rows, LANES), bf16),
         [
             pltpu.VMEM((4 * HALO, LANES + samples), bf16),
             pltpu.VMEM((windows, 4 * HALO, NFFT), bf16),
@@ -319,13 +396,19 @@
         ],
         flops=2 * 2 * rows * samples * 256,
         bytes_accessed=2 * 2**20,
-        places="v" * 7,
-    )(near, far, edge, own, edge_mix, filter_matrix, table)
-    arrived = [pieces[0]]
+        places="v" * 8,
+    )(near, far, edge, own, lead, edge_mix, filter_matrix, table)
+    arrived = []
     for step in range(1, rep):
         to = [(i, i ^ step if rep & (rep - 1) == 0 else (i + step) % rep) for i in range(rep)]
         arrived.append(lax.ppermute(pieces[step], "rep", to))
-    gathered = jnp.concatenate(arrived, axis=0)
+    gathered = call(
+        merge_kernel,
+        jax.ShapeDtypeStruct((rep * count, rows, LANES), bf16),
+        flops=2**16,
+        bytes_accessed=2**18,
+        places="v" * rep,
+    )(pieces, *arrived)
     partners = [gathered]
     for step in range(1, STEPS + 1):
         partners.append(lax.ppermute(gathered, "chan", [((i + step) % chan, i) for i in range(chan)]))

time: 38.5 us -> 35.6 us (0.925)
  the two profiles are of different devices: /device:TPU:27 before, /device:TPU:0 now
where the time goes in v7:
time: 35.6 us; the launch traced here: 34.9 us
  starting transfers between devices  14.6 us (41%)
  waiting for transfers between devices  10.6 us (30%)
  Pallas kernels  8.34 us (23%)
  local copies, waits for them, and re-layouts  1.25 us (4%)
    ppermute x4, starting transfers between devices, per_device(): lax.ppermute(gathered, 'chan', [((i + step) % chan, i) for i in range(cha...  9.03 us
    ppermute x1, waiting for transfers between devices, per_device(): near = lax.ppermute(within, 'chan', pairs_within)  6.36 us
    pallas_call x1, Pallas kernels, per_device(): call(own_kernel, [jax.ShapeDtypeStruct((blocks, 2 * HALO, LANES), f32), j...  4.12 us
    ppermute x1, starting transfers between devices, per_device(): near = lax.ppermute(within, 'chan', pairs_within)  3 us
    pallas_call x1, Pallas kernels, per_device(): call(edge_kernel, jax.ShapeDtypeStruct((rep, count + 3, rows, LANES), bf1...  2.13 us
    ppermute x3, waiting for transfers between devices, per_device(): arrived.append(lax.ppermute(pieces[step], 'rep', to))  2.11 us
    ppermute x4, waiting for transfers between devices, per_device(): lax.ppermute(gathered, 'chan', [((i + step) % chan, i) for i in range(cha...  2.1 us
    ppermute x3, starting transfers between devices, per_device(): arrived.append(lax.ppermute(pieces[step], 'rep', to))  1.93 us
  transfers between devices with their start and end apart: 9, of which 5 were waited for; matrix products, arithmetic and copies ran while one was open for 0% of the time, Pallas kernels for 13%

profile of v7, /device:TPU:0, one launch (start us, length us, event | category | flops | bytes accessed | tf_op | source)
XLA Modules:
  0.0 34.9 jit_solution(15711522287348620631)
XLA Ops:
  0.0 1.2 %copy-done = bf16[16,32768]{1,0:T(8,128)(2,1)S(1)} copy-done((bf16[16,32768]{1,0:T(8,128)(2,1)S(1)}, bf16[16,32768]{1,0:T(8,128)(2,1)}, u32[]{:S(2)}) %copy-start) | copy-done | bytes 1048600
  1.2 0.1 shard_map.46
  1.4 0.0 copy-start.2
  1.4 0.0 copy-start.3
  1.4 3.0 %collective-permute-start = (bf16[4,32768]{1,0:T(4,128)(2,1)S(1)}, bf16[4,32768]{1,0:T(4,128)(2,1)S(1)}, u32[]{:S(2)}, u32[]{:S(2)}) collective-permute-start(bf16[4,32768]{1,0:T(4,128)(2,1)S(1)} %get-tuple-element.12), channel_id=1, source_target_pairs={{0,4},{4,0},{8,12},{12,8},{16,20},{20,16},{24,28},{28,24},{1,5},{5... | collective-permute-start | bytes 786440 | tf_op jit(solution)/shard_map/ppermute | solution.py:366
  4.4 0.7 %collective-permute-start.1 = (bf16[4,32768]{1,0:T(4,128)(2,1)S(1)}, bf16[4,32768]{1,0:T(4,128)(2,1)S(1)}, u32[]{:S(2)}, u32[]{:S(2)}) collective-permute-start(bf16[4,32768]{1,0:T(4,128)(2,1)S(1)} %get-tuple-element.13), channel_id=1, source_target_pairs={{4,8},{8,4},{12,16},{16,12},{20,24},{24,20},{5,9},{9,5},{13,17},{1... | collective-permute-start | bytes 786440 | tf_op jit(solution)/shard_map/ppermute | solution.py:367
  5.1 4.1 %shard_map.47 = (f32[256,8,128]{2,1,0:T(8,128)S(1)}, f32[32,16,128]{2,1,0:T(8,128)S(1)}, f32[3,16,128]{2,1,0:T(8,128)S(1)}, bf16[256,256]{1,0:T(8,128)(2,1)S(1)}, bf16[16,8]{1,0:T(8,128)(2,1)S(1)}) custom-call(bf16[16,32768]{1,0:T(8,128)(2,1)S(1)} %copy-done, f32[60]{0:T(128)S(1)} %copy-done.2, f32[9]{0:T(128)S(1)} %copy-done.3, bf16[1024,128]{1,0:T(8,128)(2,1)S(1)} %copy-done.1), custom_call_target="tpu_custom_call" | custom-call | flops 1073741824 | bytes 4194304 | tf_op jit(solution)/shard_map/pallas_call | solution.py:370
  9.2 6.4 %collective-permute-done.near_ref = bf16[4,32768]{1,0:T(4,128)(2,1)S(1)} collective-permute-done((bf16[4,32768]{1,0:T(4,128)(2,1)S(1)}, bf16[4,32768]{1,0:T(4,128)(2,1)S(1)}, u32[]{:S(2)}, u32[]{:S(2)}) %collective-permute-start) | collective-permute-done | bytes 262176 | tf_op jit(solution)/shard_map/ppermute | solution.py:366
  15.6 0.0 collective-permute-done.1.far_ref
  15.6 2.1 %shard_map.48.pieces_ref = bf16[4,7,16,128]{3,2,1,0:T(8,128)(2,1)S(1)} custom-call(bf16[4,32768]{1,0:T(4,128)(2,1)S(1)} %collective-permute-done.near_ref, bf16[4,32768]{1,0:T(4,128)(2,1)S(1)} %collective-permute-done.1.far_ref, f32[256,8,128]{2,1,0:T(8,128)S(1)} %get-tuple-element.14.edge_ref, f32[32,16,128]{2,1,0:T(8,128)S(1)} %get-tuple-element.15.own_ref, ...), custom_call_target="tpu_custom_call" | custom-call | flops 536870912 | bytes 2097152 | tf_op jit(solution)/shard_map/pallas_call | solution.py:389
  17.8 0.2 collective-permute-start.4
  17.9 1.5 %collective-permute-start.3 = (bf16[7,16,128]{2,1,0:T(8,128)(2,1)S(1)}, bf16[7,16,128]{2,1,0:T(8,128)(2,1)S(1)}, u32[]{:S(2)}, u32[]{:S(2)}) collective-permute-start(bf16[7,16,128]{2,1,0:T(8,128)(2,1)S(1)} %get-tuple-element.20), channel_id=1, source_target_pairs={{0,2},{1,3},{2,0},{3,1},{4,6},{5,7},{6,4},{7,5},{8,10},{9,11},{10,... | collective-permute-start | bytes 86024 | tf_op jit(solution)/shard_map/ppermute | solution.py:404
  19.4 0.3 collective-permute-start.2
  19.7 1.7 %collective-permute-done.4.refs_2_ = bf16[7,16,128]{2,1,0:T(8,128)(2,1)S(1)} collective-permute-done((bf16[7,16,128]{2,1,0:T(8,128)(2,1)S(1)}, bf16[7,16,128]{2,1,0:T(8,128)(2,1)S(1)}, u32[]{:S(2)}, u32[]{:S(2)}) %collective-permute-start.4) | collective-permute-done | bytes 28704 | tf_op jit(solution)/shard_map/ppermute | solution.py:404
  21.3 0.5 %collective-permute-done.3.refs_1_ = bf16[7,16,128]{2,1,0:T(8,128)(2,1)S(1)} collective-permute-done((bf16[7,16,128]{2,1,0:T(8,128)(2,1)S(1)}, bf16[7,16,128]{2,1,0:T(8,128)(2,1)S(1)}, u32[]{:S(2)}, u32[]{:S(2)}) %collective-permute-start.3) | collective-permute-done | bytes 28704 | tf_op jit(solution)/shard_map/ppermute | solution.py:404
  21.8 0.3 shard_map.49.own_ref.refs_1_
  22.1 3.6 %collective-permute-start.8 = (bf16[16,16,128]{2,1,0:T(8,128)(2,1)S(1)}, bf16[16,16,128]{2,1,0:T(8,128)(2,1)S(1)}, u32[]{:S(2)}, u32[]{:S(2)}) collective-permute-start(bf16[16,16,128]{2,1,0:T(8,128)(2,1)S(1)} %shard_map.49.own_ref.refs_1_), channel_id=1, source_target_pairs={{16,0},{20,4},{24,8},{28,12},{0,16},{4,20},{8,24},{12,28},{17,1},{... | collective-permute-start | bytes 196616 | tf_op jit(solution)/shard_map/ppermute | solution.py:414
  25.7 1.3 %collective-permute-start.7 = (bf16[16,16,128]{2,1,0:T(8,128)(2,1)S(1)}, bf16[16,16,128]{2,1,0:T(8,128)(2,1)S(1)}, u32[]{:S(2)}, u32[]{:S(2)}) collective-permute-start(bf16[16,16,128]{2,1,0:T(8,128)(2,1)S(1)} %shard_map.49.own_ref.refs_1_), channel_id=1, source_target_pairs={{12,0},{16,4},{20,8},{24,12},{28,16},{0,20},{4,24},{8,28},{13,1},{... | collective-permute-start | bytes 196616 | tf_op jit(solution)/shard_map/ppermute | solution.py:414
  27.0 1.6 %collective-permute-start.6 = (bf16[16,16,128]{2,1,0:T(8,128)(2,1)S(1)}, bf16[16,16,128]{2,1,0:T(8,128)(2,1)S(1)}, u32[]{:S(2)}, u32[]{:S(2)}) collective-permute-start(bf16[16,16,128]{2,1,0:T(8,128)(2,1)S(1)} %shard_map.49.own_ref.refs_1_), channel_id=1, source_target_pairs={{8,0},{12,4},{16,8},{20,12},{24,16},{28,20},{0,24},{4,28},{9,1},{1... | collective-permute-start | bytes 196616 | tf_op jit(solution)/shard_map/ppermute | solution.py:414
  28.6 2.5 %collective-permute-start.5 = (bf16[16,16,128]{2,1,0:T(8,128)(2,1)S(1)}, bf16[16,16,128]{2,1,0:T(8,128)(2,1)S(1)}, u32[]{:S(2)}, u32[]{:S(2)}) collective-permute-start(bf16[16,16,128]{2,1,0:T(8,128)(2,1)S(1)} %shard_map.49.own_ref.refs_1_), channel_id=1, source_target_pairs={{4,0},{8,4},{12,8},{16,12},{20,16},{24,20},{28,24},{0,28},{5,1},{9... | collective-permute-start | bytes 196616 | tf_op jit(solution)/shard_map/ppermute | solution.py:414
  31.1 0.3 shard_map.50.refs_0_
  31.5 0.2 collective-permute-done.7.refs_4_
  31.7 1.9 %collective-permute-done.6.refs_3_ = bf16[16,16,128]{2,1,0:T(8,128)(2,1)S(1)} collective-permute-done((bf16[16,16,128]{2,1,0:T(8,128)(2,1)S(1)}, bf16[16,16,128]{2,1,0:T(8,128)(2,1)S(1)}, u32[]{:S(2)}, u32[]{:S(2)}) %collective-permute-start.6) | collective-permute-done | bytes 65568 | tf_op jit(solution)/shard_map/ppermute | solution.py:414
  33.6 1.3 %shard_map.51 = f32[16,5,8,32]{3,2,1,0:T(8,128)} custom-call(bf16[2,128,2048]{2,1,0:T(8,128)(2,1)S(1)} %shard_map.50.refs_0_, bf16[16,16,128]{2,1,0:T(8,128)(2,1)S(1)} %shard_map.49.own_ref.refs_1_, bf16[16,16,128]{2,1,0:T(8,128)(2,1)S(1)} %collective-permute-done.5.refs_2_, bf16[16,16,128]{2,1,0:T(8,128)(2,1)S(1)} %collective-permute-done.6.refs_3_, ...), custom_call_target="tpu_custom_call" | custom-call | flops 16777216 | bytes 1048576 | tf_op jit(solution)/shard_map/pallas_call | solution.py:423
  (9 shorter events, 0.0 us)
Async XLA Ops:
  0.0 1.2 %copy-start = (bf16[16,32768]{1,0:T(8,128)(2,1)S(1)}, bf16[16,32768]{1,0:T(8,128)(2,1)}, u32[]{:S(2)}) copy-start(bf16[16,32768]{1,0:T(8,128)(2,1)} %strain_ref.3) | copy-start | bytes 3145732
  1.2 3.9 %copy-start.1 = (bf16[1024,128]{1,0:T(8,128)(2,1)S(1)}, bf16[1024,128]{1,0:T(8,128)(2,1)}, u32[]{:S(2)}) copy-start(bf16[1024,128]{1,0:T(8,128)(2,1)} %constant.2.clone.dft_ref) | copy-start | bytes 786436
  1.4 3.7 %copy-start.2 = (f32[60]{0:T(128)S(1)}, f32[60]{0:T(128)}, u32[]{:S(2)}) copy-start(f32[60]{0:T(128)} %taps_ref.1) | copy-start | bytes 724
  1.4 3.7 %copy-start.3 = (f32[9]{0:T(128)S(1)}, f32[9]{0:T(128)}, u32[]{:S(2)}) copy-start(f32[9]{0:T(128)} %spatial_ref.1) | copy-start | bytes 112
  1.4 14.2 %collective-permute-start = (bf16[4,32768]{1,0:T(4,128)(2,1)S(1)}, bf16[4,32768]{1,0:T(4,128)(2,1)S(1)}, u32[]{:S(2)}, u32[]{:S(2)}) collective-permute-start(bf16[4,32768]{1,0:T(4,128)(2,1)S(1)} %get-tuple-element.12), channel_id=1, source_target_pairs={{0,4},{4,0},{8,12},{12,8},{16,20},{20,16},{24,28},{28,24},{1,5},{5... | collective-permute-start | bytes 786440 | tf_op jit(solution)/shard_map/ppermute | solution.py:366
  4.4 11.2 %collective-permute-start.1 = (bf16[4,32768]{1,0:T(4,128)(2,1)S(1)}, bf16[4,32768]{1,0:T(4,128)(2,1)S(1)}, u32[]{:S(2)}, u32[]{:S(2)}) collective-permute-start(bf16[4,32768]{1,0:T(4,128)(2,1)S(1)} %get-tuple-element.13), channel_id=1, source_target_pairs={{4,8},{8,4},{12,16},{16,12},{20,24},{24,20},{5,9},{9,5},{13,17},{1... | collective-permute-start | bytes 786440 | tf_op jit(solution)/shard_map/ppermute | solution.py:367
  17.8 3.6 %collective-permute-start.4 = (bf16[7,16,128]{2,1,0:T(8,128)(2,1)S(1)}, bf16[7,16,128]{2,1,0:T(8,128)(2,1)S(1)}, u32[]{:S(2)}, u32[]{:S(2)}) collective-permute-start(bf16[7,16,128]{2,1,0:T(8,128)(2,1)S(1)} %get-tuple-element.19), channel_id=1, source_target_pairs={{0,3},{1,2},{2,1},{3,0},{4,7},{5,6},{6,5},{7,4},{8,11},{9,10},{10,... | collective-permute-start | bytes 86024 | tf_op jit(solution)/shard_map/ppermute | solution.py:404
  17.9 3.9 %collective-permute-start.3 = (bf16[7,16,128]{2,1,0:T(8,128)(2,1)S(1)}, bf16[7,16,128]{2,1,0:T(8,128)(2,1)S(1)}, u32[]{:S(2)}, u32[]{:S(2)}) collective-permute-start(bf16[7,16,128]{2,1,0:T(8,128)(2,1)S(1)} %get-tuple-element.20), channel_id=1, source_target_pairs={{0,2},{1,3},{2,0},{3,1},{4,6},{5,7},{6,4},{7,5},{8,10},{9,11},{10,... | collective-permute-start | bytes 86024 | tf_op jit(solution)/shard_map/ppermute | solution.py:404
  19.4 2.4 %collective-permute-start.2 = (bf16[7,16,128]{2,1,0:T(8,128)(2,1)S(1)}, bf16[7,16,128]{2,1,0:T(8,128)(2,1)S(1)}, u32[]{:S(2)}, u32[]{:S(2)}) collective-permute-start(bf16[7,16,128]{2,1,0:T(8,128)(2,1)S(1)} %get-tuple-element.21), channel_id=1, source_target_pairs={{0,1},{1,0},{2,3},{3,2},{4,5},{5,4},{6,7},{7,6},{8,9},{9,8},{10,11... | collective-permute-start | bytes 86024 | tf_op jit(solution)/shard_map/ppermute | solution.py:404
  22.1 9.4 %collective-permute-start.8 = (bf16[16,16,128]{2,1,0:T(8,128)(2,1)S(1)}, bf16[16,16,128]{2,1,0:T(8,128)(2,1)S(1)}, u32[]{:S(2)}, u32[]{:S(2)}) collective-permute-start(bf16[16,16,128]{2,1,0:T(8,128)(2,1)S(1)} %shard_map.49.own_ref.refs_1_), channel_id=1, source_target_pairs={{16,0},{20,4},{24,8},{28,12},{0,16},{4,20},{8,24},{12,28},{17,1},{... | collective-permute-start | bytes 196616 | tf_op jit(solution)/shard_map/ppermute | solution.py:414
  25.7 5.9 %collective-permute-start.7 = (bf16[16,16,128]{2,1,0:T(8,128)(2,1)S(1)}, bf16[16,16,128]{2,1,0:T(8,128)(2,1)S(1)}, u32[]{:S(2)}, u32[]{:S(2)}) collective-permute-start(bf16[16,16,128]{2,1,0:T(8,128)(2,1)S(1)} %shard_map.49.own_ref.refs_1_), channel_id=1, source_target_pairs={{12,0},{16,4},{20,8},{24,12},{28,16},{0,20},{4,24},{8,28},{13,1},{... | collective-permute-start | bytes 196616 | tf_op jit(solution)/shard_map/ppermute | solution.py:414
  27.0 6.6 %collective-permute-start.6 = (bf16[16,16,128]{2,1,0:T(8,128)(2,1)S(1)}, bf16[16,16,128]{2,1,0:T(8,128)(2,1)S(1)}, u32[]{:S(2)}, u32[]{:S(2)}) collective-permute-start(bf16[16,16,128]{2,1,0:T(8,128)(2,1)S(1)} %shard_map.49.own_ref.refs_1_), channel_id=1, source_target_pairs={{8,0},{12,4},{16,8},{20,12},{24,16},{28,20},{0,24},{4,28},{9,1},{1... | collective-permute-start | bytes 196616 | tf_op jit(solution)/shard_map/ppermute | solution.py:414
  28.6 4.9 %collective-permute-start.5 = (bf16[16,16,128]{2,1,0:T(8,128)(2,1)S(1)}, bf16[16,16,128]{2,1,0:T(8,128)(2,1)S(1)}, u32[]{:S(2)}, u32[]{:S(2)}) collective-permute-start(bf16[16,16,128]{2,1,0:T(8,128)(2,1)S(1)} %shard_map.49.own_ref.refs_1_), channel_id=1, source_target_pairs={{4,0},{8,4},{12,8},{16,12},{20,16},{24,20},{28,24},{0,28},{5,1},{9... | collective-permute-start | bytes 196616 | tf_op jit(solution)/shard_map/ppermute | solution.py:414

commit v8 on v7

--- a/solution.py
+++ b/solution.py
@@ -68,16 +68,30 @@
     return jnp.concatenate([high, weight - high], axis=0).astype(bf16)
 
 
-def received_row(source, count):
-    before = (source < HALO) == (lax.axis_index("chan") % 2 != 0)
-    return source % HALO + jnp.where(before, -HALO, count)
-
-
-def edge_lags(count):
-    shape = (2 * HALO, 2 * HALO)
-    target = lax.broadcasted_iota(jnp.int32, shape, 0)
-    target = jnp.where(target < HALO, target, target + count - 2 * HALO)
-    return received_row(lax.broadcasted_iota(jnp.int32, shape, 1), count) + HALO - target
+def direct(toeplitz_ref, dft_ref, out_ref):
+    lane = lax.broadcasted_iota(jnp.int32, (LANES, LANES), 1)
+    left = [toeplitz_ref[:LANES, :LANES], toeplitz_ref[:LANES, LANES:], toeplitz_ref[LANES:, :LANES], toeplitz_ref[LANES:, LANES:]]
+    left = jnp.concatenate(left, axis=0)
+    carried = jnp.zeros((LANES, LANES), f32)
+    for block in range(NFFT // LANES + 1):
+        weights = carried
+        if block < NFFT // LANES:
+            out = dot(left, dft_ref[block * LANES : (block + 1) * LANES, :])
+            out = out + pltpu.roll(out, LANES // 2, 1)
+            weights = weights + out[:LANES] + out[LANES : 2 * LANES]
+            carried = out[2 * LANES : 3 * LANES] + out[3 * LANES :]
+        high = weights.astype(bf16).astype(f32)
+        part = jnp.where(lane < LANES // 2, high, weights - high)
+        out_ref[block * LANES : (block + 1) * LANES, :] = part.astype(bf16)
+
+
+def edge_weights(spatial_ref, out_ref):
+    row = lax.broadcasted_iota(jnp.int32, out_ref.shape[1:], 0)
+    span = 2 * HALO
+    out_ref[0] = jnp.where(row < HALO, spatial_ref[0], spatial_ref[span])
+    for lag in range(1, HALO):
+        out_ref[lag] = jnp.where(row < HALO - lag, spatial_ref[lag], 0.0)
+        out_ref[HALO - 1 + lag] = jnp.where(row >= HALO + lag, spatial_ref[span - lag], 0.0)
 
 
 def filtered(mixed_ref, first, count, rows, toeplitz_ref):
@@ -143,6 +157,7 @@
     lead_ref,
     toeplitz_ref,
     edge_mix_ref,
+    direct_ref,
     mixed_ref,
     split_ref,
     scale_ref,
@@ -151,7 +166,8 @@
     source = lax.broadcasted_iota(jnp.int32, (rows, rows), 1)
     weights = mixing(spatial_ref, source + HALO - lax.broadcasted_iota(jnp.int32, (rows, rows), 0))
     toeplitz_ref[...] = toeplitz(taps_ref)
-    edge_mix_ref[...] = mixing(spatial_ref, edge_lags(rows))
+    edge_weights(spatial_ref, edge_mix_ref)
+    direct(toeplitz_ref, dft_ref, direct_ref)
 
     def mix(columns):
         out = dot(weights, columns)
@@ -172,7 +188,8 @@
 
     def filter_step(i, _):
         band = filtered(mixed_ref, i * count, count, rows, toeplitz_ref)
-        edge_ref[pl.ds(i * count, count)] = jnp.where(near, band[:, : rows // 2], band[:, rows // 2 :])
+        edge = jnp.where(near, band[:, : rows // 2], band[:, rows // 2 :])
+        edge_ref[:, pl.ds(pl.multiple_of(i * (rows // 2), rows // 2), rows // 2)] = edge
         windowed(band, i * (step // NFFT), rows, split_ref, scale_ref)
 
         @pl.when(i == 0)
@@ -184,6 +201,9 @@
         return 0
 
     lax.fori_loop(0, samples // step, filter_step, 0)
+    row = lax.broadcasted_iota(jnp.int32, scale_ref.shape, 1)
+    inside = (row >= HALO) & (row < rows - HALO)
+    scale_ref[...] = jnp.where(inside, scale_ref[...], 1.0)
     spectra_ref[...] = spectra_of(split_ref, scale_ref, dft_ref, rows)
     lead_ref[2] = spill_of(mixed_ref[:, samples:], toeplitz_ref)
 
@@ -208,27 +228,49 @@
     mix_ref,
     toeplitz_ref,
     dft_ref,
+    direct_ref,
     out_ref,
-    mixed_ref,
-    split_ref,
-    scale_ref,
+    received_ref,
 ):
     rows = 2 * HALO
-    step = near_ref.shape[1]
-    both = jnp.concatenate([near_ref[...].astype(f32), far_ref[...].astype(f32)], axis=0).astype(bf16)
-    mixed = dot(mix_ref[...], both)
-    mixed = mixed[:rows] + mixed[rows:]
-    high = mixed.astype(bf16).astype(f32)
-    mixed_ref[:, :LANES] = jnp.zeros((2 * rows, LANES), bf16)
-    mixed_ref[:, LANES:] = jnp.concatenate([high, mixed - high], axis=0).astype(bf16)
-    band = filtered(mixed_ref, 0, step // LANES, rows, toeplitz_ref) + edge_ref[...]
-    windowed(band, 0, rows, split_ref, scale_ref)
-    scale_ref[0] = jnp.ones((rows, LANES), f32)
-    edges = spectra_of(split_ref, scale_ref, dft_ref, rows)
-    spectra = whole_block(edges, own_ref[...])
-
-    lead = whole_block(jnp.stack([band[0], remainder(band[: NFFT // LANES])]), lead_ref[:2])
-    spill = spill_of(mixed_ref[:, step:], toeplitz_ref)
+    half = near_ref.shape[1] // 2
+    even = lax.axis_index("chan") % 2 == 0
+    near, far = near_ref[...].astype(f32), far_ref[...].astype(f32)
+    both = jnp.concatenate([jnp.where(even, far, near), jnp.where(even, near, far)], axis=0)
+    both = jnp.concatenate([jnp.zeros((rows, LANES), f32), both], axis=1)
+    received_ref[...] = jnp.concatenate([both[:, : half + LANES], both[:, half:]], axis=0).astype(bf16)
+
+    def mixed(samples):
+        out = samples * mix_ref[0]
+        for lag in range(1, HALO):
+            out = out + pltpu.roll(samples, rows - lag, 1) * mix_ref[lag]
+            out = out + pltpu.roll(samples, lag, 1) * mix_ref[HALO - 1 + lag]
+        return out
+
+    parts = [received_ref[:, start : start + 2 * LANES] for start in range(0, half, LANES)]
+    out = dot(jnp.concatenate(parts, axis=0), toeplitz_ref[...])
+    out = (out[:, :LANES] + out[:, LANES:]).reshape(-1, rows, LANES)
+    band = (mixed(out) + edge_ref[...].reshape(out.shape)).reshape(edge_ref.shape)
+    power = jnp.sum((band * band).reshape(-1, NFFT // LANES, 2 * rows, LANES), axis=1)
+    power = jnp.sum(power, axis=2, keepdims=True) * (1.0 / NFFT)
+    scale = 1.0 / jnp.sqrt(power + epsilon)
+    scale = jnp.concatenate([scale[:, :rows], scale[:, rows:]], axis=0)
+    window = lax.broadcasted_iota(jnp.int32, scale.shape, 0)
+    scale = jnp.where(window == 0, 1.0, scale)
+
+    parts = [received_ref[:, start : start + NFFT + LANES] for start in range(0, half, NFFT)]
+    out = dot(jnp.concatenate(parts, axis=0), direct_ref[...])
+    out = (out + pltpu.roll(out, LANES // 2, 1)).reshape(-1, 2 * rows, LANES)
+    edges = mixed(jnp.concatenate([out[:, :rows], out[:, rows:]], axis=0))
+    own = own_ref[...]
+    near = lax.broadcasted_iota(jnp.int32, edges.shape, 1) < HALO
+    edges = (edges + jnp.where(near, own[:, :rows], own[:, rows:])) * scale
+    spectra = whole_block(edges, own)
+    band = band[: NFFT // LANES, :rows]
+
+    lead = whole_block(jnp.stack([band[0], remainder(band)]), lead_ref[:2])
+    spill = dot(received_ref[:, half:], toeplitz_ref[:LANES, :])[rows:]
+    spill = mixed((spill[:, :LANES] + spill[:, LANES:])[None])[0]
     near = lax.broadcasted_iota(jnp.int32, spill.shape, 0) < HALO
     spill = lead_ref[2] + jnp.concatenate([jnp.where(near, spill, 0.0), jnp.where(near, 0.0, spill)], axis=0)
     change = dot(jnp.concatenate(halves(spill), axis=0), dft_ref[:LANES, :])
@@ -367,14 +409,15 @@
     far = lax.ppermute(across, "chan", pairs_across)
 
     table = jnp.asarray(dft_table())
-    edge, own, lead, filter_matrix, edge_mix = call(
+    edge, own, lead, filter_matrix, edge_mix, direct_matrix = call(
         own_kernel,
         [
-            jax.ShapeDtypeStruct((blocks, 2 * HALO, LANES), f32),
+            jax.ShapeDtypeStruct((blocks // 2, rows, LANES), f32),
             jax.ShapeDtypeStruct((windows, rows, LANES), f32),
             jax.ShapeDtypeStruct((3, rows, LANES), f32),
             jax.ShapeDtypeStruct((2 * LANES, 2 * LANES), bf16),
-            jax.ShapeDtypeStruct((4 * HALO, 2 * HALO), bf16),
+            jax.ShapeDtypeStruct((2 * HALO - 1, 2 * HALO, LANES), f32),
+            jax.ShapeDtypeStruct((LANES + NFFT, LANES), bf16),
         ],
         [
             pltpu.VMEM((2 * rows, LANES + samples), bf16),
@@ -390,14 +433,12 @@
         edge_kernel,
         jax.ShapeDtypeStruct((rep, count + 3, rows, LANES), bf16),
         [
-            pltpu.VMEM((4 * HALO, LANES + samples), bf16),
-            pltpu.VMEM((windows, 4 * HALO, NFFT), bf16),
-            pltpu.VMEM((windows, 2 * HALO, LANES), f32),
+            pltpu.VMEM((4 * HALO, LANES + samples // 2), bf16),
         ],
         flops=2 * 2 * rows * samples * 256,
         bytes_accessed=2 * 2**20,
-        places="v" * 8,
-    )(near, far, edge, own, lead, edge_mix, filter_matrix, table)
+        places="v" * 9,
+    )(near, far, edge, own, lead, edge_mix, filter_matrix, table, direct_matrix)
     arrived = []
     for step in range(1, rep):
         to = [(i, i ^ step if rep & (rep - 1) == 0 else (i + step) % rep) for i in range(rep)]

time: 35.6 us -> 35 us (0.983)
  waiting for transfers between devices: 10.6 us -> 9.8 us
    pallas_call x1, Pallas kernels: 4.12 us -> 4.87 us  [per_device(): call(own_kernel, [jax.ShapeDtypeStruct((blocks // 2, rows, LANES), f32),...]
    ppermute x1, waiting for transfers between devices: 6.36 us -> 5.61 us  [per_device(): near = lax.ppermute(within, 'chan', pairs_within)]
    pallas_call x1, Pallas kernels: 2.13 us -> 1.58 us  [per_device(): call(edge_kernel, jax.ShapeDtypeStruct((rep, count + 3, rows, LANES), bf1...]
  transfers between devices with their start and end apart: 9 -> 9, of which waited for: 5 -> 5; matrix products, arithmetic and copies ran while one was open for 0% -> 0% of each run, Pallas kernels for 13% -> 15%
where the time goes in v8:
time: 35 us; the launch traced here: 34.3 us
  starting transfers between devices  14.6 us (42%)
  waiting for transfers between devices  9.8 us (28%)
  Pallas kernels  8.53 us (24%)
  local copies, waits for them, and re-layouts  1.25 us (4%)
    ppermute x4, starting transfers between devices, per_device(): lax.ppermute(gathered, 'chan', [((i + step) % chan, i) for i in range(cha...  9.04 us
    ppermute x1, waiting for transfers between devices, per_device(): near = lax.ppermute(within, 'chan', pairs_within)  5.61 us
    pallas_call x1, Pallas kernels, per_device(): call(own_kernel, [jax.ShapeDtypeStruct((blocks // 2, rows, LANES), f32),...  4.87 us
    ppermute x1, starting transfers between devices, per_device(): near = lax.ppermute(within, 'chan', pairs_within)  3 us
    ppermute x4, waiting for transfers between devices, per_device(): lax.ppermute(gathered, 'chan', [((i + step) % chan, i) for i in range(cha...  2.1 us
    ppermute x3, waiting for transfers between devices, per_device(): arrived.append(lax.ppermute(pieces[step], 'rep', to))  2.1 us
    ppermute x3, starting transfers between devices, per_device(): arrived.append(lax.ppermute(pieces[step], 'rep', to))  1.93 us
    pallas_call x1, Pallas kernels, per_device(): call(edge_kernel, jax.ShapeDtypeStruct((rep, count + 3, rows, LANES), bf1...  1.58 us
  transfers between devices with their start and end apart: 9, of which 5 were waited for; matrix products, arithmetic and copies ran while one was open for 0% of the time, Pallas kernels for 15%

profile of v8, /device:TPU:0, one launch (start us, length us, event | category | flops | bytes accessed | tf_op | source)
XLA Modules:
  0.0 34.3 jit_solution(13000350936575193153)
XLA Ops:
  0.0 1.2 %copy-done = bf16[16,32768]{1,0:T(8,128)(2,1)S(1)} copy-done((bf16[16,32768]{1,0:T(8,128)(2,1)S(1)}, bf16[16,32768]{1,0:T(8,128)(2,1)}, u32[]{:S(2)}) %copy-start) | copy-done | bytes 1048600
  1.2 0.1 shard_map.46
  1.4 0.0 copy-start.2
  1.4 0.0 copy-start.3
  1.4 3.0 %collective-permute-start = (bf16[4,32768]{1,0:T(4,128)(2,1)S(1)}, bf16[4,32768]{1,0:T(4,128)(2,1)S(1)}, u32[]{:S(2)}, u32[]{:S(2)}) collective-permute-start(bf16[4,32768]{1,0:T(4,128)(2,1)S(1)} %get-tuple-element.13), channel_id=1, source_target_pairs={{0,4},{4,0},{8,12},{12,8},{16,20},{20,16},{24,28},{28,24},{1,5},{5... | collective-permute-start | bytes 786440 | tf_op jit(solution)/shard_map/ppermute | solution.py:408
  4.4 0.7 %collective-permute-start.1 = (bf16[4,32768]{1,0:T(4,128)(2,1)S(1)}, bf16[4,32768]{1,0:T(4,128)(2,1)S(1)}, u32[]{:S(2)}, u32[]{:S(2)}) collective-permute-start(bf16[4,32768]{1,0:T(4,128)(2,1)S(1)} %get-tuple-element.14), channel_id=1, source_target_pairs={{4,8},{8,4},{12,16},{16,12},{20,24},{24,20},{5,9},{9,5},{13,17},{1... | collective-permute-start | bytes 786440 | tf_op jit(solution)/shard_map/ppermute | solution.py:409
  5.1 4.9 %shard_map.47 = (f32[128,16,128]{2,1,0:T(8,128)S(1)}, f32[32,16,128]{2,1,0:T(8,128)S(1)}, f32[3,16,128]{2,1,0:T(8,128)S(1)}, bf16[256,256]{1,0:T(8,128)(2,1)S(1)...) custom-call(bf16[16,32768]{1,0:T(8,128)(2,1)S(1)} %copy-done, f32[60]{0:T(128)S(1)} %copy-done.2, ...), custom_call_target="tpu_custom_call" | custom-call | flops 1073741824 | bytes 4194304 | tf_op jit(solution)/shard_map/pallas_call | solution.py:412
  10.0 5.6 %collective-permute-done.near_ref = bf16[4,32768]{1,0:T(4,128)(2,1)S(1)} collective-permute-done((bf16[4,32768]{1,0:T(4,128)(2,1)S(1)}, bf16[4,32768]{1,0:T(4,128)(2,1)S(1)}, u32[]{:S(2)}, u32[]{:S(2)}) %collective-permute-start) | collective-permute-done | bytes 262176 | tf_op jit(solution)/shard_map/ppermute | solution.py:408
  15.6 0.0 collective-permute-done.1.far_ref
  15.6 1.6 %shard_map.48.pieces_ref = bf16[4,7,16,128]{3,2,1,0:T(8,128)(2,1)S(1)} custom-call(bf16[4,32768]{1,0:T(4,128)(2,1)S(1)} %collective-permute-done.near_ref, bf16[4,32768]{1,0:T(4,128)(2,1)S(1)} %collective-permute-done.1.far_ref, f32[128,16,128]{2,1,0:T(8,128)S(1)} %get-tuple-element.15.edge_ref, f32[32,16,128]{2,1,0:T(8,128)S(1)} %get-tuple-element.16.own_ref, ...), custom_call_target="tpu_custom_call" | custom-call | flops 536870912 | bytes 2097152 | tf_op jit(solution)/shard_map/pallas_call | solution.py:432
  17.2 0.2 collective-permute-start.4
  17.3 1.5 %collective-permute-start.3 = (bf16[7,16,128]{2,1,0:T(8,128)(2,1)S(1)}, bf16[7,16,128]{2,1,0:T(8,128)(2,1)S(1)}, u32[]{:S(2)}, u32[]{:S(2)}) collective-permute-start(bf16[7,16,128]{2,1,0:T(8,128)(2,1)S(1)} %get-tuple-element.22), channel_id=1, source_target_pairs={{0,2},{1,3},{2,0},{3,1},{4,6},{5,7},{6,4},{7,5},{8,10},{9,11},{10,... | collective-permute-start | bytes 86024 | tf_op jit(solution)/shard_map/ppermute | solution.py:445
  18.9 0.3 collective-permute-start.2
  19.1 1.7 %collective-permute-done.4.refs_2_ = bf16[7,16,128]{2,1,0:T(8,128)(2,1)S(1)} collective-permute-done((bf16[7,16,128]{2,1,0:T(8,128)(2,1)S(1)}, bf16[7,16,128]{2,1,0:T(8,128)(2,1)S(1)}, u32[]{:S(2)}, u32[]{:S(2)}) %collective-permute-start.4) | collective-permute-done | bytes 28704 | tf_op jit(solution)/shard_map/ppermute | solution.py:445
  20.8 0.4 %collective-permute-done.3.refs_1_ = bf16[7,16,128]{2,1,0:T(8,128)(2,1)S(1)} collective-permute-done((bf16[7,16,128]{2,1,0:T(8,128)(2,1)S(1)}, bf16[7,16,128]{2,1,0:T(8,128)(2,1)S(1)}, u32[]{:S(2)}, u32[]{:S(2)}) %collective-permute-start.3) | collective-permute-done | bytes 28704 | tf_op jit(solution)/shard_map/ppermute | solution.py:445
  21.2 0.3 shard_map.49.own_ref.refs_1_
  21.5 3.7 %collective-permute-start.8 = (bf16[16,16,128]{2,1,0:T(8,128)(2,1)S(1)}, bf16[16,16,128]{2,1,0:T(8,128)(2,1)S(1)}, u32[]{:S(2)}, u32[]{:S(2)}) collective-permute-start(bf16[16,16,128]{2,1,0:T(8,128)(2,1)S(1)} %shard_map.49.own_ref.refs_1_), channel_id=1, source_target_pairs={{16,0},{20,4},{24,8},{28,12},{0,16},{4,20},{8,24},{12,28},{17,1},{... | collective-permute-start | bytes 196616 | tf_op jit(solution)/shard_map/ppermute | solution.py:455
  25.2 1.2 %collective-permute-start.7 = (bf16[16,16,128]{2,1,0:T(8,128)(2,1)S(1)}, bf16[16,16,128]{2,1,0:T(8,128)(2,1)S(1)}, u32[]{:S(2)}, u32[]{:S(2)}) collective-permute-start(bf16[16,16,128]{2,1,0:T(8,128)(2,1)S(1)} %shard_map.49.own_ref.refs_1_), channel_id=1, source_target_pairs={{12,0},{16,4},{20,8},{24,12},{28,16},{0,20},{4,24},{8,28},{13,1},{... | collective-permute-start | bytes 196616 | tf_op jit(solution)/shard_map/ppermute | solution.py:455
  26.4 1.6 %collective-permute-start.6 = (bf16[16,16,128]{2,1,0:T(8,128)(2,1)S(1)}, bf16[16,16,128]{2,1,0:T(8,128)(2,1)S(1)}, u32[]{:S(2)}, u32[]{:S(2)}) collective-permute-start(bf16[16,16,128]{2,1,0:T(8,128)(2,1)S(1)} %shard_map.49.own_ref.refs_1_), channel_id=1, source_target_pairs={{8,0},{12,4},{16,8},{20,12},{24,16},{28,20},{0,24},{4,28},{9,1},{1... | collective-permute-start | bytes 196616 | tf_op jit(solution)/shard_map/ppermute | solution.py:455
  28.1 2.5 %collective-permute-start.5 = (bf16[16,16,128]{2,1,0:T(8,128)(2,1)S(1)}, bf16[16,16,128]{2,1,0:T(8,128)(2,1)S(1)}, u32[]{:S(2)}, u32[]{:S(2)}) collective-permute-start(bf16[16,16,128]{2,1,0:T(8,128)(2,1)S(1)} %shard_map.49.own_ref.refs_1_), channel_id=1, source_target_pairs={{4,0},{8,4},{12,8},{16,12},{20,16},{24,20},{28,24},{0,28},{5,1},{9... | collective-permute-start | bytes 196616 | tf_op jit(solution)/shard_map/ppermute | solution.py:455
  30.6 0.3 shard_map.50.refs_0_
  30.9 0.3 collective-permute-done.7.refs_4_
  31.2 1.8 %collective-permute-done.6.refs_3_ = bf16[16,16,128]{2,1,0:T(8,128)(2,1)S(1)} collective-permute-done((bf16[16,16,128]{2,1,0:T(8,128)(2,1)S(1)}, bf16[16,16,128]{2,1,0:T(8,128)(2,1)S(1)}, u32[]{:S(2)}, u32[]{:S(2)}) %collective-permute-start.6) | collective-permute-done | bytes 65568 | tf_op jit(solution)/shard_map/ppermute | solution.py:455
  33.0 1.3 %shard_map.51 = f32[16,5,8,32]{3,2,1,0:T(8,128)} custom-call(bf16[2,128,2048]{2,1,0:T(8,128)(2,1)S(1)} %shard_map.50.refs_0_, bf16[16,16,128]{2,1,0:T(8,128)(2,1)S(1)} %shard_map.49.own_ref.refs_1_, bf16[16,16,128]{2,1,0:T(8,128)(2,1)S(1)} %collective-permute-done.5.refs_2_, bf16[16,16,128]{2,1,0:T(8,128)(2,1)S(1)} %collective-permute-done.6.refs_3_, ...), custom_call_target="tpu_custom_call" | custom-call | flops 16777216 | bytes 1048576 | tf_op jit(solution)/shard_map/pallas_call | solution.py:464
  (9 shorter events, 0.0 us)
Async XLA Ops:
  0.0 1.2 %copy-start = (bf16[16,32768]{1,0:T(8,128)(2,1)S(1)}, bf16[16,32768]{1,0:T(8,128)(2,1)}, u32[]{:S(2)}) copy-start(bf16[16,32768]{1,0:T(8,128)(2,1)} %strain_ref.3) | copy-start | bytes 3145732
  1.2 3.9 %copy-start.1 = (bf16[1024,128]{1,0:T(8,128)(2,1)S(1)}, bf16[1024,128]{1,0:T(8,128)(2,1)}, u32[]{:S(2)}) copy-start(bf16[1024,128]{1,0:T(8,128)(2,1)} %constant.2.clone.dft_ref) | copy-start | bytes 786436
  1.4 3.7 %copy-start.2 = (f32[60]{0:T(128)S(1)}, f32[60]{0:T(128)}, u32[]{:S(2)}) copy-start(f32[60]{0:T(128)} %taps_ref.1) | copy-start | bytes 724
  1.4 3.7 %copy-start.3 = (f32[9]{0:T(128)S(1)}, f32[9]{0:T(128)}, u32[]{:S(2)}) copy-start(f32[9]{0:T(128)} %spatial_ref.1) | copy-start | bytes 112
  1.4 14.2 %collective-permute-start = (bf16[4,32768]{1,0:T(4,128)(2,1)S(1)}, bf16[4,32768]{1,0:T(4,128)(2,1)S(1)}, u32[]{:S(2)}, u32[]{:S(2)}) collective-permute-start(bf16[4,32768]{1,0:T(4,128)(2,1)S(1)} %get-tuple-element.13), channel_id=1, source_target_pairs={{0,4},{4,0},{8,12},{12,8},{16,20},{20,16},{24,28},{28,24},{1,5},{5... | collective-permute-start | bytes 786440 | tf_op jit(solution)/shard_map/ppermute | solution.py:408
  4.4 11.2 %collective-permute-start.1 = (bf16[4,32768]{1,0:T(4,128)(2,1)S(1)}, bf16[4,32768]{1,0:T(4,128)(2,1)S(1)}, u32[]{:S(2)}, u32[]{:S(2)}) collective-permute-start(bf16[4,32768]{1,0:T(4,128)(2,1)S(1)} %get-tuple-element.14), channel_id=1, source_target_pairs={{4,8},{8,4},{12,16},{16,12},{20,24},{24,20},{5,9},{9,5},{13,17},{1... | collective-permute-start | bytes 786440 | tf_op jit(solution)/shard_map/ppermute | solution.py:409
  17.2 3.6 %collective-permute-start.4 = (bf16[7,16,128]{2,1,0:T(8,128)(2,1)S(1)}, bf16[7,16,128]{2,1,0:T(8,128)(2,1)S(1)}, u32[]{:S(2)}, u32[]{:S(2)}) collective-permute-start(bf16[7,16,128]{2,1,0:T(8,128)(2,1)S(1)} %get-tuple-element.21), channel_id=1, source_target_pairs={{0,3},{1,2},{2,1},{3,0},{4,7},{5,6},{6,5},{7,4},{8,11},{9,10},{10,... | collective-permute-start | bytes 86024 | tf_op jit(solution)/shard_map/ppermute | solution.py:445
  17.3 3.9 %collective-permute-start.3 = (bf16[7,16,128]{2,1,0:T(8,128)(2,1)S(1)}, bf16[7,16,128]{2,1,0:T(8,128)(2,1)S(1)}, u32[]{:S(2)}, u32[]{:S(2)}) collective-permute-start(bf16[7,16,128]{2,1,0:T(8,128)(2,1)S(1)} %get-tuple-element.22), channel_id=1, source_target_pairs={{0,2},{1,3},{2,0},{3,1},{4,6},{5,7},{6,4},{7,5},{8,10},{9,11},{10,... | collective-permute-start | bytes 86024 | tf_op jit(solution)/shard_map/ppermute | solution.py:445
  18.9 2.4 %collective-permute-start.2 = (bf16[7,16,128]{2,1,0:T(8,128)(2,1)S(1)}, bf16[7,16,128]{2,1,0:T(8,128)(2,1)S(1)}, u32[]{:S(2)}, u32[]{:S(2)}) collective-permute-start(bf16[7,16,128]{2,1,0:T(8,128)(2,1)S(1)} %get-tuple-element.23), channel_id=1, source_target_pairs={{0,1},{1,0},{2,3},{3,2},{4,5},{5,4},{6,7},{7,6},{8,9},{9,8},{10,11... | collective-permute-start | bytes 86024 | tf_op jit(solution)/shard_map/ppermute | solution.py:445
  21.5 9.4 %collective-permute-start.8 = (bf16[16,16,128]{2,1,0:T(8,128)(2,1)S(1)}, bf16[16,16,128]{2,1,0:T(8,128)(2,1)S(1)}, u32[]{:S(2)}, u32[]{:S(2)}) collective-permute-start(bf16[16,16,128]{2,1,0:T(8,128)(2,1)S(1)} %shard_map.49.own_ref.refs_1_), channel_id=1, source_target_pairs={{16,0},{20,4},{24,8},{28,12},{0,16},{4,20},{8,24},{12,28},{17,1},{... | collective-permute-start | bytes 196616 | tf_op jit(solution)/shard_map/ppermute | solution.py:455
  25.2 6.0 %collective-permute-start.7 = (bf16[16,16,128]{2,1,0:T(8,128)(2,1)S(1)}, bf16[16,16,128]{2,1,0:T(8,128)(2,1)S(1)}, u32[]{:S(2)}, u32[]{:S(2)}) collective-permute-start(bf16[16,16,128]{2,1,0:T(8,128)(2,1)S(1)} %shard_map.49.own_ref.refs_1_), channel_id=1, source_target_pairs={{12,0},{16,4},{20,8},{24,12},{28,16},{0,20},{4,24},{8,28},{13,1},{... | collective-permute-start | bytes 196616 | tf_op jit(solution)/shard_map/ppermute | solution.py:455
  26.4 6.6 %collective-permute-start.6 = (bf16[16,16,128]{2,1,0:T(8,128)(2,1)S(1)}, bf16[16,16,128]{2,1,0:T(8,128)(2,1)S(1)}, u32[]{:S(2)}, u32[]{:S(2)}) collective-permute-start(bf16[16,16,128]{2,1,0:T(8,128)(2,1)S(1)} %shard_map.49.own_ref.refs_1_), channel_id=1, source_target_pairs={{8,0},{12,4},{16,8},{20,12},{24,16},{28,20},{0,24},{4,28},{9,1},{1... | collective-permute-start | bytes 196616 | tf_op jit(solution)/shard_map/ppermute | solution.py:455
  28.1 4.9 %collective-permute-start.5 = (bf16[16,16,128]{2,1,0:T(8,128)(2,1)S(1)}, bf16[16,16,128]{2,1,0:T(8,128)(2,1)S(1)}, u32[]{:S(2)}, u32[]{:S(2)}) collective-permute-start(bf16[16,16,128]{2,1,0:T(8,128)(2,1)S(1)} %shard_map.49.own_ref.refs_1_), channel_id=1, source_target_pairs={{4,0},{8,4},{12,8},{16,12},{20,16},{24,20},{28,24},{0,28},{5,1},{9... | collective-permute-start | bytes 196616 | tf_op jit(solution)/shard_map/ppermute | solution.py:455

commit v9 on v8

--- a/solution.py
+++ b/solution.py
@@ -86,12 +86,10 @@
 
 
 def edge_weights(spatial_ref, out_ref):
-    row = lax.broadcasted_iota(jnp.int32, out_ref.shape[1:], 0)
-    span = 2 * HALO
-    out_ref[0] = jnp.where(row < HALO, spatial_ref[0], spatial_ref[span])
-    for lag in range(1, HALO):
+    row = lax.broadcasted_iota(jnp.int32, out_ref.shape[1:], 0) % HALO
+    for lag in range(HALO):
         out_ref[lag] = jnp.where(row < HALO - lag, spatial_ref[lag], 0.0)
-        out_ref[HALO - 1 + lag] = jnp.where(row >= HALO + lag, spatial_ref[span - lag], 0.0)
+        out_ref[HALO + lag] = jnp.where(row >= lag, spatial_ref[2 * HALO - lag], 0.0)
 
 
 def filtered(mixed_ref, first, count, rows, toeplitz_ref):
@@ -188,8 +186,18 @@
 
     def filter_step(i, _):
         band = filtered(mixed_ref, i * count, count, rows, toeplitz_ref)
-        edge = jnp.where(near, band[:, : rows // 2], band[:, rows // 2 :])
-        edge_ref[:, pl.ds(pl.multiple_of(i * (rows // 2), rows // 2), rows // 2)] = edge
+        first, last = band[:, : rows // 2], band[:, rows // 2 :]
+
+        @pl.when(i == 0)
+        def _():
+            edge_ref[:, : rows // 2] = first
+            edge_ref[:, rows // 2 :] = pltpu.roll(last, HALO, 1)
+
+        @pl.when(i > 0)
+        def _():
+            edge_ref[:, : rows // 2] = jnp.where(near, edge_ref[:, : rows // 2], pltpu.roll(first, HALO, 1))
+            edge_ref[:, rows // 2 :] = jnp.where(near, edge_ref[:, rows // 2 :], last)
+
         windowed(band, i * (step // NFFT), rows, split_ref, scale_ref)
 
         @pl.when(i == 0)
@@ -236,41 +244,51 @@
     half = near_ref.shape[1] // 2
     even = lax.axis_index("chan") % 2 == 0
     near, far = near_ref[...].astype(f32), far_ref[...].astype(f32)
-    both = jnp.concatenate([jnp.where(even, far, near), jnp.where(even, near, far)], axis=0)
-    both = jnp.concatenate([jnp.zeros((rows, LANES), f32), both], axis=1)
-    received_ref[...] = jnp.concatenate([both[:, : half + LANES], both[:, half:]], axis=0).astype(bf16)
+    pad = jnp.zeros((HALO, LANES), f32)
+    parts = []
+    for rim in (jnp.where(even, far, near), jnp.where(even, near, far)):
+        parts += [jnp.concatenate([pad, rim[:, :half]], axis=1), rim[:, half - LANES :]]
+    received_ref[...] = jnp.concatenate(parts, axis=0).astype(bf16)
+    low = lax.broadcasted_iota(jnp.int32, (rows, LANES), 0) < HALO
 
     def mixed(samples):
-        out = samples * mix_ref[0]
+        first, last = samples[:, :rows], samples[:, rows:]
+        out = [first * mix_ref[0], last * mix_ref[HALO]]
         for lag in range(1, HALO):
-            out = out + pltpu.roll(samples, rows - lag, 1) * mix_ref[lag]
-            out = out + pltpu.roll(samples, lag, 1) * mix_ref[HALO - 1 + lag]
-        return out
-
+            out[0] = out[0] + pltpu.roll(first, rows - lag, 1) * mix_ref[lag]
+            out[1] = out[1] + pltpu.roll(last, lag, 1) * mix_ref[HALO + lag]
+        return jnp.concatenate(out, axis=1)
+
+    def early(values):
+        return jnp.where(low, values[:, :rows], pltpu.roll(values[:, rows:], HALO, 1))
+
+    def late(values):
+        return jnp.where(low, pltpu.roll(values[:, :rows], HALO, 1), values[:, rows:])
+
+    spans = [received_ref[:, start : start + NFFT + LANES] for start in range(0, half, NFFT)]
+    flat = dot(jnp.concatenate(spans, axis=0), direct_ref[...])
+    flat = (flat + pltpu.roll(flat, LANES // 2, 1)).reshape(-1, 2 * rows, LANES)
     parts = [received_ref[:, start : start + 2 * LANES] for start in range(0, half, LANES)]
     out = dot(jnp.concatenate(parts, axis=0), toeplitz_ref[...])
-    out = (out[:, :LANES] + out[:, LANES:]).reshape(-1, rows, LANES)
-    band = (mixed(out) + edge_ref[...].reshape(out.shape)).reshape(edge_ref.shape)
+    out = (out[:, :LANES] + out[:, LANES:]).reshape(edge_ref.shape)
+    band = mixed(out) + edge_ref[...]
     power = jnp.sum((band * band).reshape(-1, NFFT // LANES, 2 * rows, LANES), axis=1)
+    power = jnp.concatenate([early(power), late(power)], axis=0)
     power = jnp.sum(power, axis=2, keepdims=True) * (1.0 / NFFT)
     scale = 1.0 / jnp.sqrt(power + epsilon)
-    scale = jnp.concatenate([scale[:, :rows], scale[:, rows:]], axis=0)
     window = lax.broadcasted_iota(jnp.int32, scale.shape, 0)
     scale = jnp.where(window == 0, 1.0, scale)
 
-    parts = [received_ref[:, start : start + NFFT + LANES] for start in range(0, half, NFFT)]
-    out = dot(jnp.concatenate(parts, axis=0), direct_ref[...])
-    out = (out + pltpu.roll(out, LANES // 2, 1)).reshape(-1, 2 * rows, LANES)
-    edges = mixed(jnp.concatenate([out[:, :rows], out[:, rows:]], axis=0))
+    edges = mixed(flat)
+    edges = jnp.concatenate([early(edges), late(edges)], axis=0)
     own = own_ref[...]
-    near = lax.broadcasted_iota(jnp.int32, edges.shape, 1) < HALO
-    edges = (edges + jnp.where(near, own[:, :rows], own[:, rows:])) * scale
+    edges = (edges + jnp.where(low, own[:, :rows], own[:, rows:])) * scale
     spectra = whole_block(edges, own)
-    band = band[: NFFT // LANES, :rows]
+    band = early(band[: NFFT // LANES])
 
     lead = whole_block(jnp.stack([band[0], remainder(band)]), lead_ref[:2])
-    spill = dot(received_ref[:, half:], toeplitz_ref[:LANES, :])[rows:]
-    spill = mixed((spill[:, :LANES] + spill[:, LANES:])[None])[0]
+    spill = dot(received_ref[:, half:], toeplitz_ref[:LANES, :])
+    spill = late(mixed((spill[:, :LANES] + spill[:, LANES:])[None]))[0]
     near = lax.broadcasted_iota(jnp.int32, spill.shape, 0) < HALO
     spill = lead_ref[2] + jnp.concatenate([jnp.where(near, spill, 0.0), jnp.where(near, 0.0, spill)], axis=0)
     change = dot(jnp.concatenate(halves(spill), axis=0), dft_ref[:LANES, :])
@@ -311,7 +329,7 @@
 
 def merge_kernel(pieces_ref, *refs):
     out_ref = refs[-1]
-    parts = [pieces_ref.at[0], *refs[:-1]]
+    parts = [pieces_ref.at[0], *(refs[i] for i in (0, 2, 1))]
     count = pieces_ref.shape[1] - 3
     groups = len(parts)
     here = lax.axis_index("rep")
@@ -367,26 +385,35 @@
 
 
 def tile_kernel(scale, left_ref, *refs):
-    partner_refs, out_ref = refs[:-1], refs[-1]
+    *partner_refs, out_ref, tile_ref, done = refs
     parts, rows, _ = partner_refs[0].shape
     right = jnp.concatenate(
         [jnp.concatenate([ref[part] for part in range(parts)], axis=1) for ref in partner_refs], axis=0
     )
     real = dot_t(left_ref[0], right) * scale
     imag = dot_t(left_ref[1], right) * scale
+    copies = []
+    span = rows // 2
     for c in range(rows):
         for s in range(len(partner_refs)):
             a = real[c * GROUP : (c + 1) * GROUP, s * rows : (s + 1) * rows]
             b = imag[c * GROUP : (c + 1) * GROUP, s * rows : (s + 1) * rows]
-            out_ref[c, s] = jnp.concatenate([a, b], axis=1)
-
-
-def call(kernel, out_shape, scratch=(), flops=0, bytes_accessed=0, places="v"):
+            tile_ref[c, s] = jnp.concatenate([a, b], axis=1)
+        if c % span == span - 1:
+            run = slice(c + 1 - span, c + 1)
+            copies.append(pltpu.make_async_copy(tile_ref.at[run], out_ref.at[run], done.at[c // span]))
+            copies[-1].start()
+    for copy in copies:
+        copy.wait()
+
+
+def call(kernel, out_shape, scratch=(), flops=0, bytes_accessed=0, places="v", out_specs=None):
     whole = {"v": pl.BlockSpec(memory_space=pltpu.VMEM), "s": pl.BlockSpec(memory_space=pltpu.SMEM)}
     return pl.pallas_call(
         kernel,
         out_shape=out_shape,
         in_specs=[whole[place] for place in places],
+        **({} if out_specs is None else {"out_specs": out_specs}),
         scratch_shapes=list(scratch),
         compiler_params=pltpu.CompilerParams(vmem_limit_bytes=32 * 2**20),
         cost_estimate=pl.CostEstimate(flops=flops, bytes_accessed=bytes_accessed, transcendentals=0),
@@ -416,7 +443,7 @@
             jax.ShapeDtypeStruct((windows, rows, LANES), f32),
             jax.ShapeDtypeStruct((3, rows, LANES), f32),
             jax.ShapeDtypeStruct((2 * LANES, 2 * LANES), bf16),
-            jax.ShapeDtypeStruct((2 * HALO - 1, 2 * HALO, LANES), f32),
+            jax.ShapeDtypeStruct((2 * HALO, 2 * HALO, LANES), f32),
             jax.ShapeDtypeStruct((LANES + NFFT, LANES), bf16),
         ],
         [
@@ -449,7 +476,7 @@
         flops=2**16,
         bytes_accessed=2**18,
         places="v" * rep,
-    )(pieces, *arrived)
+    )(pieces, *(arrived[i] for i in (0, 2, 1)))
     partners = [gathered]
     for step in range(1, STEPS + 1):
         partners.append(lax.ppermute(gathered, "chan", [((i + step) % chan, i) for i in range(chan)]))
@@ -461,9 +488,12 @@
         bytes_accessed=2**20,
     )(gathered)
     scale = 1.0 / (windows * rep)
+    tiles = (rows, STEPS + 1, BINS // rep, 2 * rows)
     return call(
         lambda *refs: tile_kernel(scale, *refs),
-        jax.ShapeDtypeStruct((rows, STEPS + 1, BINS // rep, 2 * rows), f32),
+        jax.ShapeDtypeStruct(tiles, f32),
+        [pltpu.VMEM(tiles, f32), pltpu.SemaphoreType.DMA((2,))],
+        out_specs=pl.BlockSpec(memory_space=pl.ANY),
         flops=2**24,
         bytes_accessed=2**20,
         places="v" * (STEPS + 2),

time: 35 us -> 34.5 us (0.986); the launches traced: 34.3 us -> 34.3 us
  waiting for transfers between devices: 9.8 us -> 8.89 us
  Pallas kernels: 8.53 us -> 9.13 us
    pallas_call x1, Pallas kernels: 4.87 us -> 5.81 us  [per_device(): call(own_kernel, [jax.ShapeDtypeStruct((blocks // 2, rows, LANES), f32),...]
    ppermute x1, waiting for transfers between devices: 5.61 us -> 4.66 us  [per_device(): near = lax.ppermute(within, 'chan', pairs_within)]
    ppermute x3, waiting for transfers between devices: 2.1 us -> 2.67 us  [per_device(): arrived.append(lax.ppermute(pieces[step], 'rep', to))]
    ppermute x4, waiting for transfers between devices: 2.1 us -> 1.54 us  [per_device(): lax.ppermute(gathered, 'chan', [((i + step) % chan, i) for i in range(cha...]
  transfers between devices with their start and end apart: 9 -> 9, of which waited for: 5 -> 5; matrix products, arithmetic and copies ran while one was open for 0% -> 0% of each run, Pallas kernels for 15% -> 18%
where the time goes in v9:
time: 34.5 us; the launch traced here: 34.3 us
  starting transfers between devices  14.9 us (43%)
  Pallas kernels  9.13 us (26%)
  waiting for transfers between devices  8.89 us (26%)
  local copies, waits for them, and re-layouts  1.25 us (4%)
    ppermute x4, starting transfers between devices, per_device(): lax.ppermute(gathered, 'chan', [((i + step) % chan, i) for i in range(cha...  9.04 us
    pallas_call x1, Pallas kernels, per_device(): call(own_kernel, [jax.ShapeDtypeStruct((blocks // 2, rows, LANES), f32),...  5.81 us
    ppermute x1, waiting for transfers between devices, per_device(): near = lax.ppermute(within, 'chan', pairs_within)  4.66 us
    ppermute x1, starting transfers between devices, per_device(): near = lax.ppermute(within, 'chan', pairs_within)  3 us
    ppermute x3, waiting for transfers between devices, per_device(): arrived.append(lax.ppermute(pieces[step], 'rep', to))  2.67 us
    ppermute x3, starting transfers between devices, per_device(): arrived.append(lax.ppermute(pieces[step], 'rep', to))  2.21 us
    ppermute x4, waiting for transfers between devices, per_device(): lax.ppermute(gathered, 'chan', [((i + step) % chan, i) for i in range(cha...  1.54 us
    pallas_call x1, Pallas kernels, per_device(): call(lambda *refs: tile_kernel(scale, *refs), jax.ShapeDtypeStruct(tiles,...  1.29 us
  transfers between devices with their start and end apart: 9, of which 5 were waited for; matrix products, arithmetic and copies ran while one was open for 0% of the time, Pallas kernels for 18%

profile of v9, /device:TPU:0, one launch (start us, length us, event | category | flops | bytes accessed | tf_op | source)
XLA Modules:
  0.0 34.3 jit_solution(16229340046352837861)
XLA Ops:
  0.0 1.2 %copy-done = bf16[16,32768]{1,0:T(8,128)(2,1)S(1)} copy-done((bf16[16,32768]{1,0:T(8,128)(2,1)S(1)}, bf16[16,32768]{1,0:T(8,128)(2,1)}, u32[]{:S(2)}) %copy-start) | copy-done | bytes 1048600
  1.2 0.1 shard_map.46
  1.4 0.0 copy-start.2
  1.4 0.0 copy-start.3
  1.4 3.0 %collective-permute-start = (bf16[4,32768]{1,0:T(4,128)(2,1)S(1)}, bf16[4,32768]{1,0:T(4,128)(2,1)S(1)}, u32[]{:S(2)}, u32[]{:S(2)}) collective-permute-start(bf16[4,32768]{1,0:T(4,128)(2,1)S(1)} %get-tuple-element.13), channel_id=1, source_target_pairs={{0,4},{4,0},{8,12},{12,8},{16,20},{20,16},{24,28},{28,24},{1,5},{5... | collective-permute-start | bytes 786440 | tf_op jit(solution)/shard_map/ppermute | solution.py:435
  4.4 0.7 %collective-permute-start.1 = (bf16[4,32768]{1,0:T(4,128)(2,1)S(1)}, bf16[4,32768]{1,0:T(4,128)(2,1)S(1)}, u32[]{:S(2)}, u32[]{:S(2)}) collective-permute-start(bf16[4,32768]{1,0:T(4,128)(2,1)S(1)} %get-tuple-element.14), channel_id=1, source_target_pairs={{4,8},{8,4},{12,16},{16,12},{20,24},{24,20},{5,9},{9,5},{13,17},{1... | collective-permute-start | bytes 786440 | tf_op jit(solution)/shard_map/ppermute | solution.py:436
  5.1 5.8 %shard_map.47 = (f32[128,16,128]{2,1,0:T(8,128)S(1)}, f32[32,16,128]{2,1,0:T(8,128)S(1)}, f32[3,16,128]{2,1,0:T(8,128)S(1)}, bf16[256,256]{1,0:T(8,128)(2,1)S(1)...) custom-call(bf16[16,32768]{1,0:T(8,128)(2,1)S(1)} %copy-done, f32[60]{0:T(128)S(1)} %copy-done.2, ...), custom_call_target="tpu_custom_call" | custom-call | flops 1073741824 | bytes 4194304 | tf_op jit(solution)/shard_map/pallas_call | solution.py:439
  10.9 4.7 %collective-permute-done.near_ref = bf16[4,32768]{1,0:T(4,128)(2,1)S(1)} collective-permute-done((bf16[4,32768]{1,0:T(4,128)(2,1)S(1)}, bf16[4,32768]{1,0:T(4,128)(2,1)S(1)}, u32[]{:S(2)}, u32[]{:S(2)}) %collective-permute-start) | collective-permute-done | bytes 262176 | tf_op jit(solution)/shard_map/ppermute | solution.py:435
  15.6 0.0 collective-permute-done.1.far_ref
  15.6 1.3 %shard_map.48.pieces_ref = bf16[4,7,16,128]{3,2,1,0:T(8,128)(2,1)S(1)} custom-call(bf16[4,32768]{1,0:T(4,128)(2,1)S(1)} %collective-permute-done.near_ref, bf16[4,32768]{1,0:T(4,128)(2,1)S(1)} %collective-permute-done.1.far_ref, f32[128,16,128]{2,1,0:T(8,128)S(1)} %get-tuple-element.15.edge_ref, f32[32,16,128]{2,1,0:T(8,128)S(1)} %get-tuple-element.16.own_ref, ...), custom_call_target="tpu_custom_call" | custom-call | flops 536870912 | bytes 2097152 | tf_op jit(solution)/shard_map/pallas_call | solution.py:459
  16.9 1.6 %collective-permute-start.4 = (bf16[7,16,128]{2,1,0:T(8,128)(2,1)S(1)}, bf16[7,16,128]{2,1,0:T(8,128)(2,1)S(1)}, u32[]{:S(2)}, u32[]{:S(2)}) collective-permute-start(bf16[7,16,128]{2,1,0:T(8,128)(2,1)S(1)} %get-tuple-element.21), channel_id=1, source_target_pairs={{0,2},{1,3},{2,0},{3,1},{4,6},{5,7},{6,4},{7,5},{8,10},{9,11},{10,... | collective-permute-start | bytes 86024 | tf_op jit(solution)/shard_map/ppermute | solution.py:472
  18.5 0.6 %collective-permute-start.2 = (bf16[7,16,128]{2,1,0:T(8,128)(2,1)S(1)}, bf16[7,16,128]{2,1,0:T(8,128)(2,1)S(1)}, u32[]{:S(2)}, u32[]{:S(2)}) collective-permute-start(bf16[7,16,128]{2,1,0:T(8,128)(2,1)S(1)} %get-tuple-element.23), channel_id=1, source_target_pairs={{0,1},{1,0},{2,3},{3,2},{4,5},{5,4},{6,7},{7,6},{8,9},{9,8},{10,11... | collective-permute-start | bytes 86024 | tf_op jit(solution)/shard_map/ppermute | solution.py:472
  19.1 1.7 %collective-permute-done.4.refs_2_ = bf16[7,16,128]{2,1,0:T(8,128)(2,1)S(1)} collective-permute-done((bf16[7,16,128]{2,1,0:T(8,128)(2,1)S(1)}, bf16[7,16,128]{2,1,0:T(8,128)(2,1)S(1)}, u32[]{:S(2)}, u32[]{:S(2)}) %collective-permute-start.4) | collective-permute-done | bytes 28704 | tf_op jit(solution)/shard_map/ppermute | solution.py:472
  20.8 0.9 %collective-permute-done.3.refs_1_ = bf16[7,16,128]{2,1,0:T(8,128)(2,1)S(1)} collective-permute-done((bf16[7,16,128]{2,1,0:T(8,128)(2,1)S(1)}, bf16[7,16,128]{2,1,0:T(8,128)(2,1)S(1)}, u32[]{:S(2)}, u32[]{:S(2)}) %collective-permute-start.3) | collective-permute-done | bytes 28704 | tf_op jit(solution)/shard_map/ppermute | solution.py:472
  21.8 0.3 shard_map.49.own_ref.refs_1_
  22.1 3.6 %collective-permute-start.8 = (bf16[16,16,128]{2,1,0:T(8,128)(2,1)S(1)}, bf16[16,16,128]{2,1,0:T(8,128)(2,1)S(1)}, u32[]{:S(2)}, u32[]{:S(2)}) collective-permute-start(bf16[16,16,128]{2,1,0:T(8,128)(2,1)S(1)} %shard_map.49.own_ref.refs_1_), channel_id=1, source_target_pairs={{16,0},{20,4},{24,8},{28,12},{0,16},{4,20},{8,24},{12,28},{17,1},{... | collective-permute-start | bytes 196616 | tf_op jit(solution)/shard_map/ppermute | solution.py:482
  25.7 1.3 %collective-permute-start.7 = (bf16[16,16,128]{2,1,0:T(8,128)(2,1)S(1)}, bf16[16,16,128]{2,1,0:T(8,128)(2,1)S(1)}, u32[]{:S(2)}, u32[]{:S(2)}) collective-permute-start(bf16[16,16,128]{2,1,0:T(8,128)(2,1)S(1)} %shard_map.49.own_ref.refs_1_), channel_id=1, source_target_pairs={{12,0},{16,4},{20,8},{24,12},{28,16},{0,20},{4,24},{8,28},{13,1},{... | collective-permute-start | bytes 196616 | tf_op jit(solution)/shard_map/ppermute | solution.py:482
  27.0 1.7 %collective-permute-start.6 = (bf16[16,16,128]{2,1,0:T(8,128)(2,1)S(1)}, bf16[16,16,128]{2,1,0:T(8,128)(2,1)S(1)}, u32[]{:S(2)}, u32[]{:S(2)}) collective-permute-start(bf16[16,16,128]{2,1,0:T(8,128)(2,1)S(1)} %shard_map.49.own_ref.refs_1_), channel_id=1, source_target_pairs={{8,0},{12,4},{16,8},{20,12},{24,16},{28,20},{0,24},{4,28},{9,1},{1... | collective-permute-start | bytes 196616 | tf_op jit(solution)/shard_map/ppermute | solution.py:482
  28.6 2.5 %collective-permute-start.5 = (bf16[16,16,128]{2,1,0:T(8,128)(2,1)S(1)}, bf16[16,16,128]{2,1,0:T(8,128)(2,1)S(1)}, u32[]{:S(2)}, u32[]{:S(2)}) collective-permute-start(bf16[16,16,128]{2,1,0:T(8,128)(2,1)S(1)} %shard_map.49.own_ref.refs_1_), channel_id=1, source_target_pairs={{4,0},{8,4},{12,8},{16,12},{20,16},{24,20},{28,24},{0,28},{5,1},{9... | collective-permute-start | bytes 196616 | tf_op jit(solution)/shard_map/ppermute | solution.py:482
  31.1 0.3 shard_map.50.refs_0_
  31.5 0.0 collective-permute-done.7.refs_4_
  31.5 0.1 collective-permute-done.6.refs_3_
  31.6 1.5 %collective-permute-done.5.refs_2_ = bf16[16,16,128]{2,1,0:T(8,128)(2,1)S(1)} collective-permute-done((bf16[16,16,128]{2,1,0:T(8,128)(2,1)S(1)}, bf16[16,16,128]{2,1,0:T(8,128)(2,1)S(1)}, u32[]{:S(2)}, u32[]{:S(2)}) %collective-permute-start.5) | collective-permute-done | bytes 65568 | tf_op jit(solution)/shard_map/ppermute | solution.py:482
  33.0 1.3 %shard_map.51 = f32[16,5,8,32]{3,2,1,0:T(8,128)} custom-call(bf16[2,128,2048]{2,1,0:T(8,128)(2,1)S(1)} %shard_map.50.refs_0_, bf16[16,16,128]{2,1,0:T(8,128)(2,1)S(1)} %shard_map.49.own_ref.refs_1_, bf16[16,16,128]{2,1,0:T(8,128)(2,1)S(1)} %collective-permute-done.5.refs_2_, bf16[16,16,128]{2,1,0:T(8,128)(2,1)S(1)} %collective-permute-done.6.refs_3_, ...), custom_call_target="tpu_custom_call" | custom-call | flops 16777216 | bytes 1048576 | tf_op jit(solution)/shard_map/pallas_call | solution.py:492
  (9 shorter events, 0.0 us)
Async XLA Ops:
  0.0 1.2 %copy-start = (bf16[16,32768]{1,0:T(8,128)(2,1)S(1)}, bf16[16,32768]{1,0:T(8,128)(2,1)}, u32[]{:S(2)}) copy-start(bf16[16,32768]{1,0:T(8,128)(2,1)} %strain_ref.3) | copy-start | bytes 3145732
  1.2 3.9 %copy-start.1 = (bf16[1024,128]{1,0:T(8,128)(2,1)S(1)}, bf16[1024,128]{1,0:T(8,128)(2,1)}, u32[]{:S(2)}) copy-start(bf16[1024,128]{1,0:T(8,128)(2,1)} %constant.2.clone.dft_ref) | copy-start | bytes 786436
  1.4 3.7 %copy-start.2 = (f32[60]{0:T(128)S(1)}, f32[60]{0:T(128)}, u32[]{:S(2)}) copy-start(f32[60]{0:T(128)} %taps_ref.1) | copy-start | bytes 724
  1.4 3.7 %copy-start.3 = (f32[9]{0:T(128)S(1)}, f32[9]{0:T(128)}, u32[]{:S(2)}) copy-start(f32[9]{0:T(128)} %spatial_ref.1) | copy-start | bytes 112
  1.4 14.2 %collective-permute-start = (bf16[4,32768]{1,0:T(4,128)(2,1)S(1)}, bf16[4,32768]{1,0:T(4,128)(2,1)S(1)}, u32[]{:S(2)}, u32[]{:S(2)}) collective-permute-start(bf16[4,32768]{1,0:T(4,128)(2,1)S(1)} %get-tuple-element.13), channel_id=1, source_target_pairs={{0,4},{4,0},{8,12},{12,8},{16,20},{20,16},{24,28},{28,24},{1,5},{5... | collective-permute-start | bytes 786440 | tf_op jit(solution)/shard_map/ppermute | solution.py:435
  4.4 11.2 %collective-permute-start.1 = (bf16[4,32768]{1,0:T(4,128)(2,1)S(1)}, bf16[4,32768]{1,0:T(4,128)(2,1)S(1)}, u32[]{:S(2)}, u32[]{:S(2)}) collective-permute-start(bf16[4,32768]{1,0:T(4,128)(2,1)S(1)} %get-tuple-element.14), channel_id=1, source_target_pairs={{4,8},{8,4},{12,16},{16,12},{20,24},{24,20},{5,9},{9,5},{13,17},{1... | collective-permute-start | bytes 786440 | tf_op jit(solution)/shard_map/ppermute | solution.py:436
  16.9 3.9 %collective-permute-start.4 = (bf16[7,16,128]{2,1,0:T(8,128)(2,1)S(1)}, bf16[7,16,128]{2,1,0:T(8,128)(2,1)S(1)}, u32[]{:S(2)}, u32[]{:S(2)}) collective-permute-start(bf16[7,16,128]{2,1,0:T(8,128)(2,1)S(1)} %get-tuple-element.21), channel_id=1, source_target_pairs={{0,2},{1,3},{2,0},{3,1},{4,6},{5,7},{6,4},{7,5},{8,10},{9,11},{10,... | collective-permute-start | bytes 86024 | tf_op jit(solution)/shard_map/ppermute | solution.py:472
  18.5 3.3 %collective-permute-start.3 = (bf16[7,16,128]{2,1,0:T(8,128)(2,1)S(1)}, bf16[7,16,128]{2,1,0:T(8,128)(2,1)S(1)}, u32[]{:S(2)}, u32[]{:S(2)}) collective-permute-start(bf16[7,16,128]{2,1,0:T(8,128)(2,1)S(1)} %get-tuple-element.22), channel_id=1, source_target_pairs={{0,3},{1,2},{2,1},{3,0},{4,7},{5,6},{6,5},{7,4},{8,11},{9,10},{10,... | collective-permute-start | bytes 86024 | tf_op jit(solution)/shard_map/ppermute | solution.py:472
  18.5 3.3 %collective-permute-start.2 = (bf16[7,16,128]{2,1,0:T(8,128)(2,1)S(1)}, bf16[7,16,128]{2,1,0:T(8,128)(2,1)S(1)}, u32[]{:S(2)}, u32[]{:S(2)}) collective-permute-start(bf16[7,16,128]{2,1,0:T(8,128)(2,1)S(1)} %get-tuple-element.23), channel_id=1, source_target_pairs={{0,1},{1,0},{2,3},{3,2},{4,5},{5,4},{6,7},{7,6},{8,9},{9,8},{10,11... | collective-permute-start | bytes 86024 | tf_op jit(solution)/shard_map/ppermute | solution.py:472
  22.1 9.4 %collective-permute-start.8 = (bf16[16,16,128]{2,1,0:T(8,128)(2,1)S(1)}, bf16[16,16,128]{2,1,0:T(8,128)(2,1)S(1)}, u32[]{:S(2)}, u32[]{:S(2)}) collective-permute-start(bf16[16,16,128]{2,1,0:T(8,128)(2,1)S(1)} %shard_map.49.own_ref.refs_1_), channel_id=1, source_target_pairs={{16,0},{20,4},{24,8},{28,12},{0,16},{4,20},{8,24},{12,28},{17,1},{... | collective-permute-start | bytes 196616 | tf_op jit(solution)/shard_map/ppermute | solution.py:482
  25.7 5.8 %collective-permute-start.7 = (bf16[16,16,128]{2,1,0:T(8,128)(2,1)S(1)}, bf16[16,16,128]{2,1,0:T(8,128)(2,1)S(1)}, u32[]{:S(2)}, u32[]{:S(2)}) collective-permute-start(bf16[16,16,128]{2,1,0:T(8,128)(2,1)S(1)} %shard_map.49.own_ref.refs_1_), channel_id=1, source_target_pairs={{12,0},{16,4},{20,8},{24,12},{28,16},{0,20},{4,24},{8,28},{13,1},{... | collective-permute-start | bytes 196616 | tf_op jit(solution)/shard_map/ppermute | solution.py:482
  27.0 4.6 %collective-permute-start.6 = (bf16[16,16,128]{2,1,0:T(8,128)(2,1)S(1)}, bf16[16,16,128]{2,1,0:T(8,128)(2,1)S(1)}, u32[]{:S(2)}, u32[]{:S(2)}) collective-permute-start(bf16[16,16,128]{2,1,0:T(8,128)(2,1)S(1)} %shard_map.49.own_ref.refs_1_), channel_id=1, source_target_pairs={{8,0},{12,4},{16,8},{20,12},{24,16},{28,20},{0,24},{4,28},{9,1},{1... | collective-permute-start | bytes 196616 | tf_op jit(solution)/shard_map/ppermute | solution.py:482
  28.6 4.4 %collective-permute-start.5 = (bf16[16,16,128]{2,1,0:T(8,128)(2,1)S(1)}, bf16[16,16,128]{2,1,0:T(8,128)(2,1)S(1)}, u32[]{:S(2)}, u32[]{:S(2)}) collective-permute-start(bf16[16,16,128]{2,1,0:T(8,128)(2,1)S(1)} %shard_map.49.own_ref.refs_1_), channel_id=1, source_target_pairs={{4,0},{8,4},{12,8},{16,12},{20,16},{24,20},{28,24},{0,28},{5,1},{9... | collective-permute-start | bytes 196616 | tf_op jit(solution)/shard_map/ppermute | solution.py:482

commit v10 on v9

--- a/solution.py
+++ b/solution.py
@@ -1,3 +1,4 @@
+import functools
 import math
 
 import jax
@@ -372,49 +373,50 @@
 
 def left_kernel(own_ref, left_ref):
     parts, rows, _ = own_ref.shape
-    lane = lax.broadcasted_iota(jnp.int32, (GROUP, LANES), 1)
-    mask = lane % GROUP == lax.broadcasted_iota(jnp.int32, (GROUP, LANES), 0)
-    real_lane = lax.broadcasted_iota(jnp.int32, (rows, LANES), 1) % (2 * GROUP) < GROUP
-
-    for part in range(parts):
-        value = own_ref[part].astype(f32)
-        turned = jnp.where(real_lane, pltpu.roll(value, LANES - GROUP, 1), -pltpu.roll(value, GROUP, 1))
-        for half, source in enumerate((value, turned)):
-            spread = [jnp.where(mask, jnp.broadcast_to(source[c : c + 1], (GROUP, LANES)), 0.0) for c in range(rows)]
-            left_ref[half, :, part * LANES : (part + 1) * LANES] = jnp.concatenate(spread, axis=0).astype(bf16)
-
-
-def tile_kernel(scale, left_ref, *refs):
-    *partner_refs, out_ref, tile_ref, done = refs
+    values = jnp.concatenate([own_ref[part] for part in range(parts)], axis=1).astype(f32)
+    lane = lax.broadcasted_iota(jnp.int32, values.shape, 1)
+    width = values.shape[1]
+    turned = jnp.where(lane % (2 * GROUP) < GROUP, pltpu.roll(values, width - GROUP, 1), -pltpu.roll(values, GROUP, 1))
+    column = lax.broadcasted_iota(jnp.int32, (rows, rows * GROUP), 1)
+    spread = jnp.where(column // GROUP == lax.broadcasted_iota(jnp.int32, column.shape, 0), 1.0, 0.0).astype(bf16)
+    shape = (width, rows * GROUP)
+    mask = lax.broadcasted_iota(jnp.int32, shape, 0) % GROUP == lax.broadcasted_iota(jnp.int32, shape, 1) % GROUP
+    for half, source in enumerate((values, turned)):
+        out = lax.dot_general(source.astype(bf16), spread, (((0,), (0,)), ((), ())), preferred_element_type=f32)
+        left_ref[:, half * shape[1] : (half + 1) * shape[1]] = jnp.where(mask, out, 0.0).astype(bf16)
+
+
+def tile_kernel(scale, steps, left_ref, *refs):
+    partner_refs, (out_ref, tile_ref, done) = refs[: len(steps)], refs[-3:]
     parts, rows, _ = partner_refs[0].shape
     right = jnp.concatenate(
         [jnp.concatenate([ref[part] for part in range(parts)], axis=1) for ref in partner_refs], axis=0
     )
-    real = dot_t(left_ref[0], right) * scale
-    imag = dot_t(left_ref[1], right) * scale
+    out = dot(right, left_ref[...]) * scale
+    out = jnp.concatenate([out, jnp.zeros((LANES - out.shape[0], out.shape[1]), f32)], axis=0)
+    real, imag = out[:, :LANES].T, out[:, LANES:].T
     copies = []
-    span = rows // 2
-    for c in range(rows):
-        for s in range(len(partner_refs)):
-            a = real[c * GROUP : (c + 1) * GROUP, s * rows : (s + 1) * rows]
-            b = imag[c * GROUP : (c + 1) * GROUP, s * rows : (s + 1) * rows]
-            tile_ref[c, s] = jnp.concatenate([a, b], axis=1)
-        if c % span == span - 1:
-            run = slice(c + 1 - span, c + 1)
-            copies.append(pltpu.make_async_copy(tile_ref.at[run], out_ref.at[run], done.at[c // span]))
-            copies[-1].start()
+    for index, step in enumerate(steps):
+        for c in range(rows):
+            a = real[c * GROUP : (c + 1) * GROUP, index * rows : (index + 1) * rows]
+            b = imag[c * GROUP : (c + 1) * GROUP, index * rows : (index + 1) * rows]
+            tile_ref[index, c] = jnp.concatenate([a, b], axis=1)
+        copies.append(pltpu.make_async_copy(tile_ref.at[index], out_ref.at[:, step], done.at[index]))
+        copies[-1].start()
     for copy in copies:
         copy.wait()
 
 
-def call(kernel, out_shape, scratch=(), flops=0, bytes_accessed=0, places="v", out_specs=None):
-    whole = {"v": pl.BlockSpec(memory_space=pltpu.VMEM), "s": pl.BlockSpec(memory_space=pltpu.SMEM)}
+def call(kernel, out_shape, scratch=(), flops=0, bytes_accessed=0, places="v", out_specs=None, aliases=None):
+    whole = {"v": pltpu.VMEM, "s": pltpu.SMEM, "a": pl.ANY}
+    whole = {place: pl.BlockSpec(memory_space=space) for place, space in whole.items()}
     return pl.pallas_call(
         kernel,
         out_shape=out_shape,
         in_specs=[whole[place] for place in places],
         **({} if out_specs is None else {"out_specs": out_specs}),
         scratch_shapes=list(scratch),
+        input_output_aliases=aliases or {},
         compiler_params=pltpu.CompilerParams(vmem_limit_bytes=32 * 2**20),
         cost_estimate=pl.CostEstimate(flops=flops, bytes_accessed=bytes_accessed, transcendentals=0),
     )
@@ -483,21 +485,26 @@
     parts = gathered.shape[0]
     left = call(
         left_kernel,
-        jax.ShapeDtypeStruct((2, rows * GROUP, parts * LANES), bf16),
+        jax.ShapeDtypeStruct((parts * LANES, 2 * rows * GROUP), bf16),
         flops=2**20,
         bytes_accessed=2**20,
     )(gathered)
     scale = 1.0 / (windows * rep)
     tiles = (rows, STEPS + 1, BINS // rep, 2 * rows)
-    return call(
-        lambda *refs: tile_kernel(scale, *refs),
-        jax.ShapeDtypeStruct(tiles, f32),
-        [pltpu.VMEM(tiles, f32), pltpu.SemaphoreType.DMA((2,))],
-        out_specs=pl.BlockSpec(memory_space=pl.ANY),
-        flops=2**24,
-        bytes_accessed=2**20,
-        places="v" * (STEPS + 2),
-    )(left, *partners)
+
+    def tile_call(steps, *before):
+        return call(
+            functools.partial(tile_kernel, scale, steps),
+            jax.ShapeDtypeStruct(tiles, f32),
+            [pltpu.VMEM((len(steps), rows, *tiles[2:]), f32), pltpu.SemaphoreType.DMA((len(steps),))],
+            flops=2**24,
+            bytes_accessed=2**20,
+            places="v" * (len(steps) + 1) + "a" * len(before),
+            out_specs=pl.BlockSpec(memory_space=pl.ANY),
+            aliases={len(steps) + 1: 0} if before else None,
+        )(left, *(partners[step] for step in steps), *before)
+
+    return tile_call((1, 2, 3), tile_call((0, 4)))
 
 
 def solution(mesh):

time: 34.5 us -> 34.3 us (level)
  waiting for transfers between devices: 8.89 us -> 7.5 us
  Pallas kernels: 9.13 us -> 10.4 us
    ppermute x4, waiting for transfers between devices: 1.54 us -> 0.16 us  [per_device(): lax.ppermute(gathered, 'chan', [((i + step) % chan, i) for i in range(cha...]
    pallas_call x2 -> x3, Pallas kernels: 1.62 us -> 2.89 us  [the longest x2 2.3 us: tile_call(): call(functools.partial(tile_kernel, scale, steps), jax.ShapeDtypeStruct(t...]
  transfers between devices with their start and end apart: 9 -> 9, of which waited for: 5 -> 4; matrix products, arithmetic and copies ran while one was open for 0% -> 0% of each run, Pallas kernels for 18% -> 22%
where the time goes in v10:
time: 34.3 us; the launch traced here: 34.2 us
  starting transfers between devices  14.9 us (43%)
  Pallas kernels  10.4 us (30%)
  waiting for transfers between devices  7.5 us (22%)
  local copies, waits for them, and re-layouts  1.25 us (4%)
    ppermute x4, starting transfers between devices, per_device(): lax.ppermute(gathered, 'chan', [((i + step) % chan, i) for i in range(cha...  9.04 us
    pallas_call x1, Pallas kernels, per_device(): call(own_kernel, [jax.ShapeDtypeStruct((blocks // 2, rows, LANES), f32),...  5.81 us
    ppermute x1, waiting for transfers between devices, per_device(): near = lax.ppermute(within, 'chan', pairs_within)  4.66 us
    ppermute x1, starting transfers between devices, per_device(): near = lax.ppermute(within, 'chan', pairs_within)  3 us
    ppermute x3, waiting for transfers between devices, per_device(): arrived.append(lax.ppermute(pieces[step], 'rep', to))  2.67 us
    pallas_call x2, Pallas kernels, tile_call(): call(functools.partial(tile_kernel, scale, steps), jax.ShapeDtypeStruct(t...  2.3 us
    ppermute x3, starting transfers between devices, per_device(): arrived.append(lax.ppermute(pieces[step], 'rep', to))  2.21 us
    pallas_call x1, Pallas kernels, per_device(): call(edge_kernel, jax.ShapeDtypeStruct((rep, count + 3, rows, LANES), bf1...  1.27 us
  transfers between devices with their start and end apart: 9, of which 4 were waited for; matrix products, arithmetic and copies ran while one was open for 0% of the time, Pallas kernels for 22%

profile of v10, /device:TPU:0, one launch (start us, length us, event | category | flops | bytes accessed | tf_op | source)
XLA Modules:
  0.0 34.2 jit_solution(10351954143221861801)
XLA Ops:
  0.0 1.2 %copy-done = bf16[16,32768]{1,0:T(8,128)(2,1)S(1)} copy-done((bf16[16,32768]{1,0:T(8,128)(2,1)S(1)}, bf16[16,32768]{1,0:T(8,128)(2,1)}, u32[]{:S(2)}) %copy-start) | copy-done | bytes 1048600
  1.2 0.1 shard_map.46
  1.4 0.0 copy-start.2
  1.4 0.0 copy-start.3
  1.4 3.0 %collective-permute-start = (bf16[4,32768]{1,0:T(4,128)(2,1)S(1)}, bf16[4,32768]{1,0:T(4,128)(2,1)S(1)}, u32[]{:S(2)}, u32[]{:S(2)}) collective-permute-start(bf16[4,32768]{1,0:T(4,128)(2,1)S(1)} %get-tuple-element.13), channel_id=1, source_target_pairs={{0,4},{4,0},{8,12},{12,8},{16,20},{20,16},{24,28},{28,24},{1,5},{5... | collective-permute-start | bytes 786440 | tf_op jit(solution)/shard_map/ppermute | solution.py:437
  4.4 0.7 %collective-permute-start.1 = (bf16[4,32768]{1,0:T(4,128)(2,1)S(1)}, bf16[4,32768]{1,0:T(4,128)(2,1)S(1)}, u32[]{:S(2)}, u32[]{:S(2)}) collective-permute-start(bf16[4,32768]{1,0:T(4,128)(2,1)S(1)} %get-tuple-element.14), channel_id=1, source_target_pairs={{4,8},{8,4},{12,16},{16,12},{20,24},{24,20},{5,9},{9,5},{13,17},{1... | collective-permute-start | bytes 786440 | tf_op jit(solution)/shard_map/ppermute | solution.py:438
  5.1 5.8 %shard_map.47 = (f32[128,16,128]{2,1,0:T(8,128)S(1)}, f32[32,16,128]{2,1,0:T(8,128)S(1)}, f32[3,16,128]{2,1,0:T(8,128)S(1)}, bf16[256,256]{1,0:T(8,128)(2,1)S(1)...) custom-call(bf16[16,32768]{1,0:T(8,128)(2,1)S(1)} %copy-done, f32[60]{0:T(128)S(1)} %copy-done.2, ...), custom_call_target="tpu_custom_call" | custom-call | flops 1073741824 | bytes 4194304 | tf_op jit(solution)/shard_map/pallas_call | solution.py:441
  10.9 4.7 %collective-permute-done.near_ref = bf16[4,32768]{1,0:T(4,128)(2,1)S(1)} collective-permute-done((bf16[4,32768]{1,0:T(4,128)(2,1)S(1)}, bf16[4,32768]{1,0:T(4,128)(2,1)S(1)}, u32[]{:S(2)}, u32[]{:S(2)}) %collective-permute-start) | collective-permute-done | bytes 262176 | tf_op jit(solution)/shard_map/ppermute | solution.py:437
  15.6 0.0 collective-permute-done.1.far_ref
  15.6 1.3 %shard_map.48.pieces_ref = bf16[4,7,16,128]{3,2,1,0:T(8,128)(2,1)S(1)} custom-call(bf16[4,32768]{1,0:T(4,128)(2,1)S(1)} %collective-permute-done.near_ref, bf16[4,32768]{1,0:T(4,128)(2,1)S(1)} %collective-permute-done.1.far_ref, f32[128,16,128]{2,1,0:T(8,128)S(1)} %get-tuple-element.15.edge_ref, f32[32,16,128]{2,1,0:T(8,128)S(1)} %get-tuple-element.16.own_ref, ...), custom_call_target="tpu_custom_call" | custom-call | flops 536870912 | bytes 2097152 | tf_op jit(solution)/shard_map/pallas_call | solution.py:461
  16.9 1.6 %collective-permute-start.4 = (bf16[7,16,128]{2,1,0:T(8,128)(2,1)S(1)}, bf16[7,16,128]{2,1,0:T(8,128)(2,1)S(1)}, u32[]{:S(2)}, u32[]{:S(2)}) collective-permute-start(bf16[7,16,128]{2,1,0:T(8,128)(2,1)S(1)} %get-tuple-element.21), channel_id=1, source_target_pairs={{0,2},{1,3},{2,0},{3,1},{4,6},{5,7},{6,4},{7,5},{8,10},{9,11},{10,... | collective-permute-start | bytes 86024 | tf_op jit(solution)/shard_map/ppermute | solution.py:474
  18.5 0.0 collective-permute-start.3
  18.5 0.6 %collective-permute-start.2 = (bf16[7,16,128]{2,1,0:T(8,128)(2,1)S(1)}, bf16[7,16,128]{2,1,0:T(8,128)(2,1)S(1)}, u32[]{:S(2)}, u32[]{:S(2)}) collective-permute-start(bf16[7,16,128]{2,1,0:T(8,128)(2,1)S(1)} %get-tuple-element.23), channel_id=1, source_target_pairs={{0,1},{1,0},{2,3},{3,2},{4,5},{5,4},{6,7},{7,6},{8,9},{9,8},{10,11... | collective-permute-start | bytes 86024 | tf_op jit(solution)/shard_map/ppermute | solution.py:474
  19.1 1.7 %collective-permute-done.4.refs_2_ = bf16[7,16,128]{2,1,0:T(8,128)(2,1)S(1)} collective-permute-done((bf16[7,16,128]{2,1,0:T(8,128)(2,1)S(1)}, bf16[7,16,128]{2,1,0:T(8,128)(2,1)S(1)}, u32[]{:S(2)}, u32[]{:S(2)}) %collective-permute-start.4) | collective-permute-done | bytes 28704 | tf_op jit(solution)/shard_map/ppermute | solution.py:474
  20.8 0.9 %collective-permute-done.3.refs_1_ = bf16[7,16,128]{2,1,0:T(8,128)(2,1)S(1)} collective-permute-done((bf16[7,16,128]{2,1,0:T(8,128)(2,1)S(1)}, bf16[7,16,128]{2,1,0:T(8,128)(2,1)S(1)}, u32[]{:S(2)}, u32[]{:S(2)}) %collective-permute-start.3) | collective-permute-done | bytes 28704 | tf_op jit(solution)/shard_map/ppermute | solution.py:474
  21.8 0.3 shard_map.49.own_ref.refs_0_
  22.1 3.6 %collective-permute-start.8 = (bf16[16,16,128]{2,1,0:T(8,128)(2,1)S(1)}, bf16[16,16,128]{2,1,0:T(8,128)(2,1)S(1)}, u32[]{:S(2)}, u32[]{:S(2)}) collective-permute-start(bf16[16,16,128]{2,1,0:T(8,128)(2,1)S(1)} %shard_map.49.own_ref.refs_0_), channel_id=1, source_target_pairs={{16,0},{20,4},{24,8},{28,12},{0,16},{4,20},{8,24},{12,28},{17,1},{... | collective-permute-start | bytes 196616 | tf_op jit(solution)/shard_map/ppermute | solution.py:484
  25.7 1.3 %collective-permute-start.7 = (bf16[16,16,128]{2,1,0:T(8,128)(2,1)S(1)}, bf16[16,16,128]{2,1,0:T(8,128)(2,1)S(1)}, u32[]{:S(2)}, u32[]{:S(2)}) collective-permute-start(bf16[16,16,128]{2,1,0:T(8,128)(2,1)S(1)} %shard_map.49.own_ref.refs_0_), channel_id=1, source_target_pairs={{12,0},{16,4},{20,8},{24,12},{28,16},{0,20},{4,24},{8,28},{13,1},{... | collective-permute-start | bytes 196616 | tf_op jit(solution)/shard_map/ppermute | solution.py:484
  27.0 1.7 %collective-permute-start.6 = (bf16[16,16,128]{2,1,0:T(8,128)(2,1)S(1)}, bf16[16,16,128]{2,1,0:T(8,128)(2,1)S(1)}, u32[]{:S(2)}, u32[]{:S(2)}) collective-permute-start(bf16[16,16,128]{2,1,0:T(8,128)(2,1)S(1)} %shard_map.49.own_ref.refs_0_), channel_id=1, source_target_pairs={{8,0},{12,4},{16,8},{20,12},{24,16},{28,20},{0,24},{4,28},{9,1},{1... | collective-permute-start | bytes 196616 | tf_op jit(solution)/shard_map/ppermute | solution.py:484
  28.6 2.5 %collective-permute-start.5 = (bf16[16,16,128]{2,1,0:T(8,128)(2,1)S(1)}, bf16[16,16,128]{2,1,0:T(8,128)(2,1)S(1)}, u32[]{:S(2)}, u32[]{:S(2)}) collective-permute-start(bf16[16,16,128]{2,1,0:T(8,128)(2,1)S(1)} %shard_map.49.own_ref.refs_0_), channel_id=1, source_target_pairs={{4,0},{8,4},{12,8},{16,12},{20,16},{24,20},{28,24},{0,28},{5,1},{9... | collective-permute-start | bytes 196616 | tf_op jit(solution)/shard_map/ppermute | solution.py:484
  31.1 0.6 %shard_map.50.left_ref = bf16[2048,256]{1,0:T(8,128)(2,1)S(1)} custom-call(bf16[16,16,128]{2,1,0:T(8,128)(2,1)S(1)} %shard_map.49.own_ref.refs_0_), custom_call_target="tpu_custom_call" | custom-call | flops 1048576 | bytes 1048576 | tf_op jit(solution)/shard_map/pallas_call | solution.py:486
  31.7 1.1 %shard_map.51.refs_3_ = f32[16,5,8,32]{3,2,1,0:T(8,128)} custom-call(bf16[2048,256]{1,0:T(8,128)(2,1)S(1)} %shard_map.50.left_ref, bf16[16,16,128]{2,1,0:T(8,128)(2,1)S(1)} %shard_map.49.own_ref.refs_0_, bf16[16,16,128]{2,1,0:T(8,128)(2,1)S(1)} %collective-permute-done.8.refs_1_), custom_call_target="tpu_custom_call" | custom-call | flops 16777216 | bytes 1048576 | tf_op jit(solution)/shard_map/pallas_call | solution.py:496
  32.9 0.2 collective-permute-done.5.refs_0_
  33.0 1.2 %shard_map.52 = f32[16,5,8,32]{3,2,1,0:T(8,128)} custom-call(bf16[2048,256]{1,0:T(8,128)(2,1)S(1)} %shard_map.50.left_ref, bf16[16,16,128]{2,1,0:T(8,128)(2,1)S(1)} %collective-permute-done.5.refs_0_, bf16[16,16,128]{2,1,0:T(8,128)(2,1)S(1)} %collective-permute-done.6.refs_1_, ...), custom_call_target="tpu_custom_call", output_to_operand_aliasing={{}: (4, {})} | custom-call | flops 16777216 | bytes 1048576 | tf_op jit(solution)/shard_map/pallas_call | solution.py:496
  (10 shorter events, 0.0 us)
Async XLA Ops:
  0.0 1.2 %copy-start = (bf16[16,32768]{1,0:T(8,128)(2,1)S(1)}, bf16[16,32768]{1,0:T(8,128)(2,1)}, u32[]{:S(2)}) copy-start(bf16[16,32768]{1,0:T(8,128)(2,1)} %strain_ref.3) | copy-start | bytes 3145732
  1.2 3.9 %copy-start.1 = (bf16[1024,128]{1,0:T(8,128)(2,1)S(1)}, bf16[1024,128]{1,0:T(8,128)(2,1)}, u32[]{:S(2)}) copy-start(bf16[1024,128]{1,0:T(8,128)(2,1)} %constant.2.clone.dft_ref) | copy-start | bytes 786436
  1.4 3.7 %copy-start.2 = (f32[60]{0:T(128)S(1)}, f32[60]{0:T(128)}, u32[]{:S(2)}) copy-start(f32[60]{0:T(128)} %taps_ref.1) | copy-start | bytes 724
  1.4 3.7 %copy-start.3 = (f32[9]{0:T(128)S(1)}, f32[9]{0:T(128)}, u32[]{:S(2)}) copy-start(f32[9]{0:T(128)} %spatial_ref.1) | copy-start | bytes 112
  1.4 14.2 %collective-permute-start = (bf16[4,32768]{1,0:T(4,128)(2,1)S(1)}, bf16[4,32768]{1,0:T(4,128)(2,1)S(1)}, u32[]{:S(2)}, u32[]{:S(2)}) collective-permute-start(bf16[4,32768]{1,0:T(4,128)(2,1)S(1)} %get-tuple-element.13), channel_id=1, source_target_pairs={{0,4},{4,0},{8,12},{12,8},{16,20},{20,16},{24,28},{28,24},{1,5},{5... | collective-permute-start | bytes 786440 | tf_op jit(solution)/shard_map/ppermute | solution.py:437
  4.4 11.2 %collective-permute-start.1 = (bf16[4,32768]{1,0:T(4,128)(2,1)S(1)}, bf16[4,32768]{1,0:T(4,128)(2,1)S(1)}, u32[]{:S(2)}, u32[]{:S(2)}) collective-permute-start(bf16[4,32768]{1,0:T(4,128)(2,1)S(1)} %get-tuple-element.14), channel_id=1, source_target_pairs={{4,8},{8,4},{12,16},{16,12},{20,24},{24,20},{5,9},{9,5},{13,17},{1... | collective-permute-start | bytes 786440 | tf_op jit(solution)/shard_map/ppermute | solution.py:438
  16.9 3.9 %collective-permute-start.4 = (bf16[7,16,128]{2,1,0:T(8,128)(2,1)S(1)}, bf16[7,16,128]{2,1,0:T(8,128)(2,1)S(1)}, u32[]{:S(2)}, u32[]{:S(2)}) collective-permute-start(bf16[7,16,128]{2,1,0:T(8,128)(2,1)S(1)} %get-tuple-element.21), channel_id=1, source_target_pairs={{0,2},{1,3},{2,0},{3,1},{4,6},{5,7},{6,4},{7,5},{8,10},{9,11},{10,... | collective-permute-start | bytes 86024 | tf_op jit(solution)/shard_map/ppermute | solution.py:474
  18.5 3.3 %collective-permute-start.3 = (bf16[7,16,128]{2,1,0:T(8,128)(2,1)S(1)}, bf16[7,16,128]{2,1,0:T(8,128)(2,1)S(1)}, u32[]{:S(2)}, u32[]{:S(2)}) collective-permute-start(bf16[7,16,128]{2,1,0:T(8,128)(2,1)S(1)} %get-tuple-element.22), channel_id=1, source_target_pairs={{0,3},{1,2},{2,1},{3,0},{4,7},{5,6},{6,5},{7,4},{8,11},{9,10},{10,... | collective-permute-start | bytes 86024 | tf_op jit(solution)/shard_map/ppermute | solution.py:474
  18.5 3.3 %collective-permute-start.2 = (bf16[7,16,128]{2,1,0:T(8,128)(2,1)S(1)}, bf16[7,16,128]{2,1,0:T(8,128)(2,1)S(1)}, u32[]{:S(2)}, u32[]{:S(2)}) collective-permute-start(bf16[7,16,128]{2,1,0:T(8,128)(2,1)S(1)} %get-tuple-element.23), channel_id=1, source_target_pairs={{0,1},{1,0},{2,3},{3,2},{4,5},{5,4},{6,7},{7,6},{8,9},{9,8},{10,11... | collective-permute-start | bytes 86024 | tf_op jit(solution)/shard_map/ppermute | solution.py:474
  22.1 9.6 %collective-permute-start.8 = (bf16[16,16,128]{2,1,0:T(8,128)(2,1)S(1)}, bf16[16,16,128]{2,1,0:T(8,128)(2,1)S(1)}, u32[]{:S(2)}, u32[]{:S(2)}) collective-permute-start(bf16[16,16,128]{2,1,0:T(8,128)(2,1)S(1)} %shard_map.49.own_ref.refs_0_), channel_id=1, source_target_pairs={{16,0},{20,4},{24,8},{28,12},{0,16},{4,20},{8,24},{12,28},{17,1},{... | collective-permute-start | bytes 196616 | tf_op jit(solution)/shard_map/ppermute | solution.py:484
  25.7 7.1 %collective-permute-start.7 = (bf16[16,16,128]{2,1,0:T(8,128)(2,1)S(1)}, bf16[16,16,128]{2,1,0:T(8,128)(2,1)S(1)}, u32[]{:S(2)}, u32[]{:S(2)}) collective-permute-start(bf16[16,16,128]{2,1,0:T(8,128)(2,1)S(1)} %shard_map.49.own_ref.refs_0_), channel_id=1, source_target_pairs={{12,0},{16,4},{20,8},{24,12},{28,16},{0,20},{4,24},{8,28},{13,1},{... | collective-permute-start | bytes 196616 | tf_op jit(solution)/shard_map/ppermute | solution.py:484
  27.0 5.9 %collective-permute-start.6 = (bf16[16,16,128]{2,1,0:T(8,128)(2,1)S(1)}, bf16[16,16,128]{2,1,0:T(8,128)(2,1)S(1)}, u32[]{:S(2)}, u32[]{:S(2)}) collective-permute-start(bf16[16,16,128]{2,1,0:T(8,128)(2,1)S(1)} %shard_map.49.own_ref.refs_0_), channel_id=1, source_target_pairs={{8,0},{12,4},{16,8},{20,12},{24,16},{28,20},{0,24},{4,28},{9,1},{1... | collective-permute-start | bytes 196616 | tf_op jit(solution)/shard_map/ppermute | solution.py:484
  28.6 4.4 %collective-permute-start.5 = (bf16[16,16,128]{2,1,0:T(8,128)(2,1)S(1)}, bf16[16,16,128]{2,1,0:T(8,128)(2,1)S(1)}, u32[]{:S(2)}, u32[]{:S(2)}) collective-permute-start(bf16[16,16,128]{2,1,0:T(8,128)(2,1)S(1)} %shard_map.49.own_ref.refs_0_), channel_id=1, source_target_pairs={{4,0},{8,4},{12,8},{16,12},{20,16},{24,20},{28,24},{0,28},{5,1},{9... | collective-permute-start | bytes 196616 | tf_op jit(solution)/shard_map/ppermute | solution.py:484

commit v11 on v10

--- a/solution.py
+++ b/solution.py
@@ -157,6 +157,7 @@
     toeplitz_ref,
     edge_mix_ref,
     direct_ref,
+    packed_ref,
     mixed_ref,
     split_ref,
     scale_ref,
@@ -213,7 +214,12 @@
     row = lax.broadcasted_iota(jnp.int32, scale_ref.shape, 1)
     inside = (row >= HALO) & (row < rows - HALO)
     scale_ref[...] = jnp.where(inside, scale_ref[...], 1.0)
-    spectra_ref[...] = spectra_of(split_ref, scale_ref, dft_ref, rows)
+    spectra = spectra_of(split_ref, scale_ref, dft_ref, rows)
+    spectra_ref[...] = spectra
+    groups = packed_ref.shape[0]
+    for group in range(groups):
+        for outer, tile in enumerate(tiles_of(spectra, group, groups)):
+            packed_ref[group, outer] = tile
     lead_ref[2] = spill_of(mixed_ref[:, samples:], toeplitz_ref)
 
 
@@ -226,6 +232,22 @@
 def place_of(group, groups):
     here = lax.axis_index("rep")
     return jnp.bitwise_xor(group, here) if groups & (groups - 1) == 0 else lax.rem(group - here + groups, groups)
+
+
+def tiles_of(spectra, group, groups):
+    width = 2 * GROUP
+    across = LANES // width
+    slot = lax.broadcasted_iota(jnp.int32, spectra.shape[1:], 1) // width
+    tiles = []
+    for first in range(0, spectra.shape[0], across):
+        tile = None
+        for inner in range(across):
+            shift = (inner - group) % groups * width
+            value = spectra[first + inner]
+            value = pltpu.roll(value, shift, 1) if shift else value
+            tile = value if tile is None else jnp.where(slot == inner, value, tile)
+        tiles.append(tile)
+    return tiles
 
 
 def edge_kernel(
@@ -238,6 +260,7 @@
     toeplitz_ref,
     dft_ref,
     direct_ref,
+    packed_ref,
     out_ref,
     received_ref,
 ):
@@ -284,7 +307,7 @@
     edges = jnp.concatenate([early(edges), late(edges)], axis=0)
     own = own_ref[...]
     edges = (edges + jnp.where(low, own[:, :rows], own[:, rows:])) * scale
-    spectra = whole_block(edges, own)
+    spectra = whole_block(edges[:1], own[:1])
     band = early(band[: NFFT // LANES])
 
     lead = whole_block(jnp.stack([band[0], remainder(band)]), lead_ref[:2])
@@ -301,7 +324,6 @@
         return high, values - high
 
     width = 2 * GROUP
-    across = LANES // width
     lane = lax.broadcasted_iota(jnp.int32, spectra.shape[1:], 1)
     slot = lane // width
     samples = parted(jnp.where(lane < LANES // 2, lead[0], pltpu.roll(spill, LANES // 2, 1)))
@@ -315,11 +337,10 @@
             shift = (to - group) * width % LANES
             return pltpu.roll(value, shift, 1) if shift else value
 
-        for outer in range(out_ref.shape[1] - 3):
-            tile = moved(spectra[outer * across], 0)
-            for inner in range(1, across):
-                tile = jnp.where(slot == inner, moved(spectra[outer * across + inner], inner), tile)
-            out_ref[place, outer] = tile.astype(bf16)
+        for outer, tile in enumerate(tiles_of(edges, group, groups)):
+            inside = packed_ref[group, outer]
+            whole = [jnp.where(low, tile, inside[:rows]), jnp.where(low, inside[rows:], tile)]
+            out_ref[place, outer] = jnp.concatenate(whole, axis=0).astype(bf16)
         extra = [parted(moved(spectra[0], 0))[1], moved(change[0], 1), moved(change[1], 2), *rest]
         tile = extra[0]
         for inner in range(1, len(extra)):
@@ -438,7 +459,7 @@
     far = lax.ppermute(across, "chan", pairs_across)
 
     table = jnp.asarray(dft_table())
-    edge, own, lead, filter_matrix, edge_mix, direct_matrix = call(
+    edge, own, lead, filter_matrix, edge_mix, direct_matrix, inside = call(
         own_kernel,
         [
             jax.ShapeDtypeStruct((blocks // 2, rows, LANES), f32),
@@ -447,6 +468,7 @@
             jax.ShapeDtypeStruct((2 * LANES, 2 * LANES), bf16),
             jax.ShapeDtypeStruct((2 * HALO, 2 * HALO, LANES), f32),
             jax.ShapeDtypeStruct((LANES + NFFT, LANES), bf16),
+            jax.ShapeDtypeStruct((rep, windows * 2 * GROUP // LANES, rows, LANES), f32),
         ],
         [
             pltpu.VMEM((2 * rows, LANES + samples), bf16),
@@ -466,8 +488,8 @@
         ],
         flops=2 * 2 * rows * samples * 256,
         bytes_accessed=2 * 2**20,
-        places="v" * 9,
-    )(near, far, edge, own, lead, edge_mix, filter_matrix, table, direct_matrix)
+        places="v" * 10,
+    )(near, far, edge, own, lead, edge_mix, filter_matrix, table, direct_matrix, inside)
     arrived = []
     for step in range(1, rep):
         to = [(i, i ^ step if rep & (rep - 1) == 0 else (i + step) % rep) for i in range(rep)]

time: 34.3 us -> 34.3 us (level)
  no operation moved by 1% of the time
where the time goes in v11:
time: 34.3 us; the launch traced here: 34.1 us
  starting transfers between devices  14.9 us (43%)
  Pallas kernels  10.5 us (31%)
  waiting for transfers between devices  7.36 us (21%)
  local copies, waits for them, and re-layouts  1.25 us (4%)
    ppermute x4, starting transfers between devices, per_device(): lax.ppermute(gathered, 'chan', [((i + step) % chan, i) for i in range(cha...  9.04 us
    pallas_call x1, Pallas kernels, per_device(): call(own_kernel, [jax.ShapeDtypeStruct((blocks // 2, rows, LANES), f32),...  5.95 us
    ppermute x1, waiting for transfers between devices, per_device(): near = lax.ppermute(within, 'chan', pairs_within)  4.52 us
    ppermute x1, starting transfers between devices, per_device(): near = lax.ppermute(within, 'chan', pairs_within)  3 us
    ppermute x3, waiting for transfers between devices, per_device(): arrived.append(lax.ppermute(pieces[step], 'rep', to))  2.68 us
    pallas_call x2, Pallas kernels, tile_call(): call(functools.partial(tile_kernel, scale, steps), jax.ShapeDtypeStruct(t...  2.3 us
    ppermute x3, starting transfers between devices, per_device(): arrived.append(lax.ppermute(pieces[step], 'rep', to))  2.21 us
    unnamed x8, local copies, waits for them, and re-layouts  1.24 us
  transfers between devices with their start and end apart: 9, of which 4 were waited for; matrix products, arithmetic and copies ran while one was open for 0% of the time, Pallas kernels for 22%

profile of v11, /device:TPU:0, one launch (start us, length us, event | category | flops | bytes accessed | tf_op | source)
XLA Modules:
  0.0 34.1 jit_solution(2320960294786253985)
XLA Ops:
  0.0 1.2 %copy-done = bf16[16,32768]{1,0:T(8,128)(2,1)S(1)} copy-done((bf16[16,32768]{1,0:T(8,128)(2,1)S(1)}, bf16[16,32768]{1,0:T(8,128)(2,1)}, u32[]{:S(2)}) %copy-start) | copy-done | bytes 1048600
  1.2 0.1 shard_map.46
  1.4 0.0 copy-start.2
  1.4 0.0 copy-start.3
  1.4 3.0 %collective-permute-start = (bf16[4,32768]{1,0:T(4,128)(2,1)S(1)}, bf16[4,32768]{1,0:T(4,128)(2,1)S(1)}, u32[]{:S(2)}, u32[]{:S(2)}) collective-permute-start(bf16[4,32768]{1,0:T(4,128)(2,1)S(1)} %get-tuple-element.14), channel_id=1, source_target_pairs={{0,4},{4,0},{8,12},{12,8},{16,20},{20,16},{24,28},{28,24},{1,5},{5... | collective-permute-start | bytes 786440 | tf_op jit(solution)/shard_map/ppermute | solution.py:458
  4.4 0.7 %collective-permute-start.1 = (bf16[4,32768]{1,0:T(4,128)(2,1)S(1)}, bf16[4,32768]{1,0:T(4,128)(2,1)S(1)}, u32[]{:S(2)}, u32[]{:S(2)}) collective-permute-start(bf16[4,32768]{1,0:T(4,128)(2,1)S(1)} %get-tuple-element.15), channel_id=1, source_target_pairs={{4,8},{8,4},{12,16},{16,12},{20,24},{24,20},{5,9},{9,5},{13,17},{1... | collective-permute-start | bytes 786440 | tf_op jit(solution)/shard_map/ppermute | solution.py:459
  5.1 5.9 %shard_map.47 = (f32[128,16,128]{2,1,0:T(8,128)S(1)}, f32[32,16,128]{2,1,0:T(8,128)S(1)}, f32[3,16,128]{2,1,0:T(8,128)S(1)}, bf16[256,256]{1,0:T(8,128)(2,1)S(1)...) custom-call(bf16[16,32768]{1,0:T(8,128)(2,1)S(1)} %copy-done, ...), custom_call_target="tpu_custom_call" | custom-call | flops 1073741824 | bytes 4194304 | tf_op jit(solution)/shard_map/pallas_call | solution.py:462
  11.1 4.5 %collective-permute-done.near_ref = bf16[4,32768]{1,0:T(4,128)(2,1)S(1)} collective-permute-done((bf16[4,32768]{1,0:T(4,128)(2,1)S(1)}, bf16[4,32768]{1,0:T(4,128)(2,1)S(1)}, u32[]{:S(2)}, u32[]{:S(2)}) %collective-permute-start) | collective-permute-done | bytes 262176 | tf_op jit(solution)/shard_map/ppermute | solution.py:458
  15.6 0.0 collective-permute-done.1.far_ref
  15.6 1.2 %shard_map.48.pieces_ref = bf16[4,7,16,128]{3,2,1,0:T(8,128)(2,1)S(1)} custom-call(bf16[4,32768]{1,0:T(4,128)(2,1)S(1)} %collective-permute-done.near_ref, bf16[4,32768]{1,0:T(4,128)(2,1)S(1)} %collective-permute-done.1.far_ref, f32[128,16,128]{2,1,0:T(8,128)S(1)} %get-tuple-element.16.edge_ref, f32[32,16,128]{2,1,0:T(8,128)S(1)} %get-tuple-element.17.own_ref, ...), custom_call_target="tpu_custom_call" | custom-call | flops 536870912 | bytes 2097152 | tf_op jit(solution)/shard_map/pallas_call | solution.py:483
  16.8 1.6 %collective-permute-start.4 = (bf16[7,16,128]{2,1,0:T(8,128)(2,1)S(1)}, bf16[7,16,128]{2,1,0:T(8,128)(2,1)S(1)}, u32[]{:S(2)}, u32[]{:S(2)}) collective-permute-start(bf16[7,16,128]{2,1,0:T(8,128)(2,1)S(1)} %get-tuple-element.23), channel_id=1, source_target_pairs={{0,2},{1,3},{2,0},{3,1},{4,6},{5,7},{6,4},{7,5},{8,10},{9,11},{10,... | collective-permute-start | bytes 86024 | tf_op jit(solution)/shard_map/ppermute | solution.py:496
  18.4 0.0 collective-permute-start.3
  18.4 0.6 %collective-permute-start.2 = (bf16[7,16,128]{2,1,0:T(8,128)(2,1)S(1)}, bf16[7,16,128]{2,1,0:T(8,128)(2,1)S(1)}, u32[]{:S(2)}, u32[]{:S(2)}) collective-permute-start(bf16[7,16,128]{2,1,0:T(8,128)(2,1)S(1)} %get-tuple-element.25), channel_id=1, source_target_pairs={{0,1},{1,0},{2,3},{3,2},{4,5},{5,4},{6,7},{7,6},{8,9},{9,8},{10,11... | collective-permute-start | bytes 86024 | tf_op jit(solution)/shard_map/ppermute | solution.py:496
  19.1 1.7 %collective-permute-done.4.refs_2_ = bf16[7,16,128]{2,1,0:T(8,128)(2,1)S(1)} collective-permute-done((bf16[7,16,128]{2,1,0:T(8,128)(2,1)S(1)}, bf16[7,16,128]{2,1,0:T(8,128)(2,1)S(1)}, u32[]{:S(2)}, u32[]{:S(2)}) %collective-permute-start.4) | collective-permute-done | bytes 28704 | tf_op jit(solution)/shard_map/ppermute | solution.py:496
  20.8 0.9 %collective-permute-done.3.refs_1_ = bf16[7,16,128]{2,1,0:T(8,128)(2,1)S(1)} collective-permute-done((bf16[7,16,128]{2,1,0:T(8,128)(2,1)S(1)}, bf16[7,16,128]{2,1,0:T(8,128)(2,1)S(1)}, u32[]{:S(2)}, u32[]{:S(2)}) %collective-permute-start.3) | collective-permute-done | bytes 28704 | tf_op jit(solution)/shard_map/ppermute | solution.py:496
  21.7 0.3 shard_map.49.own_ref.refs_0_
  22.0 3.6 %collective-permute-start.8 = (bf16[16,16,128]{2,1,0:T(8,128)(2,1)S(1)}, bf16[16,16,128]{2,1,0:T(8,128)(2,1)S(1)}, u32[]{:S(2)}, u32[]{:S(2)}) collective-permute-start(bf16[16,16,128]{2,1,0:T(8,128)(2,1)S(1)} %shard_map.49.own_ref.refs_0_), channel_id=1, source_target_pairs={{16,0},{20,4},{24,8},{28,12},{0,16},{4,20},{8,24},{12,28},{17,1},{... | collective-permute-start | bytes 196616 | tf_op jit(solution)/shard_map/ppermute | solution.py:506
  25.7 1.3 %collective-permute-start.7 = (bf16[16,16,128]{2,1,0:T(8,128)(2,1)S(1)}, bf16[16,16,128]{2,1,0:T(8,128)(2,1)S(1)}, u32[]{:S(2)}, u32[]{:S(2)}) collective-permute-start(bf16[16,16,128]{2,1,0:T(8,128)(2,1)S(1)} %shard_map.49.own_ref.refs_0_), channel_id=1, source_target_pairs={{12,0},{16,4},{20,8},{24,12},{28,16},{0,20},{4,24},{8,28},{13,1},{... | collective-permute-start | bytes 196616 | tf_op jit(solution)/shard_map/ppermute | solution.py:506
  26.9 1.7 %collective-permute-start.6 = (bf16[16,16,128]{2,1,0:T(8,128)(2,1)S(1)}, bf16[16,16,128]{2,1,0:T(8,128)(2,1)S(1)}, u32[]{:S(2)}, u32[]{:S(2)}) collective-permute-start(bf16[16,16,128]{2,1,0:T(8,128)(2,1)S(1)} %shard_map.49.own_ref.refs_0_), channel_id=1, source_target_pairs={{8,0},{12,4},{16,8},{20,12},{24,16},{28,20},{0,24},{4,28},{9,1},{1... | collective-permute-start | bytes 196616 | tf_op jit(solution)/shard_map/ppermute | solution.py:506
  28.6 2.5 %collective-permute-start.5 = (bf16[16,16,128]{2,1,0:T(8,128)(2,1)S(1)}, bf16[16,16,128]{2,1,0:T(8,128)(2,1)S(1)}, u32[]{:S(2)}, u32[]{:S(2)}) collective-permute-start(bf16[16,16,128]{2,1,0:T(8,128)(2,1)S(1)} %shard_map.49.own_ref.refs_0_), channel_id=1, source_target_pairs={{4,0},{8,4},{12,8},{16,12},{20,16},{24,20},{28,24},{0,28},{5,1},{9... | collective-permute-start | bytes 196616 | tf_op jit(solution)/shard_map/ppermute | solution.py:506
  31.1 0.6 %shard_map.50.left_ref = bf16[2048,256]{1,0:T(8,128)(2,1)S(1)} custom-call(bf16[16,16,128]{2,1,0:T(8,128)(2,1)S(1)} %shard_map.49.own_ref.refs_0_), custom_call_target="tpu_custom_call" | custom-call | flops 1048576 | bytes 1048576 | tf_op jit(solution)/shard_map/pallas_call | solution.py:508
  31.7 1.1 %shard_map.51.refs_3_ = f32[16,5,8,32]{3,2,1,0:T(8,128)} custom-call(bf16[2048,256]{1,0:T(8,128)(2,1)S(1)} %shard_map.50.left_ref, bf16[16,16,128]{2,1,0:T(8,128)(2,1)S(1)} %shard_map.49.own_ref.refs_0_, bf16[16,16,128]{2,1,0:T(8,128)(2,1)S(1)} %collective-permute-done.8.refs_1_), custom_call_target="tpu_custom_call" | custom-call | flops 16777216 | bytes 1048576 | tf_op jit(solution)/shard_map/pallas_call | solution.py:518
  32.8 0.2 collective-permute-done.5.refs_0_
  33.0 1.2 %shard_map.52 = f32[16,5,8,32]{3,2,1,0:T(8,128)} custom-call(bf16[2048,256]{1,0:T(8,128)(2,1)S(1)} %shard_map.50.left_ref, bf16[16,16,128]{2,1,0:T(8,128)(2,1)S(1)} %collective-permute-done.5.refs_0_, bf16[16,16,128]{2,1,0:T(8,128)(2,1)S(1)} %collective-permute-done.6.refs_1_, ...), custom_call_target="tpu_custom_call", output_to_operand_aliasing={{}: (4, {})} | custom-call | flops 16777216 | bytes 1048576 | tf_op jit(solution)/shard_map/pallas_call | solution.py:518
  (10 shorter events, 0.0 us)
Async XLA Ops:
  0.0 1.2 %copy-start = (bf16[16,32768]{1,0:T(8,128)(2,1)S(1)}, bf16[16,32768]{1,0:T(8,128)(2,1)}, u32[]{:S(2)}) copy-start(bf16[16,32768]{1,0:T(8,128)(2,1)} %strain_ref.3) | copy-start | bytes 3145732
  1.2 3.9 %copy-start.1 = (bf16[1024,128]{1,0:T(8,128)(2,1)S(1)}, bf16[1024,128]{1,0:T(8,128)(2,1)}, u32[]{:S(2)}) copy-start(bf16[1024,128]{1,0:T(8,128)(2,1)} %constant.2.clone.dft_ref) | copy-start | bytes 786436
  1.4 3.7 %copy-start.2 = (f32[60]{0:T(128)S(1)}, f32[60]{0:T(128)}, u32[]{:S(2)}) copy-start(f32[60]{0:T(128)} %taps_ref.1) | copy-start | bytes 724
  1.4 3.7 %copy-start.3 = (f32[9]{0:T(128)S(1)}, f32[9]{0:T(128)}, u32[]{:S(2)}) copy-start(f32[9]{0:T(128)} %spatial_ref.1) | copy-start | bytes 112
  1.4 14.2 %collective-permute-start = (bf16[4,32768]{1,0:T(4,128)(2,1)S(1)}, bf16[4,32768]{1,0:T(4,128)(2,1)S(1)}, u32[]{:S(2)}, u32[]{:S(2)}) collective-permute-start(bf16[4,32768]{1,0:T(4,128)(2,1)S(1)} %get-tuple-element.14), channel_id=1, source_target_pairs={{0,4},{4,0},{8,12},{12,8},{16,20},{20,16},{24,28},{28,24},{1,5},{5... | collective-permute-start | bytes 786440 | tf_op jit(solution)/shard_map/ppermute | solution.py:458
  4.4 11.2 %collective-permute-start.1 = (bf16[4,32768]{1,0:T(4,128)(2,1)S(1)}, bf16[4,32768]{1,0:T(4,128)(2,1)S(1)}, u32[]{:S(2)}, u32[]{:S(2)}) collective-permute-start(bf16[4,32768]{1,0:T(4,128)(2,1)S(1)} %get-tuple-element.15), channel_id=1, source_target_pairs={{4,8},{8,4},{12,16},{16,12},{20,24},{24,20},{5,9},{9,5},{13,17},{1... | collective-permute-start | bytes 786440 | tf_op jit(solution)/shard_map/ppermute | solution.py:459
  16.8 3.9 %collective-permute-start.4 = (bf16[7,16,128]{2,1,0:T(8,128)(2,1)S(1)}, bf16[7,16,128]{2,1,0:T(8,128)(2,1)S(1)}, u32[]{:S(2)}, u32[]{:S(2)}) collective-permute-start(bf16[7,16,128]{2,1,0:T(8,128)(2,1)S(1)} %get-tuple-element.23), channel_id=1, source_target_pairs={{0,2},{1,3},{2,0},{3,1},{4,6},{5,7},{6,4},{7,5},{8,10},{9,11},{10,... | collective-permute-start | bytes 86024 | tf_op jit(solution)/shard_map/ppermute | solution.py:496
  18.4 3.3 %collective-permute-start.3 = (bf16[7,16,128]{2,1,0:T(8,128)(2,1)S(1)}, bf16[7,16,128]{2,1,0:T(8,128)(2,1)S(1)}, u32[]{:S(2)}, u32[]{:S(2)}) collective-permute-start(bf16[7,16,128]{2,1,0:T(8,128)(2,1)S(1)} %get-tuple-element.24), channel_id=1, source_target_pairs={{0,3},{1,2},{2,1},{3,0},{4,7},{5,6},{6,5},{7,4},{8,11},{9,10},{10,... | collective-permute-start | bytes 86024 | tf_op jit(solution)/shard_map/ppermute | solution.py:496
  18.4 3.3 %collective-permute-start.2 = (bf16[7,16,128]{2,1,0:T(8,128)(2,1)S(1)}, bf16[7,16,128]{2,1,0:T(8,128)(2,1)S(1)}, u32[]{:S(2)}, u32[]{:S(2)}) collective-permute-start(bf16[7,16,128]{2,1,0:T(8,128)(2,1)S(1)} %get-tuple-element.25), channel_id=1, source_target_pairs={{0,1},{1,0},{2,3},{3,2},{4,5},{5,4},{6,7},{7,6},{8,9},{9,8},{10,11... | collective-permute-start | bytes 86024 | tf_op jit(solution)/shard_map/ppermute | solution.py:496
  22.0 9.6 %collective-permute-start.8 = (bf16[16,16,128]{2,1,0:T(8,128)(2,1)S(1)}, bf16[16,16,128]{2,1,0:T(8,128)(2,1)S(1)}, u32[]{:S(2)}, u32[]{:S(2)}) collective-permute-start(bf16[16,16,128]{2,1,0:T(8,128)(2,1)S(1)} %shard_map.49.own_ref.refs_0_), channel_id=1, source_target_pairs={{16,0},{20,4},{24,8},{28,12},{0,16},{4,20},{8,24},{12,28},{17,1},{... | collective-permute-start | bytes 196616 | tf_op jit(solution)/shard_map/ppermute | solution.py:506
  25.7 7.1 %collective-permute-start.7 = (bf16[16,16,128]{2,1,0:T(8,128)(2,1)S(1)}, bf16[16,16,128]{2,1,0:T(8,128)(2,1)S(1)}, u32[]{:S(2)}, u32[]{:S(2)}) collective-permute-start(bf16[16,16,128]{2,1,0:T(8,128)(2,1)S(1)} %shard_map.49.own_ref.refs_0_), channel_id=1, source_target_pairs={{12,0},{16,4},{20,8},{24,12},{28,16},{0,20},{4,24},{8,28},{13,1},{... | collective-permute-start | bytes 196616 | tf_op jit(solution)/shard_map/ppermute | solution.py:506
  26.9 5.9 %collective-permute-start.6 = (bf16[16,16,128]{2,1,0:T(8,128)(2,1)S(1)}, bf16[16,16,128]{2,1,0:T(8,128)(2,1)S(1)}, u32[]{:S(2)}, u32[]{:S(2)}) collective-permute-start(bf16[16,16,128]{2,1,0:T(8,128)(2,1)S(1)} %shard_map.49.own_ref.refs_0_), channel_id=1, source_target_pairs={{8,0},{12,4},{16,8},{20,12},{24,16},{28,20},{0,24},{4,28},{9,1},{1... | collective-permute-start | bytes 196616 | tf_op jit(solution)/shard_map/ppermute | solution.py:506
  28.6 4.4 %collective-permute-start.5 = (bf16[16,16,128]{2,1,0:T(8,128)(2,1)S(1)}, bf16[16,16,128]{2,1,0:T(8,128)(2,1)S(1)}, u32[]{:S(2)}, u32[]{:S(2)}) collective-permute-start(bf16[16,16,128]{2,1,0:T(8,128)(2,1)S(1)} %shard_map.49.own_ref.refs_0_), channel_id=1, source_target_pairs={{4,0},{8,4},{12,8},{16,12},{20,16},{24,20},{28,24},{0,28},{5,1},{9... | collective-permute-start | bytes 196616 | tf_op jit(solution)/shard_map/ppermute | solution.py:506

commit v12 on v9

--- a/solution.py
+++ b/solution.py
@@ -228,8 +228,8 @@
 
 
 def edge_kernel(
+    far_ref,
     near_ref,
-    far_ref,
     edge_ref,
     own_ref,
     lead_ref,
@@ -362,12 +362,11 @@
             out_ref[step * count + index] = part[index]
 
 
-def rim_kernel(strain_ref, within_ref, across_ref):
+def rim_kernel(last_if_even, strain_ref, *refs):
+    rim_ref = refs[-1]
     rows = strain_ref.shape[0]
-    even = lax.axis_index("chan") % 2 == 0
-    head, tail = strain_ref[:HALO], strain_ref[rows - HALO :]
-    within_ref[...] = jnp.where(even, tail, head)
-    across_ref[...] = jnp.where(even, head, tail)
+    last = (lax.axis_index("chan") % 2 == 0) == last_if_even
+    rim_ref[...] = jnp.where(last, strain_ref[rows - HALO :], strain_ref[:HALO])
 
 
 def left_kernel(own_ref, left_ref):
@@ -431,7 +430,8 @@
     pairs_across = [(i, j) for i in range(chan) for j in (i + 1 if i % 2 else i - 1,) if 0 <= j < chan]
 
     rim = jax.ShapeDtypeStruct((HALO, samples), bf16)
-    within, across = call(rim_kernel, [rim, rim], bytes_accessed=2**20)(strain)
+    within = call(lambda *refs: rim_kernel(True, *refs), rim, bytes_accessed=2**20)(strain)
+    across = call(lambda *refs: rim_kernel(False, *refs), rim, bytes_accessed=2**20)(strain)
     near = lax.ppermute(within, "chan", pairs_within)
     far = lax.ppermute(across, "chan", pairs_across)
 
@@ -465,7 +465,7 @@
         flops=2 * 2 * rows * samples * 256,
         bytes_accessed=2 * 2**20,
         places="v" * 9,
-    )(near, far, edge, own, lead, edge_mix, filter_matrix, table, direct_matrix)
+    )(far, near, edge, own, lead, edge_mix, filter_matrix, table, direct_matrix)
     arrived = []
     for step in range(1, rep):
         to = [(i, i ^ step if rep & (rep - 1) == 0 else (i + step) % rep) for i in range(rep)]

time: 34.5 us -> 34.4 us (level)
  no operation moved by 1% of the time
where the time goes in v12:
time: 34.4 us; the launch traced here: 34.2 us
  starting transfers between devices  14.9 us (43%)
  Pallas kernels  9.12 us (27%)
  waiting for transfers between devices  8.79 us (26%)
  local copies, waits for them, and re-layouts  1.25 us (4%)
    ppermute x4, starting transfers between devices, per_device(): lax.ppermute(gathered, 'chan', [((i + step) % chan, i) for i in range(cha...  9.05 us
    pallas_call x1, Pallas kernels, per_device(): call(own_kernel, [jax.ShapeDtypeStruct((blocks // 2, rows, LANES), f32),...  5.81 us
    ppermute x1, waiting for transfers between devices, per_device(): near = lax.ppermute(within, 'chan', pairs_within)  4.57 us
    ppermute x1, starting transfers between devices, per_device(): near = lax.ppermute(within, 'chan', pairs_within)  3 us
    ppermute x3, waiting for transfers between devices, per_device(): arrived.append(lax.ppermute(pieces[step], 'rep', to))  2.68 us
    ppermute x3, starting transfers between devices, per_device(): arrived.append(lax.ppermute(pieces[step], 'rep', to))  2.21 us
    ppermute x4, waiting for transfers between devices, per_device(): lax.ppermute(gathered, 'chan', [((i + step) % chan, i) for i in range(cha...  1.54 us
    pallas_call x1, Pallas kernels, per_device(): call(lambda *refs: tile_kernel(scale, *refs), jax.ShapeDtypeStruct(tiles,...  1.27 us
  transfers between devices with their start and end apart: 9, of which 5 were waited for; matrix products, arithmetic and copies ran while one was open for 0% of the time, Pallas kernels for 18%

profile of v12, /device:TPU:0, one launch (start us, length us, event | category | flops | bytes accessed | tf_op | source)
XLA Modules:
  0.0 34.2 jit_solution(18365474957153405071)
XLA Ops:
  0.0 1.2 %copy-done = bf16[16,32768]{1,0:T(8,128)(2,1)S(1)} copy-done((bf16[16,32768]{1,0:T(8,128)(2,1)S(1)}, bf16[16,32768]{1,0:T(8,128)(2,1)}, u32[]{:S(2)}) %copy-start) | copy-done | bytes 1048600
  1.2 0.1 shard_map.47
  1.3 0.0 copy-start.1
  1.3 0.0 copy-start.2
  1.3 0.0 copy-start.3
  1.3 3.0 %collective-permute-start.1 = (bf16[4,32768]{1,0:T(4,128)(2,1)S(1)}, bf16[4,32768]{1,0:T(4,128)(2,1)S(1)}, u32[]{:S(2)}, u32[]{:S(2)}) collective-permute-start(bf16[4,32768]{1,0:T(4,128)(2,1)S(1)} %shard_map.47), channel_id=1, source_target_pairs={{0,4},{4,0},{8,12},{12,8},{16,20},{20,16},{24,28},{28,24},{1,5},{5... | collective-permute-start | bytes 786440 | tf_op jit(solution)/shard_map/ppermute | solution.py:435
  4.3 0.1 shard_map.46
  4.4 0.7 %collective-permute-start = (bf16[4,32768]{1,0:T(4,128)(2,1)S(1)}, bf16[4,32768]{1,0:T(4,128)(2,1)S(1)}, u32[]{:S(2)}, u32[]{:S(2)}) collective-permute-start(bf16[4,32768]{1,0:T(4,128)(2,1)S(1)} %shard_map.46), channel_id=1, source_target_pairs={{4,8},{8,4},{12,16},{16,12},{20,24},{24,20},{5,9},{9,5},{13,17},{1... | collective-permute-start | bytes 786440 | tf_op jit(solution)/shard_map/ppermute | solution.py:436
  5.1 5.8 %shard_map.48 = (f32[128,16,128]{2,1,0:T(8,128)S(1)}, f32[32,16,128]{2,1,0:T(8,128)S(1)}, f32[3,16,128]{2,1,0:T(8,128)S(1)}, bf16[256,256]{1,0:T(8,128)(2,1)S(1)...) custom-call(bf16[16,32768]{1,0:T(8,128)(2,1)S(1)} %copy-done, f32[60]{0:T(128)S(1)} %copy-done.2, ...), custom_call_target="tpu_custom_call" | custom-call | flops 1073741824 | bytes 4194304 | tf_op jit(solution)/shard_map/pallas_call | solution.py:439
  11.0 4.6 %collective-permute-done.1.near_ref = bf16[4,32768]{1,0:T(4,128)(2,1)S(1)} collective-permute-done((bf16[4,32768]{1,0:T(4,128)(2,1)S(1)}, bf16[4,32768]{1,0:T(4,128)(2,1)S(1)}, u32[]{:S(2)}, u32[]{:S(2)}) %collective-permute-start.1) | collective-permute-done | bytes 262176 | tf_op jit(solution)/shard_map/ppermute | solution.py:435
  15.5 1.3 %shard_map.49.pieces_ref = bf16[4,7,16,128]{3,2,1,0:T(8,128)(2,1)S(1)} custom-call(bf16[4,32768]{1,0:T(4,128)(2,1)S(1)} %collective-permute-done.far_ref, bf16[4,32768]{1,0:T(4,128)(2,1)S(1)} %collective-permute-done.1.near_ref, f32[128,16,128]{2,1,0:T(8,128)S(1)} %get-tuple-element.11.edge_ref, f32[32,16,128]{2,1,0:T(8,128)S(1)} %get-tuple-element.12.own_ref, ...), custom_call_target="tpu_custom_call" | custom-call | flops 536870912 | bytes 2097152 | tf_op jit(solution)/shard_map/pallas_call | solution.py:459
  16.8 1.6 %collective-permute-start.4 = (bf16[7,16,128]{2,1,0:T(8,128)(2,1)S(1)}, bf16[7,16,128]{2,1,0:T(8,128)(2,1)S(1)}, u32[]{:S(2)}, u32[]{:S(2)}) collective-permute-start(bf16[7,16,128]{2,1,0:T(8,128)(2,1)S(1)} %get-tuple-element.17), channel_id=1, source_target_pairs={{0,2},{1,3},{2,0},{3,1},{4,6},{5,7},{6,4},{7,5},{8,10},{9,11},{10,... | collective-permute-start | bytes 86024 | tf_op jit(solution)/shard_map/ppermute | solution.py:472
  18.4 0.6 %collective-permute-start.2 = (bf16[7,16,128]{2,1,0:T(8,128)(2,1)S(1)}, bf16[7,16,128]{2,1,0:T(8,128)(2,1)S(1)}, u32[]{:S(2)}, u32[]{:S(2)}) collective-permute-start(bf16[7,16,128]{2,1,0:T(8,128)(2,1)S(1)} %get-tuple-element.19), channel_id=1, source_target_pairs={{0,1},{1,0},{2,3},{3,2},{4,5},{5,4},{6,7},{7,6},{8,9},{9,8},{10,11... | collective-permute-start | bytes 86024 | tf_op jit(solution)/shard_map/ppermute | solution.py:472
  19.0 1.7 %collective-permute-done.4.refs_2_ = bf16[7,16,128]{2,1,0:T(8,128)(2,1)S(1)} collective-permute-done((bf16[7,16,128]{2,1,0:T(8,128)(2,1)S(1)}, bf16[7,16,128]{2,1,0:T(8,128)(2,1)S(1)}, u32[]{:S(2)}, u32[]{:S(2)}) %collective-permute-start.4) | collective-permute-done | bytes 28704 | tf_op jit(solution)/shard_map/ppermute | solution.py:472
  20.8 0.9 %collective-permute-done.3.refs_1_ = bf16[7,16,128]{2,1,0:T(8,128)(2,1)S(1)} collective-permute-done((bf16[7,16,128]{2,1,0:T(8,128)(2,1)S(1)}, bf16[7,16,128]{2,1,0:T(8,128)(2,1)S(1)}, u32[]{:S(2)}, u32[]{:S(2)}) %collective-permute-start.3) | collective-permute-done | bytes 28704 | tf_op jit(solution)/shard_map/ppermute | solution.py:472
  21.7 0.3 shard_map.50.own_ref.refs_1_
  22.0 3.6 %collective-permute-start.8 = (bf16[16,16,128]{2,1,0:T(8,128)(2,1)S(1)}, bf16[16,16,128]{2,1,0:T(8,128)(2,1)S(1)}, u32[]{:S(2)}, u32[]{:S(2)}) collective-permute-start(bf16[16,16,128]{2,1,0:T(8,128)(2,1)S(1)} %shard_map.50.own_ref.refs_1_), channel_id=1, source_target_pairs={{16,0},{20,4},{24,8},{28,12},{0,16},{4,20},{8,24},{12,28},{17,1},{... | collective-permute-start | bytes 196616 | tf_op jit(solution)/shard_map/ppermute | solution.py:482
  25.6 1.3 %collective-permute-start.7 = (bf16[16,16,128]{2,1,0:T(8,128)(2,1)S(1)}, bf16[16,16,128]{2,1,0:T(8,128)(2,1)S(1)}, u32[]{:S(2)}, u32[]{:S(2)}) collective-permute-start(bf16[16,16,128]{2,1,0:T(8,128)(2,1)S(1)} %shard_map.50.own_ref.refs_1_), channel_id=1, source_target_pairs={{12,0},{16,4},{20,8},{24,12},{28,16},{0,20},{4,24},{8,28},{13,1},{... | collective-permute-start | bytes 196616 | tf_op jit(solution)/shard_map/ppermute | solution.py:482
  26.9 1.7 %collective-permute-start.6 = (bf16[16,16,128]{2,1,0:T(8,128)(2,1)S(1)}, bf16[16,16,128]{2,1,0:T(8,128)(2,1)S(1)}, u32[]{:S(2)}, u32[]{:S(2)}) collective-permute-start(bf16[16,16,128]{2,1,0:T(8,128)(2,1)S(1)} %shard_map.50.own_ref.refs_1_), channel_id=1, source_target_pairs={{8,0},{12,4},{16,8},{20,12},{24,16},{28,20},{0,24},{4,28},{9,1},{1... | collective-permute-start | bytes 196616 | tf_op jit(solution)/shard_map/ppermute | solution.py:482
  28.6 2.5 %collective-permute-start.5 = (bf16[16,16,128]{2,1,0:T(8,128)(2,1)S(1)}, bf16[16,16,128]{2,1,0:T(8,128)(2,1)S(1)}, u32[]{:S(2)}, u32[]{:S(2)}) collective-permute-start(bf16[16,16,128]{2,1,0:T(8,128)(2,1)S(1)} %shard_map.50.own_ref.refs_1_), channel_id=1, source_target_pairs={{4,0},{8,4},{12,8},{16,12},{20,16},{24,20},{28,24},{0,28},{5,1},{9... | collective-permute-start | bytes 196616 | tf_op jit(solution)/shard_map/ppermute | solution.py:482
  31.0 0.3 shard_map.51.refs_0_
  31.4 0.1 collective-permute-done.6.refs_3_
  31.5 1.5 %collective-permute-done.5.refs_2_ = bf16[16,16,128]{2,1,0:T(8,128)(2,1)S(1)} collective-permute-done((bf16[16,16,128]{2,1,0:T(8,128)(2,1)S(1)}, bf16[16,16,128]{2,1,0:T(8,128)(2,1)S(1)}, u32[]{:S(2)}, u32[]{:S(2)}) %collective-permute-start.5) | collective-permute-done | bytes 65568 | tf_op jit(solution)/shard_map/ppermute | solution.py:482
  32.9 1.3 %shard_map.52 = f32[16,5,8,32]{3,2,1,0:T(8,128)} custom-call(bf16[2,128,2048]{2,1,0:T(8,128)(2,1)S(1)} %shard_map.51.refs_0_, bf16[16,16,128]{2,1,0:T(8,128)(2,1)S(1)} %shard_map.50.own_ref.refs_1_, bf16[16,16,128]{2,1,0:T(8,128)(2,1)S(1)} %collective-permute-done.5.refs_2_, bf16[16,16,128]{2,1,0:T(8,128)(2,1)S(1)} %collective-permute-done.6.refs_3_, ...), custom_call_target="tpu_custom_call" | custom-call | flops 16777216 | bytes 1048576 | tf_op jit(solution)/shard_map/pallas_call | solution.py:492
  (10 shorter events, 0.0 us)
Async XLA Ops:
  0.0 1.2 %copy-start = (bf16[16,32768]{1,0:T(8,128)(2,1)S(1)}, bf16[16,32768]{1,0:T(8,128)(2,1)}, u32[]{:S(2)}) copy-start(bf16[16,32768]{1,0:T(8,128)(2,1)} %strain_ref.1) | copy-start | bytes 3145732
  1.3 3.8 %copy-start.1 = (bf16[1024,128]{1,0:T(8,128)(2,1)S(1)}, bf16[1024,128]{1,0:T(8,128)(2,1)}, u32[]{:S(2)}) copy-start(bf16[1024,128]{1,0:T(8,128)(2,1)} %constant.2.clone.dft_ref) | copy-start | bytes 786436
  1.3 3.8 %copy-start.2 = (f32[60]{0:T(128)S(1)}, f32[60]{0:T(128)}, u32[]{:S(2)}) copy-start(f32[60]{0:T(128)} %taps_ref.1) | copy-start | bytes 724
  1.3 3.8 %copy-start.3 = (f32[9]{0:T(128)S(1)}, f32[9]{0:T(128)}, u32[]{:S(2)}) copy-start(f32[9]{0:T(128)} %spatial_ref.1) | copy-start | bytes 112
  1.3 14.2 %collective-permute-start.1 = (bf16[4,32768]{1,0:T(4,128)(2,1)S(1)}, bf16[4,32768]{1,0:T(4,128)(2,1)S(1)}, u32[]{:S(2)}, u32[]{:S(2)}) collective-permute-start(bf16[4,32768]{1,0:T(4,128)(2,1)S(1)} %shard_map.47), channel_id=1, source_target_pairs={{0,4},{4,0},{8,12},{12,8},{16,20},{20,16},{24,28},{28,24},{1,5},{5... | collective-permute-start | bytes 786440 | tf_op jit(solution)/shard_map/ppermute | solution.py:435
  4.4 11.1 %collective-permute-start = (bf16[4,32768]{1,0:T(4,128)(2,1)S(1)}, bf16[4,32768]{1,0:T(4,128)(2,1)S(1)}, u32[]{:S(2)}, u32[]{:S(2)}) collective-permute-start(bf16[4,32768]{1,0:T(4,128)(2,1)S(1)} %shard_map.46), channel_id=1, source_target_pairs={{4,8},{8,4},{12,16},{16,12},{20,24},{24,20},{5,9},{9,5},{13,17},{1... | collective-permute-start | bytes 786440 | tf_op jit(solution)/shard_map/ppermute | solution.py:436
  16.8 3.9 %collective-permute-start.4 = (bf16[7,16,128]{2,1,0:T(8,128)(2,1)S(1)}, bf16[7,16,128]{2,1,0:T(8,128)(2,1)S(1)}, u32[]{:S(2)}, u32[]{:S(2)}) collective-permute-start(bf16[7,16,128]{2,1,0:T(8,128)(2,1)S(1)} %get-tuple-element.17), channel_id=1, source_target_pairs={{0,2},{1,3},{2,0},{3,1},{4,6},{5,7},{6,4},{7,5},{8,10},{9,11},{10,... | collective-permute-start | bytes 86024 | tf_op jit(solution)/shard_map/ppermute | solution.py:472
  18.4 3.3 %collective-permute-start.3 = (bf16[7,16,128]{2,1,0:T(8,128)(2,1)S(1)}, bf16[7,16,128]{2,1,0:T(8,128)(2,1)S(1)}, u32[]{:S(2)}, u32[]{:S(2)}) collective-permute-start(bf16[7,16,128]{2,1,0:T(8,128)(2,1)S(1)} %get-tuple-element.18), channel_id=1, source_target_pairs={{0,3},{1,2},{2,1},{3,0},{4,7},{5,6},{6,5},{7,4},{8,11},{9,10},{10,... | collective-permute-start | bytes 86024 | tf_op jit(solution)/shard_map/ppermute | solution.py:472
  18.4 3.3 %collective-permute-start.2 = (bf16[7,16,128]{2,1,0:T(8,128)(2,1)S(1)}, bf16[7,16,128]{2,1,0:T(8,128)(2,1)S(1)}, u32[]{:S(2)}, u32[]{:S(2)}) collective-permute-start(bf16[7,16,128]{2,1,0:T(8,128)(2,1)S(1)} %get-tuple-element.19), channel_id=1, source_target_pairs={{0,1},{1,0},{2,3},{3,2},{4,5},{5,4},{6,7},{7,6},{8,9},{9,8},{10,11... | collective-permute-start | bytes 86024 | tf_op jit(solution)/shard_map/ppermute | solution.py:472
  22.0 9.4 %collective-permute-start.8 = (bf16[16,16,128]{2,1,0:T(8,128)(2,1)S(1)}, bf16[16,16,128]{2,1,0:T(8,128)(2,1)S(1)}, u32[]{:S(2)}, u32[]{:S(2)}) collective-permute-start(bf16[16,16,128]{2,1,0:T(8,128)(2,1)S(1)} %shard_map.50.own_ref.refs_1_), channel_id=1, source_target_pairs={{16,0},{20,4},{24,8},{28,12},{0,16},{4,20},{8,24},{12,28},{17,1},{... | collective-permute-start | bytes 196616 | tf_op jit(solution)/shard_map/ppermute | solution.py:482
  25.6 5.8 %collective-permute-start.7 = (bf16[16,16,128]{2,1,0:T(8,128)(2,1)S(1)}, bf16[16,16,128]{2,1,0:T(8,128)(2,1)S(1)}, u32[]{:S(2)}, u32[]{:S(2)}) collective-permute-start(bf16[16,16,128]{2,1,0:T(8,128)(2,1)S(1)} %shard_map.50.own_ref.refs_1_), channel_id=1, source_target_pairs={{12,0},{16,4},{20,8},{24,12},{28,16},{0,20},{4,24},{8,28},{13,1},{... | collective-permute-start | bytes 196616 | tf_op jit(solution)/shard_map/ppermute | solution.py:482
  26.9 4.6 %collective-permute-start.6 = (bf16[16,16,128]{2,1,0:T(8,128)(2,1)S(1)}, bf16[16,16,128]{2,1,0:T(8,128)(2,1)S(1)}, u32[]{:S(2)}, u32[]{:S(2)}) collective-permute-start(bf16[16,16,128]{2,1,0:T(8,128)(2,1)S(1)} %shard_map.50.own_ref.refs_1_), channel_id=1, source_target_pairs={{8,0},{12,4},{16,8},{20,12},{24,16},{28,20},{0,24},{4,28},{9,1},{1... | collective-permute-start | bytes 196616 | tf_op jit(solution)/shard_map/ppermute | solution.py:482
  28.6 4.4 %collective-permute-start.5 = (bf16[16,16,128]{2,1,0:T(8,128)(2,1)S(1)}, bf16[16,16,128]{2,1,0:T(8,128)(2,1)S(1)}, u32[]{:S(2)}, u32[]{:S(2)}) collective-permute-start(bf16[16,16,128]{2,1,0:T(8,128)(2,1)S(1)} %shard_map.50.own_ref.refs_1_), channel_id=1, source_target_pairs={{4,0},{8,4},{12,8},{16,12},{20,16},{24,20},{28,24},{0,28},{5,1},{9... | collective-permute-start | bytes 196616 | tf_op jit(solution)/shard_map/ppermute | solution.py:482
